TPU v7x, 256 devices: a whole 4x4x8 slice. The times are simulated.
256 devices in a mesh: wide: 64 (over z, y, core), narrow: 4 (over x).
Axes of the slice: x: 4, y: 4, z: 8, core: 2. Of those that a mesh axis runs over, the one named last changes fastest.
Arguments:
- queries: bfloat16 [98304, 4096], P(('wide', 'narrow')), may hold values from -17 to 17
- output_gradient: bfloat16 [98304, 4096], P(('wide', 'narrow')), may hold values from -6 to 6
- response_keys: bfloat16 [98304, 512], P(('wide', 'narrow')), may hold values from -17 to 17
- response_values: bfloat16 [98304, 512], P(('wide', 'narrow')), may hold values from -6 to 6
- prompt_key_rows: bfloat16 [64, 256, 512], P('wide', 'narrow'), may hold values from -6 to 6
- prompt_value_rows: bfloat16 [64, 256, 512], P('wide', 'narrow'), may hold values from -6 to 6
- prompt_index: int32 [12288, 1], P(('wide', 'narrow')), may hold values from 0 to 63; in each aligned block of 48 rows (0 to 47, 48 to 95, ...) at most 2 rows name the same one
Outputs:
- query_grad: bfloat16 [98304, 4096], P(('wide', 'narrow'))
- response_key_gradient: bfloat16 [98304, 512], P(('wide', 'narrow'))
- response_value_gradient: bfloat16 [98304, 512], P(('wide', 'narrow'))
- prompt_key_grad: bfloat16 [64, 256, 512], P('wide', 'narrow')
- prompt_value_grad: bfloat16 [64, 256, 512], P('wide', 'narrow')
Inputs may be any that keep to these rules, and one draw needn't show every extreme that they name: `prompt_index`: at most 2 of the responses held by one device have the same prompt.
All inputs are finite; a program needn't handle non-finite values.
Results may differ from a plain program's by a relative error of at most 0.015.
Values may be sent and summed in bfloat16 or wider, within the bound.
No kernel may reach another device: no remote copies, remote signals or barrier semaphores. Data moves between devices by JAX's collectives and lax.ppermute only.
A program may use at most 256 MiB of HBM per device.

v0:
```python
import math

import jax
import jax.numpy as jnp
from jax import lax
from jax.sharding import PartitionSpec as P

QUERY_HEADS = 32
KEY_VALUE_HEADS = 4
HEAD_DIMENSION = 128
RESPONSE_LENGTH = 8


def shortened(value):
    return jax.tree.map(lambda a: a.astype(jnp.bfloat16) if a.dtype == jnp.float32 else a, value)


def self_parts(q_rows, k_rows):
    batch = q_rows.shape[0]
    resp_len = q_rows.shape[1]
    q_total_heads = q_rows.shape[-1] // HEAD_DIMENSION
    kv_total = k_rows.shape[-1] // HEAD_DIMENSION
    per_group = q_total_heads // kv_total
    q_view = q_rows.reshape(batch, resp_len, kv_total, per_group, HEAD_DIMENSION)
    k_view = k_rows.reshape(batch, resp_len, kv_total, HEAD_DIMENSION)
    return (q_view, k_view, q_total_heads)


def self_flat(left_view, right_view, scale_by):
    batch = left_view.shape[0]
    resp_len = left_view.shape[1]
    lanes = resp_len * left_view.shape[2] * left_view.shape[3]
    raw = jnp.einsum("brhgd,bshd->bsrhg", left_view, right_view, preferred_element_type=jnp.float32)
    return raw.reshape(batch, resp_len, lanes) * scale_by


def causal_mask(resp_len, q_total_heads):
    key_pos = jnp.arange(resp_len, dtype=jnp.int32)[:, None]
    query_pos = (jnp.arange(resp_len * q_total_heads, dtype=jnp.int32) // q_total_heads)[None, :]
    return query_pos >= key_pos


def self_scores_all(q_rows, k_rows):
    q_view, k_view, q_total_heads = self_parts(q_rows, k_rows)
    resp_len = q_rows.shape[1]
    raw = self_flat(q_view, k_view, 1.0 / math.sqrt(HEAD_DIMENSION))
    return (jnp.where(causal_mask(resp_len, q_total_heads)[None], raw, -jnp.inf), q_view, k_view)


def self_stats_all(q_rows, d_rows, k_rows, v_rows):
    batch = q_rows.shape[0]
    resp_len = q_rows.shape[1]
    scores, q_view, k_view = self_scores_all(q_rows, k_rows)
    d_view, v_view, q_total_heads = self_parts(d_rows, v_rows)
    inners = self_flat(d_view, v_view, 1.0)
    maxima = jnp.max(scores, axis=1)
    weights = jnp.exp(scores - maxima[:, None, :])
    shape_out = (batch, resp_len, q_total_heads)
    return (
        maxima.reshape(shape_out),
        jnp.sum(weights, axis=1).reshape(shape_out),
        jnp.sum(weights * inners, axis=1).reshape(shape_out),
    )


def self_grads_all(q_rows, d_rows, k_rows, v_rows, log_norm, delta):
    batch = q_rows.shape[0]
    resp_len = q_rows.shape[1]
    scaling = 1.0 / math.sqrt(HEAD_DIMENSION)
    scores, q_view, k_view = self_scores_all(q_rows, k_rows)
    d_view, v_view, q_total_heads = self_parts(d_rows, v_rows)
    inners = self_flat(d_view, v_view, 1.0)
    chances = jnp.exp(scores - log_norm.reshape(batch, 1, -1))
    d_scores = (chances * (inners - delta.reshape(batch, 1, -1))).astype(jnp.bfloat16)
    view_shape = (batch, resp_len, resp_len, k_view.shape[2], q_view.shape[3])
    d_scores = d_scores.reshape(view_shape)
    weights = chances.astype(jnp.bfloat16).reshape(view_shape)
    query_gradient = (
        jnp.einsum("bsrhg,bshd->brhgd", d_scores, k_view, preferred_element_type=jnp.float32)
        * scaling
    )
    key_gradient = (
        jnp.einsum("bsrhg,brhgd->bshd", d_scores, q_view, preferred_element_type=jnp.float32)
        * scaling
    )
    value_gradient = jnp.einsum(
        "bsrhg,brhgd->bshd", weights, d_view, preferred_element_type=jnp.float32
    )
    return (
        query_gradient.reshape(batch, resp_len, q_total_heads * HEAD_DIMENSION),
        key_gradient.reshape(batch, resp_len, -1),
        value_gradient.reshape(batch, resp_len, -1),
    )


def merge_stats(first, second):
    maxima = jnp.maximum(first[0], second[0])
    left = jnp.exp(first[0] - maxima)
    right = jnp.exp(second[0] - maxima)
    totals = first[1] * left + second[1] * right
    return (maxima + jnp.log(totals), (first[2] * left + second[2] * right) / totals)


def prompt_part(q_head, d_head, k_all, v_all, self_part):
    scaling = 1.0 / math.sqrt(HEAD_DIMENSION)
    scores = (
        jnp.einsum("brgd,pd->brgp", q_head, k_all, preferred_element_type=jnp.float32) * scaling
    )
    inners = jnp.einsum("brgd,pd->brgp", d_head, v_all, preferred_element_type=jnp.float32)
    maxima = jnp.max(scores, axis=-1)
    weights = jnp.exp(scores - maxima[..., None])
    prompt_stats = (maxima, jnp.sum(weights, axis=-1), jnp.sum(weights * inners, axis=-1))
    log_norm, delta = merge_stats(self_part, prompt_stats)
    chances = weights * jnp.exp(maxima - log_norm)[..., None]
    d_scores = (chances * (inners - delta[..., None])).astype(jnp.bfloat16)
    query_gradient = (
        jnp.einsum("brgp,pd->brgd", d_scores, k_all, preferred_element_type=jnp.float32) * scaling
    )
    key_gradient = (
        jnp.einsum("brgp,brgd->pd", d_scores, q_head, preferred_element_type=jnp.float32) * scaling
    )
    value_gradient = jnp.einsum(
        "brgp,brgd->pd", chances.astype(jnp.bfloat16), d_head, preferred_element_type=jnp.float32
    )
    return (query_gradient, key_gradient, value_gradient, log_norm, delta)


def head_split(values, key_value_head, queries_per_group):
    picked = values[
        ...,
        key_value_head
        * queries_per_group
        * HEAD_DIMENSION : (key_value_head + 1)
        * queries_per_group
        * HEAD_DIMENSION,
    ]
    return picked.reshape(values.shape[:-1] + (queries_per_group, HEAD_DIMENSION))


def key_split(values, key_value_head):
    return values[..., key_value_head * HEAD_DIMENSION : (key_value_head + 1) * HEAD_DIMENSION]


def body(
    queries,
    output_gradient,
    response_keys,
    response_values,
    prompt_key_rows,
    prompt_value_rows,
    prompt_index,
):
    groups = lax.axis_size("wide")
    response_count = prompt_index.shape[0]
    queries_per_group = QUERY_HEADS // KEY_VALUE_HEADS
    capacity = max(2, response_count // groups)
    slot_count = groups * capacity
    block_length = math.gcd(slot_count, max(1, 512 // RESPONSE_LENGTH))
    block_count = slot_count // block_length
    targets = prompt_index[:, 0]
    position = jnp.arange(response_count, dtype=jnp.int32)
    earlier = jnp.sum(
        ((targets[None, :] == targets[:, None]) & (position[None, :] < position[:, None])).astype(
            jnp.int32
        ),
        axis=1,
    )
    placement = targets * capacity + earlier
    matches = placement[None, :] == jnp.arange(slot_count, dtype=jnp.int32)[:, None]
    owner_prompts = jnp.sum(jnp.where(matches, position[None, :], 0), axis=1)
    filled = jnp.any(matches, axis=1)

    def to_slots(rows):
        return jnp.where(filled[:, None, None], rows[owner_prompts], jnp.zeros((), rows.dtype))

    def from_slots(back):
        return back[placement]

    def blocked(values):
        return values.reshape((block_count, block_length) + values.shape[1:])

    def unblocked(values):
        return values.reshape((slot_count,) + values.shape[2:])

    queries_3 = queries.reshape(response_count, RESPONSE_LENGTH, QUERY_HEADS * HEAD_DIMENSION)
    grads_3 = output_gradient.reshape(response_count, RESPONSE_LENGTH, QUERY_HEADS * HEAD_DIMENSION)
    keys_rank_3 = response_keys.reshape(
        response_count, RESPONSE_LENGTH, KEY_VALUE_HEADS * HEAD_DIMENSION
    )
    values_rank_3 = response_values.reshape(
        response_count, RESPONSE_LENGTH, KEY_VALUE_HEADS * HEAD_DIMENSION
    )
    keys_all, values_all = (
        lax.all_gather(prompt_key_rows, "narrow", axis=1, tiled=True),
        lax.all_gather(prompt_value_rows, "narrow", axis=1, tiled=True),
    )
    keys_all = keys_all[0]
    values_all = values_all[0]
    prompt_rows = keys_all.shape[0]
    q_in, d_in, k_in, v_in = (
        lax.all_to_all(to_slots(queries_3), "wide", split_axis=0, concat_axis=0, tiled=True),
        lax.all_to_all(to_slots(grads_3), "wide", split_axis=0, concat_axis=0, tiled=True),
        lax.all_to_all(to_slots(keys_rank_3), "wide", split_axis=0, concat_axis=0, tiled=True),
        lax.all_to_all(to_slots(values_rank_3), "wide", split_axis=0, concat_axis=0, tiled=True),
    )

    def visit(loop_state, input_arrays):
        q_block, d_block, k_block, v_block = input_arrays
        own = self_stats_all(q_block, d_block, k_block, v_block)
        pre_parts = []
        norm_parts = []
        delta_parts = []
        key_parts = []
        value_parts = []
        for key_value_head in range(KEY_VALUE_HEADS):
            lower = key_value_head * queries_per_group
            upper = lower + queries_per_group
            own_head = (
                own[0][..., lower:upper],
                own[1][..., lower:upper],
                own[2][..., lower:upper],
            )
            q_pre, prefix_keys, prefix_values, log_norm, delta = prompt_part(
                head_split(q_block, key_value_head, queries_per_group),
                head_split(d_block, key_value_head, queries_per_group),
                key_split(keys_all, key_value_head),
                key_split(values_all, key_value_head),
                own_head,
            )
            pre_parts.append(
                q_pre.astype(jnp.bfloat16).reshape(
                    block_length, RESPONSE_LENGTH, queries_per_group * HEAD_DIMENSION
                )
            )
            norm_parts.append(log_norm)
            delta_parts.append(delta)
            key_parts.append(prefix_keys)
            value_parts.append(prefix_values)
        q_own, k_own, v_own = self_grads_all(
            q_block,
            d_block,
            k_block,
            v_block,
            jnp.concatenate(norm_parts, axis=-1),
            jnp.concatenate(delta_parts, axis=-1),
        )
        rounded_pre = lax.optimization_barrier(jnp.concatenate(pre_parts, axis=-1))
        q_total = (rounded_pre.astype(jnp.float32) + q_own).astype(jnp.bfloat16)
        new_state = (
            loop_state[0] + jnp.concatenate(key_parts, axis=-1),
            loop_state[1] + jnp.concatenate(value_parts, axis=-1),
        )
        return (new_state, (q_total, k_own.astype(jnp.bfloat16), v_own.astype(jnp.bfloat16)))

    wide_empty = jnp.zeros((prompt_rows, KEY_VALUE_HEADS * HEAD_DIMENSION), jnp.float32)
    sums, output_arrays = lax.scan(
        visit,
        (wide_empty, wide_empty),
        (blocked(q_in), blocked(d_in), blocked(k_in), blocked(v_in)),
    )
    key_total = sums[0]
    value_total = sums[1]
    back_q, back_k, back_v = (
        lax.all_to_all(
            shortened(unblocked(output_arrays[0])), "wide", split_axis=0, concat_axis=0, tiled=True
        ),
        lax.all_to_all(
            shortened(unblocked(output_arrays[1])), "wide", split_axis=0, concat_axis=0, tiled=True
        ),
        lax.all_to_all(
            shortened(unblocked(output_arrays[2])), "wide", split_axis=0, concat_axis=0, tiled=True
        ),
    )
    query_grad = from_slots(back_q)
    response_key_gradient = from_slots(back_k)
    response_value_gradient = from_slots(back_v)
    key_share, value_share = (
        lax.psum_scatter(
            key_total.astype(jnp.bfloat16), "narrow", scatter_dimension=0, tiled=True
        ).astype(jnp.float32),
        lax.psum_scatter(
            value_total.astype(jnp.bfloat16), "narrow", scatter_dimension=0, tiled=True
        ).astype(jnp.float32),
    )
    return (
        query_grad.reshape(response_count * RESPONSE_LENGTH, QUERY_HEADS * HEAD_DIMENSION),
        response_key_gradient.reshape(
            response_count * RESPONSE_LENGTH, KEY_VALUE_HEADS * HEAD_DIMENSION
        ),
        response_value_gradient.reshape(
            response_count * RESPONSE_LENGTH, KEY_VALUE_HEADS * HEAD_DIMENSION
        ),
        key_share.astype(jnp.bfloat16)[None],
        value_share.astype(jnp.bfloat16)[None],
    )


def solution(mesh):
    placed = (
        P(("wide", "narrow"), None),
        P(("wide", "narrow"), None),
        P(("wide", "narrow"), None),
        P(("wide", "narrow"), None),
        P("wide", "narrow", None),
        P("wide", "narrow", None),
        P(("wide", "narrow"), None),
    )
    return jax.shard_map(
        body,
        mesh=mesh,
        in_specs=placed,
        out_specs=(
            P(("wide", "narrow"), None),
            P(("wide", "narrow"), None),
            P(("wide", "narrow"), None),
            P("wide", "narrow", None),
            P("wide", "narrow", None),
        ),
        check_vma=False,
    )
```

profile of v0, /device:TPU:8, one launch (start us, length us, event | category | flops | bytes accessed | tf_op | source)
XLA Modules:
  0.0 1206.3 jit_solution(6592757768957138345)
XLA Ops:
  17.0 40.8 %all_to_all.35 = bf16[128,8,512]{2,1,0:T(8,128)(2,1)} all-to-all(bf16[128,8,512]{2,1,0:T(8,128)(2,1)S(1)} %get-tuple-element.285), channel_id=1, replica_groups=mesh['wide'=64,'narrow'=4] {'wide'}, dimensions={0} | all-to-all | bytes 2097152 | tf_op jit(solution)/shard_map/all_to_all | solution.py:203
  63.7 6.4 gather_fusion.2
  70.1 8.4 gather_fusion
  78.5 11.5 broadcast_select_fusion
  92.4 194.1 %all_to_all.36 = bf16[128,8,4096]{2,1,0:T(8,128)(2,1)} all-to-all(bf16[128,8,4096]{2,1,0:T(8,128)(2,1)} %get-tuple-element.287), channel_id=1, replica_groups=mesh['wide'=64,'narrow'=4] {'wide'}, dimensions={0} | all-to-all | bytes 16777216 | tf_op jit(solution)/shard_map/all_to_all | solution.py:201
  292.4 12.6 %all_gather.6 = bf16[1,256,512]{2,1,0:T(8,128)(2,1)S(1)} all-gather(bf16[1,64,512]{2,1,0:T(8,128)(2,1)S(1)} %copy-done.66), channel_id=1, replica_groups=mesh['wide'=64,'narrow'=4] {'narrow'}, dimensions={1}, use_global_device_ids=true | all-gather | bytes 327680 | tf_op jit(solution)/shard_map/all_gather | solution.py:194
  305.0 13.0 %all_gather.7 = bf16[1,256,512]{2,1,0:T(8,128)(2,1)} all-gather(bf16[1,64,512]{2,1,0:T(8,128)(2,1)S(1)} %copy-done.67), channel_id=1, replica_groups=mesh['wide'=64,'narrow'=4] {'narrow'}, dimensions={1}, use_global_device_ids=true | all-gather | bytes 327680 | tf_op jit(solution)/shard_map/all_gather | solution.py:195
  318.0 160.8 %all-to-all-done.2 = bf16[128,8,4096]{2,1,0:T(8,128)(2,1)} async-done(((bf16[128,8,4096]{2,1,0:T(8,128)(2,1)}), bf16[128,8,4096]{2,1,0:T(8,128)(2,1)}, u32[]{:S(2)}, u32[]{:S(2)}) %all-to-all-start.2) | async-done | bytes 8388640 | tf_op jit(solution)/shard_map/all_to_all | solution.py:202
  478.7 453.9 %while.21 = (s32[]{:T(128)}, f32[256,512]{0,1:T(8,128)}, f32[256,512]{0,1:T(8,128)}, bf16[2,64,8,4096]{3,2,1,0:T(8,128)(2,1)}, bf16[2,64,8,512]{3,2,1,0:T(8,128)...) while((s32[]{:T(128)}, f32[256,512]{0,1:T(8,128)}, ...), condition=%wide.region_19.20_spmd.clone, body=%wide.region_3.19_spmd.clone.sunk | while | flops 5642138624 | bytes 587032576 | solution.py:256
  486.0 7.7 dynamic-slice_bitcast_fusion.7
  500.3 22.1 %fusion.254 = (f32[64,8,4,8]{3,1,2,0:T(8,128)}, f32[64,4,8,8,8]{4,2,3,1,0:T(8,128)}) fusion(pred[8,8,4,8]{3,0,1,2:T(8,128)(4,1)S(1)} %iota_compare_fusion.4, bf16[2,64,8,512]{3,2,1,0:T(8,128)(2,1)S(1)} %copy-done.38, s32[]{:T(128)S(6)} %copy.434, bf16[64,8,32,128]{3,1,2,0:T(8,128)(2,1)S(1)} %get-tuple-element.421), kind=kOutput, calls=%fused_computation.19.clone.1 | convolution fusion | flops 33931264 | bytes 5341188 | tf_op jit(solution)/shard_map/while/body/eval_jaxpr/brhgd,bshd->bsrhg/dot_general | solution.py:33
  522.4 28.4 %fusion.255 = (f32[64,8,4,8]{3,1,2,0:T(8,128)}, f32[64,8,4,8]{3,1,2,0:T(8,128)}, f32[64,4,8,8,8]{4,2,3,1,0:T(8,128)}) fusion(f32[64,4,8,8,8]{4,2,3,1,0:T(8,128)} %get-tuple-element.422, f32[64,8,4,8]{3,1,2,0:T(8,128)} %get-tuple-element.423, pred[8,8,4,8]{3,0,1,2:T(8,128)(4,1)S(1)} %iota_compare_fusion.4, ...), kind=kOutput, calls=%fused_computation.17.clone.1 | convolution fusion | flops 34308096 | bytes 14813188 | tf_op jit(solution)/shard_map/while/body/eval_jaxpr/brhgd,bshd->bsrhg/dot_general | solution.py:33
  641.2 7.8 fusion.268
  655.3 9.4 reshape.452
  684.4 6.9 fusion.269
  710.7 7.7 dynamic-slice_bitcast_fusion.7
  725.0 22.1 %fusion.254 = (f32[64,8,4,8]{3,1,2,0:T(8,128)}, f32[64,4,8,8,8]{4,2,3,1,0:T(8,128)}) fusion(pred[8,8,4,8]{3,0,1,2:T(8,128)(4,1)S(1)} %iota_compare_fusion.4, bf16[2,64,8,512]{3,2,1,0:T(8,128)(2,1)S(1)} %copy-done.38, s32[]{:T(128)S(6)} %copy.434, bf16[64,8,32,128]{3,1,2,0:T(8,128)(2,1)S(1)} %get-tuple-element.421), kind=kOutput, calls=%fused_computation.19.clone.1 | convolution fusion | flops 33931264 | bytes 5341188 | tf_op jit(solution)/shard_map/while/body/eval_jaxpr/brhgd,bshd->bsrhg/dot_general | solution.py:33
  747.1 28.4 %fusion.255 = (f32[64,8,4,8]{3,1,2,0:T(8,128)}, f32[64,8,4,8]{3,1,2,0:T(8,128)}, f32[64,4,8,8,8]{4,2,3,1,0:T(8,128)}) fusion(f32[64,4,8,8,8]{4,2,3,1,0:T(8,128)} %get-tuple-element.422, f32[64,8,4,8]{3,1,2,0:T(8,128)} %get-tuple-element.423, pred[8,8,4,8]{3,0,1,2:T(8,128)(4,1)S(1)} %iota_compare_fusion.4, ...), kind=kOutput, calls=%fused_computation.17.clone.1 | convolution fusion | flops 34308096 | bytes 14813188 | tf_op jit(solution)/shard_map/while/body/eval_jaxpr/brhgd,bshd->bsrhg/dot_general | solution.py:33
  867.1 7.8 fusion.268
  881.2 9.4 reshape.452
  910.3 6.8 fusion.269
  932.6 35.1 %all_to_all.37 = bf16[128,8,512]{2,1,0:T(8,128)(2,1)} all-to-all(bf16[128,8,512]{2,1,0:T(8,128)(2,1)} %bitcast.524), channel_id=1, replica_groups=mesh['wide'=64,'narrow'=4] {'wide'}, dimensions={0} | all-to-all | bytes 2097152 | tf_op jit(solution)/shard_map/all_to_all | solution.py:267
  967.7 34.6 %all_to_all.38 = bf16[128,8,512]{2,1,0:T(8,128)(2,1)} all-to-all(bf16[128,8,512]{2,1,0:T(8,128)(2,1)} %bitcast.525), channel_id=1, replica_groups=mesh['wide'=64,'narrow'=4] {'wide'}, dimensions={0} | all-to-all | bytes 2097152 | tf_op jit(solution)/shard_map/all_to_all | solution.py:270
  1017.5 175.8 %all-to-all-done.4 = bf16[128,8,4096]{2,1,0:T(8,128)(2,1)} async-done(((bf16[128,8,4096]{2,1,0:T(8,128)(2,1)}), bf16[128,8,4096]{2,1,0:T(8,128)(2,1)}, u32[]{:S(2)}, u32[]{:S(2)}) %all-to-all-start.4) | async-done | bytes 8388640 | tf_op jit(solution)/shard_map/all_to_all | solution.py:264
  (437 shorter events, 329.2 us)
Async XLA Ops:
  7.2 56.5 %copy-start = (bf16[384,4096]{1,0:T(8,128)(2,1)S(1)}, bf16[384,4096]{1,0:T(8,128)(2,1)}, u32[]{:S(2)}) copy-start(bf16[384,4096]{1,0:T(8,128)(2,1)} %param.10) | copy-start | bytes 9437188
  57.8 34.6 %all-to-all-start.3 = ((bf16[128,8,512]{2,1,0:T(8,128)(2,1)}), bf16[128,8,512]{2,1,0:T(8,128)(2,1)}, u32[]{:S(2)}, u32[]{:S(2)}) async-start(bf16[128,8,512]{2,1,0:T(8,128)(2,1)} %get-tuple-element.284), calls=%async_computation.3 | async-start | bytes 2097152 | tf_op jit(solution)/shard_map/all_to_all | solution.py:204
  286.5 18.5 %copy-start.67 = (bf16[1,64,512]{2,1,0:T(8,128)(2,1)S(1)}, bf16[1,64,512]{2,1,0:T(8,128)(2,1)}, u32[]{:S(2)}) copy-start(bf16[1,64,512]{2,1,0:T(8,128)(2,1)} %param.14) | copy-start | bytes 196612
  286.5 192.2 %all-to-all-start.2 = ((bf16[128,8,4096]{2,1,0:T(8,128)(2,1)}), bf16[128,8,4096]{2,1,0:T(8,128)(2,1)}, u32[]{:S(2)}, u32[]{:S(2)}) async-start(bf16[128,8,4096]{2,1,0:T(8,128)(2,1)} %get-tuple-element.286), calls=%async_computation.2 | async-start | bytes 16777216 | tf_op jit(solution)/shard_map/all_to_all | solution.py:202
  482.5 17.8 %copy-start.15 = (bf16[64,8,32,128]{3,1,2,0:T(8,128)(2,1)}, bf16[64,8,32,128]{3,1,2,0:T(8,128)(2,1)S(1)}, u32[]{:S(2)}) copy-start(bf16[64,8,32,128]{3,1,2,0:T(8,128)(2,1)S(1)} %get-tuple-element.421) | copy-start | bytes 12582916 | tf_op jit(solution)/shard_map/while
  485.2 8.5 copy-start.29
  486.0 9.7 copy-start.2
  495.7 59.5 %copy-start.16 = (bf16[64,8,8,128]{3,1,2,0:T(8,128)(2,1)}, bf16[64,8,8,128]{3,1,2,0:T(8,128)(2,1)S(1)}, u32[]{:S(2)}) copy-start(bf16[64,8,8,128]{3,1,2,0:T(8,128)(2,1)S(1)} %get-tuple-element.429) | copy-start | bytes 3145732 | tf_op jit(solution)/shard_map/while
  495.7 75.9 %copy-start.20 = (bf16[64,8,8,128]{3,1,2,0:T(8,128)(2,1)}, bf16[64,8,8,128]{3,1,2,0:T(8,128)(2,1)S(1)}, u32[]{:S(2)}) copy-start(bf16[64,8,8,128]{3,1,2,0:T(8,128)(2,1)S(1)} %get-tuple-element.438) | copy-start | bytes 3145732 | tf_op jit(solution)/shard_map/while
  500.3 22.1 %copy-start.40 = (pred[8,8,4,8]{3,0,1,2:T(8,128)(4,1)}, pred[8,8,4,8]{3,0,1,2:T(8,128)(4,1)S(1)}, u32[]{:S(2)}) copy-start(pred[8,8,4,8]{3,0,1,2:T(8,128)(4,1)S(1)} %iota_compare_fusion.4) | copy-start | bytes 6148 | tf_op jit(solution)/shard_map/while
  560.1 10.6 copy-start.27
  707.2 17.8 %copy-start.15 = (bf16[64,8,32,128]{3,1,2,0:T(8,128)(2,1)}, bf16[64,8,32,128]{3,1,2,0:T(8,128)(2,1)S(1)}, u32[]{:S(2)}) copy-start(bf16[64,8,32,128]{3,1,2,0:T(8,128)(2,1)S(1)} %get-tuple-element.421) | copy-start | bytes 12582916 | tf_op jit(solution)/shard_map/while
  709.9 8.5 copy-start.29
  710.7 9.7 copy-start.2
  720.4 59.5 %copy-start.16 = (bf16[64,8,8,128]{3,1,2,0:T(8,128)(2,1)}, bf16[64,8,8,128]{3,1,2,0:T(8,128)(2,1)S(1)}, u32[]{:S(2)}) copy-start(bf16[64,8,8,128]{3,1,2,0:T(8,128)(2,1)S(1)} %get-tuple-element.429) | copy-start | bytes 3145732 | tf_op jit(solution)/shard_map/while
  720.4 75.9 %copy-start.20 = (bf16[64,8,8,128]{3,1,2,0:T(8,128)(2,1)}, bf16[64,8,8,128]{3,1,2,0:T(8,128)(2,1)S(1)}, u32[]{:S(2)}) copy-start(bf16[64,8,8,128]{3,1,2,0:T(8,128)(2,1)S(1)} %get-tuple-element.438) | copy-start | bytes 3145732 | tf_op jit(solution)/shard_map/while
  725.0 22.1 %copy-start.40 = (pred[8,8,4,8]{3,0,1,2:T(8,128)(4,1)}, pred[8,8,4,8]{3,0,1,2:T(8,128)(4,1)S(1)}, u32[]{:S(2)}) copy-start(pred[8,8,4,8]{3,0,1,2:T(8,128)(4,1)S(1)} %iota_compare_fusion.4) | copy-start | bytes 6148 | tf_op jit(solution)/shard_map/while
  784.9 10.6 copy-start.27
  1002.3 10.1 copy-start.68
  1002.3 10.1 copy-start.70
  1002.3 191.0 %all-to-all-start.4 = ((bf16[128,8,4096]{2,1,0:T(8,128)(2,1)}), bf16[128,8,4096]{2,1,0:T(8,128)(2,1)}, u32[]{:S(2)}, u32[]{:S(2)}) async-start(bf16[128,8,4096]{2,1,0:T(8,128)(2,1)} %bitcast.520), calls=%async_computation.4 | async-start | bytes 16777216 | tf_op jit(solution)/shard_map/all_to_all | solution.py:264
  1008.3 190.9 %reduce-scatter.3.cloned.1.call-start = ((), (), s32[]{:S(2)}) async-start(), calls=%async_computation.9 | async-start | bytes 327680 | tf_op jit(solution)/shard_map/reduce_scatter | solution.py:278
  1010.2 189.0 %reduce-scatter.5.cloned.1.call-start = ((), (), s32[]{:S(2)}) async-start(), calls=%async_computation.10 | async-start | bytes 327680 | tf_op jit(solution)/shard_map/reduce_scatter | solution.py:281
  1010.3 188.9 %copy-start.1 = (bf16[384,4096]{1,0:T(8,128)(2,1)S(1)}, bf16[384,4096]{1,0:T(8,128)(2,1)}, u32[]{:S(2)}) copy-start(bf16[384,4096]{1,0:T(8,128)(2,1)} %param.10) | copy-start | bytes 9437188
  (116 other events, 490.7 us)
Sparse Core Ops, SparseCore 0:
  1012.2 24.1 reduce-scatter.2
  1039.6 22.8 reduce-scatter.4
where the time goes:
time: 1220 us; the launch traced here: 1210 us
  waiting for transfers between devices  339 us (28%)
  blocking collectives  330 us (27%)
  matrix products  218 us (18%)
  local copies, waits for them, and re-layouts  183 us (15%)
  other arithmetic  99.2 us (8%)
  starting transfers between devices  17.7 us (1%)
  between operations  14.5 us (1%)
    all_to_all x1, blocking collectives, body(): lax.all_to_all(to_slots(queries_3), 'wide', split_axis=0, concat_axis=0,...  194 us
    all_to_all x1, waiting for transfers between devices, body(): lax.all_to_all(shortened(unblocked(output_arrays[0])), 'wide', split_axis...  176 us
    all_to_all x1, waiting for transfers between devices, body(): lax.all_to_all(to_slots(grads_3), 'wide', split_axis=0, concat_axis=0, ti...  161 us
    dot_general x4, matrix products, self_flat(): jnp.einsum('brhgd,bshd->bsrhg', left_view, right_view, preferred_element_...  101 us
    all_to_all x1, blocking collectives, body(): lax.all_to_all(to_slots(keys_rank_3), 'wide', split_axis=0, concat_axis=0...  40.8 us
    convert_element_type x8, other arithmetic, prompt_part(): d_scores = (chances * (inners - delta[..., None])).astype(jnp.bfloat16)  40.4 us
    while x262, local copies, waits for them, and re-layouts  38.3 us
    dot_general x8, matrix products, prompt_part(): jnp.einsum('brgd,pd->brgp', d_head, v_all, preferred_element_type=jnp.flo...  38.2 us
  transfers between devices with their start and end apart: 5, of which 3 were waited for; matrix products, arithmetic and copies ran while one was open for 3% of the time, Pallas kernels for 0%

commit v1 on v0

v1 whole, which is shorter than its diff:
```python
import functools
import math

import jax
import jax.numpy as jnp
from jax import lax
from jax.experimental import pallas as pl
from jax.experimental.pallas import tpu as pltpu
from jax.sharding import PartitionSpec as P

QUERY_HEADS = 32
KEY_VALUE_HEADS = 4
PER_GROUP = QUERY_HEADS // KEY_VALUE_HEADS
HEAD = 128
TOKENS = 8
ROWS = PER_GROUP * TOKENS
SCALE = 1.0 / math.sqrt(HEAD)
LOG2E = math.log2(math.e)


def paired_order(targets):
    count = targets.shape[0]
    position = jnp.arange(count, dtype=jnp.int32)
    same = targets[:, None] == targets[None, :]
    before = position[None, :] < position[:, None]
    double = jnp.sum(same, axis=1) == 2
    first = jnp.logical_not(jnp.any(same & before, axis=1))
    head_of = jnp.sum(jnp.where(same & first[None, :], position[None, :], 0), axis=1)
    leads = double & first
    pair_rank = jnp.sum(leads[None, :] & (position[None, :] < head_of[:, None]), axis=1)
    single_rank = jnp.sum(jnp.logical_not(double)[None, :] & before, axis=1)
    slot = jnp.where(
        double,
        2 * pair_rank + jnp.logical_not(first).astype(jnp.int32),
        2 * jnp.sum(leads) + single_rank,
    )
    order = jnp.sum(jnp.where(slot[None, :] == position[:, None], position[None, :], 0), axis=1)
    owners = jnp.sum(jnp.where(slot[None, :] == position[:, None], targets[None, :], 0), axis=1)
    return order.astype(jnp.int32), owners.astype(jnp.int32)


def dot(left, right, contract):
    return lax.dot_general(left, right, (contract, ((), ())), preferred_element_type=jnp.float32)


def attend_kernel(
    order, owners, q_ref, d_ref, rk_ref, rv_ref, kv_ref,
    dq_ref, drk_ref, drv_ref, dkv_ref,
    q_rows, d_rows, own_k, own_v, dq_acc, drk_acc, drv_acc,
):
    responses = q_ref.shape[0] // TOKENS
    prompts = kv_ref.shape[0]

    def clear(g, _):
        dkv_ref[g] = jnp.zeros(dkv_ref.shape[1:], dkv_ref.dtype)
        return 0

    lax.fori_loop(0, prompts, clear, 0)
    own_k[...] = rk_ref[...].astype(jnp.float32)
    own_v[...] = rv_ref[...].astype(jnp.float32)

    def relay(p, _):
        lower = pl.multiple_of(p * 2 * TOKENS, 2 * TOKENS)
        for source, target in ((q_ref, q_rows), (d_ref, d_rows)):
            block = source[pl.ds(lower, 2 * TOKENS), :].astype(jnp.float32)
            stacked = jnp.concatenate(
                [
                    block[r * TOKENS : (r + 1) * TOKENS, h * HEAD : (h + 1) * HEAD]
                    for r in range(2)
                    for h in range(PER_GROUP)
                ],
                axis=0,
            )
            target[pl.ds(pl.multiple_of(p * 2 * ROWS, 2 * ROWS), 2 * ROWS), :] = stacked.astype(jnp.bfloat16)
        return 0

    lax.fori_loop(0, responses // 2, relay, 0)

    lanes = 2 * ROWS
    key_at = lax.broadcasted_iota(jnp.int32, (TOKENS, lanes), 0)
    token_at = lax.rem(lax.broadcasted_iota(jnp.int32, (TOKENS, lanes), 1), TOKENS)
    visible = key_at <= token_at
    none = jnp.zeros((ROWS, HEAD), jnp.bfloat16)
    blank = jnp.zeros((TOKENS, 2 * HEAD), jnp.float32)
    blank_lanes = jnp.zeros((TOKENS, lanes), jnp.float32)

    def both(a, b, axis):
        return jnp.concatenate([a, b], axis=axis)

    def visit(i, _):
        a, b = order[2 * i], order[2 * i + 1]
        ga, gb = owners[2 * i], owners[2 * i + 1]

        def spread(rows):
            first = rows[pl.ds(pl.multiple_of(a * ROWS, ROWS), ROWS), :]
            second = rows[pl.ds(pl.multiple_of(b * ROWS, ROWS), ROWS), :]
            return both(both(first, none, 1), both(none, second, 1), 0)

        at_a = pl.ds(pl.multiple_of(a * TOKENS, TOKENS), TOKENS)
        at_b = pl.ds(pl.multiple_of(b * TOKENS, TOKENS), TOKENS)
        q, d = spread(q_rows), spread(d_rows)
        k = both(kv_ref[ga, :, :HEAD], kv_ref[gb, :, :HEAD], 1)
        v = both(kv_ref[ga, :, HEAD:], kv_ref[gb, :, HEAD:], 1)
        ko = both(both(own_k[at_a, :], own_k[at_b, :], 1), blank, 0).astype(jnp.bfloat16)
        vo = both(both(own_v[at_a, :], own_v[at_b, :], 1), blank, 0).astype(jnp.bfloat16)
        across, along = ((1,), (1,)), ((1,), (0,))
        s = dot(k, q, across)
        t = dot(v, d, across)
        so = jnp.where(visible, dot(ko, q, across)[:TOKENS], -1e30)
        to = dot(vo, d, across)[:TOKENS]
        top = jnp.maximum(jnp.max(s, axis=0, keepdims=True), jnp.max(so, axis=0, keepdims=True))
        e = jnp.exp2((s - top) * (SCALE * LOG2E))
        eo = jnp.exp2((so - top) * (SCALE * LOG2E))
        total = jnp.sum(e, axis=0, keepdims=True) + jnp.sum(eo, axis=0, keepdims=True)
        mixed = jnp.sum(e * t, axis=0, keepdims=True) + jnp.sum(eo * to, axis=0, keepdims=True)
        inverse = 1.0 / total
        delta = mixed * inverse
        p = e * inverse
        po = eo * inverse
        w = p.astype(jnp.bfloat16)
        ds = (p * (t - delta)).astype(jnp.bfloat16)
        wo = both(po, blank_lanes, 0).astype(jnp.bfloat16)
        dso = both(po * (to - delta), blank_lanes, 0).astype(jnp.bfloat16)
        dk = dot(ds, q, along) * SCALE
        dv = dot(w, d, along)
        dko = dot(dso, q, along)[:TOKENS] * SCALE
        dvo = dot(wo, d, along)[:TOKENS]
        down = ((0,), (0,))
        dq = (dot(ds, k, down) + dot(dso, ko, down)) * SCALE
        for at, part in ((at_a, dq[:ROWS, :HEAD]), (at_b, dq[ROWS:, HEAD:])):
            dq_acc[at, :] = jnp.concatenate(
                [part[h * TOKENS : (h + 1) * TOKENS] for h in range(PER_GROUP)], axis=1
            )
        drk_acc[at_a, :] = dko[:, :HEAD]
        drk_acc[at_b, :] = dko[:, HEAD:]
        drv_acc[at_a, :] = dvo[:, :HEAD]
        drv_acc[at_b, :] = dvo[:, HEAD:]
        shared = (ga == gb).astype(jnp.float32)
        dkv_ref[gb] = both(dk[:, HEAD:], dv[:, HEAD:], 1).astype(jnp.bfloat16)
        dkv_ref[ga] = both(
            dk[:, :HEAD] + shared * dk[:, HEAD:], dv[:, :HEAD] + shared * dv[:, HEAD:], 1
        ).astype(jnp.bfloat16)
        return 0

    lax.fori_loop(0, responses // 2, visit, 0)
    dq_ref[...] = dq_acc[...].astype(jnp.bfloat16)
    drk_ref[...] = drk_acc[...].astype(jnp.bfloat16)
    drv_ref[...] = drv_acc[...].astype(jnp.bfloat16)


def attend(order, owners, queries, cotangents, keys, values, gathered, start, heads):
    rows = queries.shape[0]
    prompts, length, _ = gathered.shape
    wide = PER_GROUP * HEAD
    here = lambda shape: pl.BlockSpec(shape, lambda i, *_: (0, start + i))
    out = lambda shape: pl.BlockSpec(shape, lambda i, *_: (0, i))
    deep = pl.BlockSpec((prompts, length, 2 * HEAD), lambda i, *_: (0, 0, i))
    return pl.pallas_call(
        attend_kernel,
        grid_spec=pltpu.PrefetchScalarGridSpec(
            num_scalar_prefetch=2,
            grid=(heads,),
            in_specs=[here((rows, wide)), here((rows, wide)), here((rows, HEAD)), here((rows, HEAD)), deep],
            out_specs=[out((rows, wide)), out((rows, HEAD)), out((rows, HEAD)), deep],
            scratch_shapes=[
                pltpu.VMEM((rows * PER_GROUP, HEAD), jnp.bfloat16),
                pltpu.VMEM((rows * PER_GROUP, HEAD), jnp.bfloat16),
                pltpu.VMEM((rows, HEAD), jnp.float32),
                pltpu.VMEM((rows, HEAD), jnp.float32),
                pltpu.VMEM((rows, wide), jnp.float32),
                pltpu.VMEM((rows, HEAD), jnp.float32),
                pltpu.VMEM((rows, HEAD), jnp.float32),
            ],
        ),
        out_shape=[
            jax.ShapeDtypeStruct((rows, heads * wide), jnp.bfloat16),
            jax.ShapeDtypeStruct((rows, heads * HEAD), jnp.bfloat16),
            jax.ShapeDtypeStruct((rows, heads * HEAD), jnp.bfloat16),
            jax.ShapeDtypeStruct((prompts, length, heads * 2 * HEAD), jnp.bfloat16),
        ],
        compiler_params=pltpu.CompilerParams(vmem_limit_bytes=56 * 2**20),
        cost_estimate=pl.CostEstimate(
            flops=heads * 10 * rows * PER_GROUP * length * HEAD,
            bytes_accessed=heads * (4 * prompts * length * 2 * HEAD + 6 * rows * wide),
            transcendentals=heads * rows * PER_GROUP * length,
        ),
    )(order, owners, queries, cotangents, keys, values, gathered)


def by_head(keys, values):
    rows = keys.shape[0]
    keys = keys.reshape(rows, KEY_VALUE_HEADS, 1, HEAD)
    values = values.reshape(rows, KEY_VALUE_HEADS, 1, HEAD)
    return jnp.concatenate([keys, values], axis=2).reshape(rows, 2 * KEY_VALUE_HEADS * HEAD)


def body(queries, output_gradient, response_keys, response_values, prompt_key_rows, prompt_value_rows, prompt_index):
    prompts = lax.axis_size("wide")
    order, owners = paired_order(prompt_index[:, 0])
    held = by_head(prompt_key_rows[0], prompt_value_rows[0])
    gathered = lax.all_gather(held, ("wide", "narrow"), axis=0, tiled=True)
    gathered = gathered.reshape(prompts, -1, held.shape[1])
    dq, drk, drv, partial = attend(
        order, owners, queries, output_gradient, response_keys, response_values, gathered, 0, KEY_VALUE_HEADS
    )
    partial = partial.reshape(-1, held.shape[1])
    sums = lax.psum_scatter(partial, "wide", scatter_dimension=0, tiled=True)
    sums = lax.psum_scatter(sums, "narrow", scatter_dimension=0, tiled=True)
    split = sums.reshape(1, -1, KEY_VALUE_HEADS, 2, HEAD)
    shape = prompt_key_rows.shape
    return dq, drk, drv, split[:, :, :, 0].reshape(shape), split[:, :, :, 1].reshape(shape)


def solution(mesh):
    spread = P(("wide", "narrow"), None)
    prompt = P("wide", "narrow", None)
    return jax.shard_map(
        body,
        mesh=mesh,
        in_specs=(spread, spread, spread, spread, prompt, prompt, spread),
        out_specs=(spread, spread, spread, prompt, prompt),
        check_vma=False,
    )
```

time: 1220 us -> 526 us (0.43); the launches traced: 1210 us -> 526 us
  blocking collectives: 330 us -> 0 us
  matrix products: 218 us -> 0 us
  local copies, waits for them, and re-layouts: 183 us -> 5.61 us
  waiting for transfers between devices: 339 us -> 437 us
  other arithmetic: 99.2 us -> 4.05 us
  Pallas kernels: 0 us -> 65.1 us
  starting transfers between devices: 17.7 us -> 0.12 us
    all_to_all x3 -> x0, waiting for transfers between devices: 339 us -> none  [the longest x1 176 us: body(): lax.all_to_all(shortened(unblocked(output_arrays[0])), 'wide', split_axis...]
    all_to_all x4 -> x0, blocking collectives: 305 us -> none  [the longest x1 194 us: body(): lax.all_to_all(to_slots(queries_3), 'wide', split_axis=0, concat_axis=0,...]
    reduce_scatter x2, waiting for transfers between devices: 0.01 us -> 284 us  [the longest x1 258 us: body(): sums = lax.psum_scatter(partial, 'wide', scatter_dimension=0, tiled=True)]
    dot_general x50 -> x0, matrix products: 218 us -> none  [the longest x4 101 us: self_flat(): jnp.einsum('brhgd,bshd->bsrhg', left_view, right_view, preferred_element_...]
    all_gather x0 -> x1, waiting for transfers between devices: none -> 153 us  [body(): gathered = lax.all_gather(held, ('wide', 'narrow'), axis=0, tiled=True)]
    pallas_call x0 -> x1, Pallas kernels: none -> 65.1 us  [attend(): pl.pallas_call(attend_kernel, grid_spec=pltpu.PrefetchScalarGridSpec(num_...]
    convert_element_type x10 -> x0, other arithmetic: 56 us -> none  [the longest x8 40.4 us: prompt_part(): d_scores = (chances * (inners - delta[..., None])).astype(jnp.bfloat16)]
    while x264 -> x0, local copies, waits for them, and re-layouts: 42.2 us -> none
  transfers between devices with their start and end apart: 5 -> 3, of which waited for: 3 -> 3; matrix products, arithmetic and copies ran while one was open for 3% -> 1% of each run, Pallas kernels for 0% -> 0%
where the time goes in v1:
time: 526 us
  waiting for transfers between devices  437 us (83%)
  Pallas kernels  65.1 us (12%)
  between operations  14.5 us (3%)
  local copies, waits for them, and re-layouts  5.61 us (1%)
    reduce_scatter x1, waiting for transfers between devices, body(): sums = lax.psum_scatter(partial, 'wide', scatter_dimension=0, tiled=True)  258 us
    all_gather x1, waiting for transfers between devices, body(): gathered = lax.all_gather(held, ('wide', 'narrow'), axis=0, tiled=True)  153 us
    pallas_call x1, Pallas kernels, attend(): pl.pallas_call(attend_kernel, grid_spec=pltpu.PrefetchScalarGridSpec(num_...  65.1 us
    reduce_scatter x1, waiting for transfers between devices, body(): sums = lax.psum_scatter(sums, 'narrow', scatter_dimension=0, tiled=True)  25.6 us
  transfers between devices with their start and end apart: 3, of which 3 were waited for; matrix products, arithmetic and copies ran while one was open for 1% of the time, Pallas kernels for 0%

profile of v1, /device:TPU:8, one launch (start us, length us, event | category | flops | bytes accessed | tf_op | source)
XLA Modules:
  0.0 526.2 jit_solution(6705269410656964702)
XLA Ops:
  7.2 0.0 all-gather.2.cloned.1.call-start
  7.2 0.9 reshape_squeeze.12
  8.1 0.9 reshape_squeeze.13
  8.9 0.1 pad_maximum_fusion
  9.0 0.1 copy.15
  9.2 0.7 reshape.49
  9.9 0.0 all-gather.2.cloned.1.call-update
  9.9 0.0 reduce-scatter.3.cloned.1.call-start
  10.0 0.9 fusion.2
  10.9 0.9 select_reduce_fusion.2
  11.8 0.6 convert_reduce_fusion.2
  13.1 0.2 convert_reduce_fusion
  13.3 1.3 select_reduce_fusion
  14.6 153.0 %all-gather.2.cloned.1.call-done = bf16[16384,1024]{1,0:T(8,128)(2,1)} async-done(((bf16[64,1024]{1,0:T(8,128)(2,1)}), bf16[16384,1024]{1,0:T(8,128)(2,1)}) %all-gather.2.cloned.1.call-update) | async-done | bytes 33554448 | tf_op jit(solution)/shard_map/all_gather | solution.py:201
  167.6 65.1 %shard_map.110 = (bf16[384,4096]{1,0:T(8,128)(2,1)}, bf16[384,512]{1,0:T(8,128)(2,1)}, bf16[384,512]{1,0:T(8,128)(2,1)}, bf16[64,256,1024]{2,1,0:T(8,128)(2,1)}) custom-call(s32[48]{0:T(128)} %get-tuple-element.16.order, s32[48]{0:T(128)} %get-tuple-element.15.owners, bf16[384,4096]{1,0:T(8,128)(2,1)} %q_ref.1, bf16[384,4096]{1,0:T(8,128)(2,1)} %d_ref.1, ...), custom_call_target="tpu_custom_call" | custom-call | flops 4026531840 | bytes 76546048 | tf_op jit(solution)/shard_map/pallas_call | solution.py:158
  232.8 0.0 reduce-scatter.3.cloned.1.call-update
  232.8 0.0 reduce-scatter.5.cloned.1.call-start
  232.8 258.2 %reduce-scatter.3.cloned.1.call-done = bf16[256,1024]{1,0:T(8,128)(2,1)} async-done(((bf16[16384,1024]{1,0:T(8,128)(2,1)}), bf16[256,1024]{1,0:T(8,128)(2,1)}) %reduce-scatter.3.cloned.1.call-update) | async-done | bytes 524304 | tf_op jit(solution)/shard_map/reduce_scatter | solution.py:207
  491.0 0.0 reduce-scatter.5.cloned.1.call-update
  491.0 25.6 %reduce-scatter.5.cloned.1.call-done = bf16[64,1024]{1,0:T(8,128)(2,1)} async-done(((bf16[256,1024]{1,0:T(8,128)(2,1)}), bf16[64,1024]{1,0:T(8,128)(2,1)}) %reduce-scatter.5.cloned.1.call-update) | async-done | bytes 131088 | tf_op jit(solution)/shard_map/reduce_scatter | solution.py:208
  516.6 1.0 reshape.52
  517.6 0.7 slice_reduce_fusion
  518.3 0.7 reshape_squeeze.15
  519.0 0.7 reshape_squeeze.14
  (3 shorter events, 0.0 us)
Async XLA Ops:
  7.2 160.5 %all-gather.2.cloned.1.call-start = ((), (), s32[]{:S(2)}) async-start(), calls=%async_computation.2 | async-start | bytes 33685504 | tf_op jit(solution)/shard_map/all_gather | solution.py:201
  9.9 481.1 %reduce-scatter.3.cloned.1.call-start = ((), (), s32[]{:S(2)}) async-start(), calls=%async_computation.3 | async-start | bytes 34078720 | tf_op jit(solution)/shard_map/reduce_scatter | solution.py:207
  232.8 283.8 %reduce-scatter.5.cloned.1.call-start = ((), (), s32[]{:S(2)}) async-start(), calls=%async_computation.4 | async-start | bytes 655360 | tf_op jit(solution)/shard_map/reduce_scatter | solution.py:208
Sparse Core Ops, SparseCore 0:
  12.4 155.1 all-gather.1
  232.9 258.0 reduce-scatter.2
  493.5 23.0 reduce-scatter.4

commit v2 on v1

--- a/solution.py
+++ b/solution.py
@@ -42,20 +42,42 @@
 def dot(left, right, contract):
     return lax.dot_general(left, right, (contract, ((), ())), preferred_element_type=jnp.float32)
 
-
-def attend_kernel(
-    order, owners, q_ref, d_ref, rk_ref, rv_ref, kv_ref,
-    dq_ref, drk_ref, drv_ref, dkv_ref,
-    q_rows, d_rows, own_k, own_v, dq_acc, drk_acc, drv_acc,
-):
+KEEP_SEND = (((0, 3), (1, 2)), ((0, 1), (3, 2)))
+NEAR_FAR = ((1, 3), (3, 1))
+BITS = {"x": 0, "c": 2, "y": 3, "z": 5}
+FIRST = ("x", "y", "x", "y")
+
+
+def attend_kernel(first, head, order, owners, spot, q_ref, d_ref, rk_ref, rv_ref, gathered, *refs):
+    dq_ref, drk_ref, drv_ref = refs[:3]
+    here_k, here_v, there, refs = refs[3:5], refs[5:7], refs[7:9], refs[9:]
+    q_rows, d_rows, own_k, own_v, dq_acc, drk_acc, drv_acc, k_in, v_in, dk_out, dv_out, arrived, left = refs
     responses = q_ref.shape[0] // TOKENS
-    prompts = kv_ref.shape[0]
+
+    def place(g):
+        core, y, z = g & 1, (g >> 1) & 3, g >> 3
+        return (core, slice(None), y, z) if first == "x" else (core, y, slice(None), z)
+
+    fetches = [
+        pltpu.make_async_copy(
+            gathered.at[:, spot[0] ^ block, :, pl.ds((KEY_VALUE_HEADS * which + head) * HEAD, HEAD)],
+            (k_in, v_in)[which].at[block],
+            arrived,
+        )
+        for which in range(2)
+        for block in range(4)
+    ]
+    for fetch in fetches:
+        fetch.start()
 
     def clear(g, _):
-        dkv_ref[g] = jnp.zeros(dkv_ref.shape[1:], dkv_ref.dtype)
+        for target in (dk_out, dv_out):
+            for core in range(2):
+                for block in range(4):
+                    target[core, block, :, g] = jnp.zeros((4,) + target.shape[4:], target.dtype)
         return 0
 
-    lax.fori_loop(0, prompts, clear, 0)
+    lax.fori_loop(0, dk_out.shape[3], clear, 0)
     own_k[...] = rk_ref[...].astype(jnp.float32)
     own_v[...] = rv_ref[...].astype(jnp.float32)
 
@@ -75,6 +97,8 @@
         return 0
 
     lax.fori_loop(0, responses // 2, relay, 0)
+    for fetch in fetches:
+        fetch.wait()
 
     lanes = 2 * ROWS
     key_at = lax.broadcasted_iota(jnp.int32, (TOKENS, lanes), 0)
@@ -91,6 +115,12 @@
         a, b = order[2 * i], order[2 * i + 1]
         ga, gb = owners[2 * i], owners[2 * i + 1]
 
+        def take(scratch, g):
+            return scratch[:, g ^ spot[1]].reshape(-1, HEAD)
+
+        def give(scratch, g, rows):
+            scratch[place(g)] = rows.astype(jnp.bfloat16).reshape((4,) + scratch.shape[4:])
+
         def spread(rows):
             first = rows[pl.ds(pl.multiple_of(a * ROWS, ROWS), ROWS), :]
             second = rows[pl.ds(pl.multiple_of(b * ROWS, ROWS), ROWS), :]
@@ -99,8 +129,8 @@
         at_a = pl.ds(pl.multiple_of(a * TOKENS, TOKENS), TOKENS)
         at_b = pl.ds(pl.multiple_of(b * TOKENS, TOKENS), TOKENS)
         q, d = spread(q_rows), spread(d_rows)
-        k = both(kv_ref[ga, :, :HEAD], kv_ref[gb, :, :HEAD], 1)
-        v = both(kv_ref[ga, :, HEAD:], kv_ref[gb, :, HEAD:], 1)
+        k = both(take(k_in, ga), take(k_in, gb), 1)
+        v = both(take(v_in, ga), take(v_in, gb), 1)
         ko = both(both(own_k[at_a, :], own_k[at_b, :], 1), blank, 0).astype(jnp.bfloat16)
         vo = both(both(own_v[at_a, :], own_v[at_b, :], 1), blank, 0).astype(jnp.bfloat16)
         across, along = ((1,), (1,)), ((1,), (0,))
@@ -127,41 +157,60 @@
         dvo = dot(wo, d, along)[:TOKENS]
         down = ((0,), (0,))
         dq = (dot(ds, k, down) + dot(dso, ko, down)) * SCALE
-        for at, part in ((at_a, dq[:ROWS, :HEAD]), (at_b, dq[ROWS:, HEAD:])):
+        for at, rows in ((at_a, dq[:ROWS, :HEAD]), (at_b, dq[ROWS:, HEAD:])):
             dq_acc[at, :] = jnp.concatenate(
-                [part[h * TOKENS : (h + 1) * TOKENS] for h in range(PER_GROUP)], axis=1
+                [rows[h * TOKENS : (h + 1) * TOKENS] for h in range(PER_GROUP)], axis=1
             )
         drk_acc[at_a, :] = dko[:, :HEAD]
         drk_acc[at_b, :] = dko[:, HEAD:]
         drv_acc[at_a, :] = dvo[:, :HEAD]
         drv_acc[at_b, :] = dvo[:, HEAD:]
         shared = (ga == gb).astype(jnp.float32)
-        dkv_ref[gb] = both(dk[:, HEAD:], dv[:, HEAD:], 1).astype(jnp.bfloat16)
-        dkv_ref[ga] = both(
-            dk[:, :HEAD] + shared * dk[:, HEAD:], dv[:, :HEAD] + shared * dv[:, HEAD:], 1
-        ).astype(jnp.bfloat16)
+        give(dk_out, gb, dk[:, HEAD:])
+        give(dv_out, gb, dv[:, HEAD:])
+        give(dk_out, ga, dk[:, :HEAD] + shared * dk[:, HEAD:])
+        give(dv_out, ga, dv[:, :HEAD] + shared * dv[:, HEAD:])
         return 0
 
-    lax.fori_loop(0, responses // 2, visit, 0)
+    lax.fori_loop(0, responses // 2, visit, 0, unroll=2)
+    stores = []
+    for which in range(2):
+        for group in range(2):
+            for slot, block in enumerate(KEEP_SEND[which][group]):
+                source = (dk_out, dv_out)[which]
+                stores.append(
+                    pltpu.make_async_copy(source.at[0, block], (here_k, here_v)[which][group].at[slot], left)
+                )
+                stores.append(pltpu.make_async_copy(source.at[1, block], there[group].at[which, slot], left))
+    for store in stores:
+        store.start()
     dq_ref[...] = dq_acc[...].astype(jnp.bfloat16)
     drk_ref[...] = drk_acc[...].astype(jnp.bfloat16)
     drv_ref[...] = drv_acc[...].astype(jnp.bfloat16)
-
-
-def attend(order, owners, queries, cotangents, keys, values, gathered, start, heads):
+    for store in stores:
+        store.wait()
+
+
+def attend(order, owners, spot, queries, cotangents, keys, values, gathered, head, gates):
     rows = queries.shape[0]
-    prompts, length, _ = gathered.shape
+    prompts, _, length, _ = gathered.shape
+    deep = prompts // 8
+    inward = pltpu.VMEM((4, prompts, length, HEAD), jnp.bfloat16)
+    positions = 4 * length
     wide = PER_GROUP * HEAD
-    here = lambda shape: pl.BlockSpec(shape, lambda i, *_: (0, start + i))
-    out = lambda shape: pl.BlockSpec(shape, lambda i, *_: (0, i))
-    deep = pl.BlockSpec((prompts, length, 2 * HEAD), lambda i, *_: (0, 0, i))
+    here = lambda shape: pl.BlockSpec(shape, lambda i, *_: (0, head))
+    out = lambda shape: pl.BlockSpec(shape, lambda i, *_: (0, 0))
+    far = pl.BlockSpec(memory_space=pl.ANY)
+    outward = pltpu.VMEM((2, 4, 4, deep, length, HEAD), jnp.bfloat16)
+    share = jax.ShapeDtypeStruct((2, 4, deep, length, HEAD), jnp.bfloat16)
     return pl.pallas_call(
-        attend_kernel,
+        functools.partial(attend_kernel, FIRST[head], head),
         grid_spec=pltpu.PrefetchScalarGridSpec(
-            num_scalar_prefetch=2,
-            grid=(heads,),
-            in_specs=[here((rows, wide)), here((rows, wide)), here((rows, HEAD)), here((rows, HEAD)), deep],
-            out_specs=[out((rows, wide)), out((rows, HEAD)), out((rows, HEAD)), deep],
+            num_scalar_prefetch=3,
+            grid=(1,),
+            in_specs=[here((rows, wide)), here((rows, wide)), here((rows, HEAD)), here((rows, HEAD))]
+            + [far],
+            out_specs=[out((rows, wide)), out((rows, HEAD)), out((rows, HEAD))] + [far] * 6,
             scratch_shapes=[
                 pltpu.VMEM((rows * PER_GROUP, HEAD), jnp.bfloat16),
                 pltpu.VMEM((rows * PER_GROUP, HEAD), jnp.bfloat16),
@@ -170,45 +219,122 @@
                 pltpu.VMEM((rows, wide), jnp.float32),
                 pltpu.VMEM((rows, HEAD), jnp.float32),
                 pltpu.VMEM((rows, HEAD), jnp.float32),
+                inward,
+                inward,
+                outward,
+                outward,
+                pltpu.SemaphoreType.DMA,
+                pltpu.SemaphoreType.DMA,
             ],
         ),
         out_shape=[
-            jax.ShapeDtypeStruct((rows, heads * wide), jnp.bfloat16),
-            jax.ShapeDtypeStruct((rows, heads * HEAD), jnp.bfloat16),
-            jax.ShapeDtypeStruct((rows, heads * HEAD), jnp.bfloat16),
-            jax.ShapeDtypeStruct((prompts, length, heads * 2 * HEAD), jnp.bfloat16),
-        ],
-        compiler_params=pltpu.CompilerParams(vmem_limit_bytes=56 * 2**20),
+            jax.ShapeDtypeStruct((rows, wide), jnp.bfloat16),
+            jax.ShapeDtypeStruct((rows, HEAD), jnp.bfloat16),
+            jax.ShapeDtypeStruct((rows, HEAD), jnp.bfloat16),
+        ]
+        + [share] * 4
+        + [jax.ShapeDtypeStruct((2,) + share.shape, jnp.bfloat16)] * 2,
+        compiler_params=pltpu.CompilerParams(vmem_limit_bytes=48 * 2**20),
         cost_estimate=pl.CostEstimate(
-            flops=heads * 10 * rows * PER_GROUP * length * HEAD,
-            bytes_accessed=heads * (4 * prompts * length * 2 * HEAD + 6 * rows * wide),
-            transcendentals=heads * rows * PER_GROUP * length,
+            flops=10 * rows * PER_GROUP * positions * HEAD,
+            bytes_accessed=16 * prompts * positions * 2 * HEAD + 6 * rows * wide,
+            transcendentals=rows * PER_GROUP * positions,
         ),
-    )(order, owners, queries, cotangents, keys, values, gathered)
-
-
-def by_head(keys, values):
-    rows = keys.shape[0]
-    keys = keys.reshape(rows, KEY_VALUE_HEADS, 1, HEAD)
-    values = values.reshape(rows, KEY_VALUE_HEADS, 1, HEAD)
-    return jnp.concatenate([keys, values], axis=2).reshape(rows, 2 * KEY_VALUE_HEADS * HEAD)
+    )(after(order, *gates), owners, spot, queries, cotangents, keys, values, gathered)
+
+
+def swap(array, axis, distance):
+    count = lax.axis_size("wide") * lax.axis_size("narrow")
+    flip = distance << BITS[axis]
+    return lax.ppermute(array, ("wide", "narrow"), [(i, i ^ flip) for i in range(count)])
+
+
+def other(axis):
+    return "y" if axis == "x" else "x"
+
+
+def after(value, *earlier):
+    return lax.optimization_barrier((value, earlier))[0] if earlier else value
+
+
+def sum_z(blocks):
+    total = blocks[0].astype(jnp.float32)
+    for step in range(1, 8):
+        total = total + swap(blocks[step], "z", step).astype(jnp.float32)
+    return total.astype(jnp.bfloat16)
+
+
+def halve_near(kept, sent, way, axis):
+    got = swap(sent, axis, NEAR_FAR[way][0])
+    return kept[0] + got[0], kept[1] + got[1]
+
+
+def halve_far(mine, other_sum, way, axis):
+    return mine + swap(other_sum, axis, NEAR_FAR[way][1])
+
+
+def pick(blocks, which):
+    return jnp.stack([blocks[b] for b in which])
+
+
+WAYS = (0, 1)
 
 
 def body(queries, output_gradient, response_keys, response_values, prompt_key_rows, prompt_value_rows, prompt_index):
-    prompts = lax.axis_size("wide")
+    here = lax.axis_index("wide").astype(jnp.int32)
     order, owners = paired_order(prompt_index[:, 0])
-    held = by_head(prompt_key_rows[0], prompt_value_rows[0])
+    owners = owners ^ here
+    spot = jnp.stack([lax.axis_index("narrow").astype(jnp.int32), here])
+
+    held = jnp.concatenate([prompt_key_rows[0], prompt_value_rows[0]], axis=1)
     gathered = lax.all_gather(held, ("wide", "narrow"), axis=0, tiled=True)
-    gathered = gathered.reshape(prompts, -1, held.shape[1])
-    dq, drk, drv, partial = attend(
-        order, owners, queries, output_gradient, response_keys, response_values, gathered, 0, KEY_VALUE_HEADS
-    )
-    partial = partial.reshape(-1, held.shape[1])
-    sums = lax.psum_scatter(partial, "wide", scatter_dimension=0, tiled=True)
-    sums = lax.psum_scatter(sums, "narrow", scatter_dimension=0, tiled=True)
-    split = sums.reshape(1, -1, KEY_VALUE_HEADS, 2, HEAD)
-    shape = prompt_key_rows.shape
-    return dq, drk, drv, split[:, :, :, 0].reshape(shape), split[:, :, :, 1].reshape(shape)
+    gathered = gathered.reshape(-1, 4, held.shape[0], held.shape[1])
+
+    def run(head, *gates):
+        return attend(
+            order, owners, spot, queries, output_gradient, response_keys, response_values, gathered, head, gates
+        )
+
+    def over_core(head, result):
+        sent_there, kept_there = swap(result[8], "c", 1), swap(result[7], "c", 1)
+        return {
+            (way, head): (result[3 + 2 * way] + kept_there[way], result[4 + 2 * way] + sent_there[way])
+            for way in WAYS
+        }
+
+    def near_first(sums):
+        return {(w, h): halve_near(kept, sent, w, FIRST[h]) for (w, h), (kept, sent) in sums.items()}
+
+    def far_first(halves, *gates):
+        return {(w, h): halve_far(mine, after(far, *gates), w, FIRST[h]) for (w, h), (mine, far) in halves.items()}
+
+    def second(mine, *gates):
+        out = {}
+        for (w, h), blocks in mine.items():
+            blocks, axis = after(blocks, *gates), other(FIRST[h])
+            kept, sent = pick(blocks, KEEP_SEND[w][0]), pick(blocks, KEEP_SEND[w][1])
+            out[w, h] = halve_far(*halve_near(kept, sent, w, axis), w, axis)
+        return out
+
+    def flat(pairs):
+        return [array for pair in pairs.values() for array in pair]
+
+    results = {0: run(0)}
+    results[1] = run(1, results[0][1])
+    sums = over_core(0, results[0]) | over_core(1, results[1])
+    results[2] = run(2, *flat(sums))
+    halves = near_first(sums)
+    results[3] = run(3, results[2][1], *flat(halves))
+    mine = far_first(halves, results[2][1])
+    total = second(mine, results[3][1])
+    sums = over_core(2, results[2]) | over_core(3, results[3])
+    total |= second(far_first(near_first(sums)))
+    joined = jnp.concatenate([total[w, h] for w in WAYS for h in range(KEY_VALUE_HEADS)], axis=-1)
+    summed = sum_z(joined)
+    width = summed.shape[1] // 2
+    key_sum, value_sum = summed[:, :width], summed[:, width:]
+    dq, drk, drv = (jnp.concatenate([results[h][i] for h in range(KEY_VALUE_HEADS)], axis=1) for i in range(3))
+    return dq, drk, drv, key_sum[None], value_sum[None]
 
 
 def solution(mesh):

time: 526 us -> 450 us (0.86)
  waiting for transfers between devices: 437 us -> 269 us
  starting transfers between devices: 0.12 us -> 56.3 us
  other arithmetic: 4.05 us -> 25.1 us
  Pallas kernels: 65.1 us -> 77.8 us
    reduce_scatter x2 -> x0, waiting for transfers between devices: 284 us -> none  [the longest x1 258 us: body(): sums = lax.psum_scatter(partial, 'wide', scatter_dimension=0, tiled=True)]
    ppermute x0 -> x47, waiting for transfers between devices: none -> 115 us  [swap(): lax.ppermute(array, ('wide', 'narrow'), [(i, i ^ flip) for i in range(cou...]
    ppermute x0 -> x47, starting transfers between devices: none -> 56.3 us  [swap(): lax.ppermute(array, ('wide', 'narrow'), [(i, i ^ flip) for i in range(cou...]
    add x0 -> x32, other arithmetic: none -> 15.8 us  [the longest x8 5.52 us: halve_far(): return mine + swap(other_sum, axis, NEAR_FAR[way][1])]
    pallas_call x1 -> x4, Pallas kernels: 65.1 us -> 77.8 us  [attend(): pl.pallas_call(functools.partial(attend_kernel, FIRST[head], head), grid_...]
  transfers between devices with their start and end apart: 3 -> 48, of which waited for: 3 -> 24; matrix products, arithmetic and copies ran while one was open for 1% -> 5% of each run, Pallas kernels for 0% -> 9%
where the time goes in v2:
time: 450 us; the launch traced here: 448 us
  waiting for transfers between devices  269 us (60%)
  Pallas kernels  77.8 us (17%)
  starting transfers between devices  56.3 us (13%)
  other arithmetic  25.1 us (6%)
  between operations  15.2 us (3%)
    all_gather x1, waiting for transfers between devices, body(): gathered = lax.all_gather(held, ('wide', 'narrow'), axis=0, tiled=True)  155 us
    ppermute x47, waiting for transfers between devices, swap(): lax.ppermute(array, ('wide', 'narrow'), [(i, i ^ flip) for i in range(cou...  115 us
    pallas_call x4, Pallas kernels, attend(): pl.pallas_call(functools.partial(attend_kernel, FIRST[head], head), grid_...  77.8 us
    ppermute x47, starting transfers between devices, swap(): lax.ppermute(array, ('wide', 'narrow'), [(i, i ^ flip) for i in range(cou...  56.3 us
  transfers between devices with their start and end apart: 48, of which 24 were waited for; matrix products, arithmetic and copies ran while one was open for 5% of the time, Pallas kernels for 9%

profile of v2, /device:TPU:8, one launch (start us, length us, event | category | flops | bytes accessed | tf_op | source)
XLA Modules:
  0.0 447.6 jit_solution(18349753089855738420)
XLA Ops:
  13.0 154.6 %all-gather.2.cloned.1.call-done = bf16[16384,1024]{1,0:T(8,128)(2,1)} async-done(((bf16[64,1024]{1,0:T(8,128)(2,1)}), bf16[16384,1024]{1,0:T(8,128)(2,1)}) %all-gather.2.cloned.1.call-update) | async-done | bytes 33554448 | tf_op jit(solution)/shard_map/all_gather | solution.py:290
  169.6 19.5 %shard_map.110 = (bf16[384,1024]{1,0:T(8,128)(2,1)S(1)}, bf16[384,128]{1,0:T(8,128)(2,1)S(1)}, bf16[384,128]{1,0:T(8,128)(2,1)S(1)}, bf16[2,4,8,64,128]{4,3,2,1,...) custom-call(s32[48]{0:T(128)S(1)} %get-tuple-element.71.order, ...), custom_call_target="tpu_custom_call" | custom-call | flops 1006632960 | bytes 69468160 | tf_op jit(solution)/shard_map/pallas_call | solution.py:206
  189.1 19.5 %shard_map.111 = (bf16[384,1024]{1,0:T(8,128)(2,1)S(1)}, bf16[384,128]{1,0:T(8,128)(2,1)S(1)}, bf16[384,128]{1,0:T(8,128)(2,1)S(1)}, bf16[2,4,8,64,128]{4,3,2,1,...) custom-call(s32[48]{0:T(128)S(1)} %get-tuple-element.71.order, ...), custom_call_target="tpu_custom_call" | custom-call | flops 1006632960 | bytes 69468160 | tf_op jit(solution)/shard_map/pallas_call | solution.py:206
  209.7 3.3 collective-permute-done.3
  222.8 19.5 %shard_map.112 = (bf16[384,1024]{1,0:T(8,128)(2,1)S(1)}, bf16[384,128]{1,0:T(8,128)(2,1)S(1)}, bf16[384,128]{1,0:T(8,128)(2,1)S(1)}, bf16[2,4,8,64,128]{4,3,2,1,...) custom-call(s32[48]{0:T(128)S(1)} %get-tuple-element.71.order, ...), custom_call_target="tpu_custom_call" | custom-call | flops 1006632960 | bytes 69468160 | tf_op jit(solution)/shard_map/pallas_call | solution.py:206
  251.4 6.7 %collective-permute-done.29 = bf16[4,8,64,128]{3,2,1,0:T(8,128)(2,1)S(1)} collective-permute-done((bf16[4,8,64,128]{3,2,1,0:T(8,128)(2,1)S(1)}, bf16[4,8,64,128]{3,2,1,0:T(8,128)(2,1)S(1)}, u32[]{:S(2)}, u32[]{:S(2)}) %collective-permute-start.29) | collective-permute-done | bytes 524320 | tf_op jit(solution)/shard_map/ppermute | solution.py:249
  264.4 8.0 %collective-permute-done.8 = bf16[4,8,64,128]{3,2,1,0:T(8,128)(2,1)S(1)} collective-permute-done((bf16[4,8,64,128]{3,2,1,0:T(8,128)(2,1)S(1)}, bf16[4,8,64,128]{3,2,1,0:T(8,128)(2,1)S(1)}, u32[]{:S(2)}, u32[]{:S(2)}) %collective-permute-start.8) | collective-permute-done | bytes 524320 | tf_op jit(solution)/shard_map/ppermute | solution.py:249
  274.3 19.4 %shard_map.113 = (bf16[384,1024]{1,0:T(8,128)(2,1)S(1)}, bf16[384,128]{1,0:T(8,128)(2,1)S(1)}, bf16[384,128]{1,0:T(8,128)(2,1)S(1)}, bf16[2,4,8,64,128]{4,3,2,1,...) custom-call(s32[48]{0:T(128)S(1)} %get-tuple-element.71.order, ...), custom_call_target="tpu_custom_call" | custom-call | flops 1006632960 | bytes 69468160 | tf_op jit(solution)/shard_map/pallas_call | solution.py:206
  297.0 6.9 %collective-permute-done.30 = bf16[2,8,64,128]{3,2,1,0:T(8,128)(2,1)S(1)} collective-permute-done((bf16[2,8,64,128]{3,2,1,0:T(8,128)(2,1)S(1)}, bf16[2,8,64,128]{3,2,1,0:T(8,128)(2,1)S(1)}, u32[]{:S(2)}, u32[]{:S(2)}) %collective-permute-start.30) | collective-permute-done | bytes 262176 | tf_op jit(solution)/shard_map/ppermute | solution.py:249
  306.8 5.1 %collective-permute-done.9 = bf16[2,8,64,128]{3,2,1,0:T(8,128)(2,1)S(1)} collective-permute-done((bf16[2,8,64,128]{3,2,1,0:T(8,128)(2,1)S(1)}, bf16[2,8,64,128]{3,2,1,0:T(8,128)(2,1)S(1)}, u32[]{:S(2)}, u32[]{:S(2)}) %collective-permute-start.9) | collective-permute-done | bytes 262176 | tf_op jit(solution)/shard_map/ppermute | solution.py:249
  321.4 20.4 %collective-permute-done.32 = bf16[2,4,8,64,128]{4,3,2,1,0:T(8,128)(2,1)S(1)} collective-permute-done((bf16[2,4,8,64,128]{4,3,2,1,0:T(8,128)(2,1)S(1)}, bf16[2,4,8,64,128]{4,3,2,1,0:T(8,128)(2,1)S(1)}, u32[]{:S(2)}, u32[]{:S(2)}) %collective-permute-start.32) | collective-permute-done | bytes 1048608 | tf_op jit(solution)/shard_map/ppermute | solution.py:249
  345.9 10.0 %collective-permute-done.33 = bf16[4,8,64,128]{3,2,1,0:T(8,128)(2,1)S(1)} collective-permute-done((bf16[4,8,64,128]{3,2,1,0:T(8,128)(2,1)S(1)}, bf16[4,8,64,128]{3,2,1,0:T(8,128)(2,1)S(1)}, u32[]{:S(2)}, u32[]{:S(2)}) %collective-permute-start.33) | collective-permute-done | bytes 524320 | tf_op jit(solution)/shard_map/ppermute | solution.py:249
  356.8 3.4 collective-permute-start.22
  361.7 19.5 %collective-permute-done.36 = bf16[2,4,8,64,128]{4,3,2,1,0:T(8,128)(2,1)S(1)} collective-permute-done((bf16[2,4,8,64,128]{4,3,2,1,0:T(8,128)(2,1)S(1)}, bf16[2,4,8,64,128]{4,3,2,1,0:T(8,128)(2,1)S(1)}, u32[]{:S(2)}, u32[]{:S(2)}) %collective-permute-start.36) | collective-permute-done | bytes 1048608 | tf_op jit(solution)/shard_map/ppermute | solution.py:249
  385.6 4.9 %collective-permute-done.18 = bf16[2,8,64,128]{3,2,1,0:T(8,128)(2,1)S(1)} collective-permute-done((bf16[2,8,64,128]{3,2,1,0:T(8,128)(2,1)S(1)}, bf16[2,8,64,128]{3,2,1,0:T(8,128)(2,1)S(1)}, u32[]{:S(2)}, u32[]{:S(2)}) %collective-permute-start.18) | collective-permute-done | bytes 262176 | tf_op jit(solution)/shard_map/ppermute | solution.py:249
  392.6 4.8 %collective-permute-done.37 = bf16[4,8,64,128]{3,2,1,0:T(8,128)(2,1)S(1)} collective-permute-done((bf16[4,8,64,128]{3,2,1,0:T(8,128)(2,1)S(1)}, bf16[4,8,64,128]{3,2,1,0:T(8,128)(2,1)S(1)}, u32[]{:S(2)}, u32[]{:S(2)}) %collective-permute-start.37) | collective-permute-done | bytes 524320 | tf_op jit(solution)/shard_map/ppermute | solution.py:249
  399.5 2.9 collective-permute-done.19
  407.5 2.5 collective-permute-done.38
  412.2 2.9 collective-permute-done.39
  415.3 3.4 collective-permute-start.41
  421.5 3.0 collective-permute-start.43
  425.6 3.2 collective-permute-start.45
  432.2 3.7 collective-permute-done.44
  437.3 2.6 collective-permute-done.46
  (162 shorter events, 82.8 us)
Async XLA Ops:
  7.2 160.5 %all-gather.2.cloned.1.call-start = ((), (), s32[]{:S(2)}) async-start(), calls=%async_computation | async-start | bytes 33685504 | tf_op jit(solution)/shard_map/all_gather | solution.py:290
  209.4 13.1 %collective-permute-start = (bf16[2,2,4,8,64,128]{5,4,3,2,1,0:T(8,128)(2,1)S(1)}, bf16[2,2,4,8,64,128]{5,4,3,2,1,0:T(8,128)(2,1)S(1)}, u32[]{:S(2)}, u32[]{:S(2)}) collective-permute-start(bf16[2,2,4,8,64,128]{5,4,3,2,1,0:T(8,128)(2,1)S(1)} %copy-done.7), channel_id=1, source_target_pairs={{0,4},{1,5},{2,6},{3,7},{4,0},{5,1},{6,2},{7,3},{8,12},{9,13},{10,... | collective-permute-start | bytes 6291464 | tf_op jit(solution)/shard_map/ppermute | solution.py:249
  214.7 27.7 %collective-permute-start.7 = (bf16[2,4,8,64,128]{4,3,2,1,0:T(8,128)(2,1)}, bf16[2,4,8,64,128]{4,3,2,1,0:T(8,128)(2,1)}, u32[]{:S(2)}, u32[]{:S(2)}) collective-permute-start(bf16[2,4,8,64,128]{4,3,2,1,0:T(8,128)(2,1)} %get-tuple-element.121), channel_id=1, source_target_pairs={{0,24},{1,25},{2,26},{3,27},{4,28},{5,29},{6,30},{7,31},{8,16},{9,... | collective-permute-start | bytes 3145736 | tf_op jit(solution)/shard_map/ppermute | solution.py:249
  216.2 27.9 %collective-permute-start.6 = (bf16[2,4,8,64,128]{4,3,2,1,0:T(8,128)(2,1)}, bf16[2,4,8,64,128]{4,3,2,1,0:T(8,128)(2,1)S(1)}, u32[]{:S(2)}, u32[]{:S(2)}) collective-permute-start(bf16[2,4,8,64,128]{4,3,2,1,0:T(8,128)(2,1)} %get-tuple-element.122), channel_id=1, source_target_pairs={{0,8},{1,9},{2,10},{3,11},{4,12},{5,13},{6,14},{7,15},{8,0},{9,1},... | collective-permute-start | bytes 3145736 | tf_op jit(solution)/shard_map/ppermute | solution.py:249
  220.7 26.9 %collective-permute-start.5 = (bf16[2,4,8,64,128]{4,3,2,1,0:T(8,128)(2,1)}, bf16[2,4,8,64,128]{4,3,2,1,0:T(8,128)(2,1)}, u32[]{:S(2)}, u32[]{:S(2)}) collective-permute-start(bf16[2,4,8,64,128]{4,3,2,1,0:T(8,128)(2,1)} %get-tuple-element.125), channel_id=1, source_target_pairs={{0,3},{1,2},{2,1},{3,0},{4,7},{5,6},{6,5},{7,4},{8,11},{9,10},{10,... | collective-permute-start | bytes 3145736 | tf_op jit(solution)/shard_map/ppermute | solution.py:249
  222.0 28.1 %collective-permute-start.4 = (bf16[2,4,8,64,128]{4,3,2,1,0:T(8,128)(2,1)}, bf16[2,4,8,64,128]{4,3,2,1,0:T(8,128)(2,1)}, u32[]{:S(2)}, u32[]{:S(2)}) collective-permute-start(bf16[2,4,8,64,128]{4,3,2,1,0:T(8,128)(2,1)} %get-tuple-element.126), channel_id=1, source_target_pairs={{0,1},{1,0},{2,3},{3,2},{4,5},{5,4},{6,7},{7,6},{8,9},{9,8},{10,11... | collective-permute-start | bytes 3145736 | tf_op jit(solution)/shard_map/ppermute | solution.py:249
  242.3 76.8 %collective-permute-start.14 = (bf16[2,2,4,8,64,128]{5,4,3,2,1,0:T(8,128)(2,1)}, bf16[2,2,4,8,64,128]{5,4,3,2,1,0:T(8,128)(2,1)S(1)}, u32[]{:S(2)}, u32[]{:S(2)}) collective-permute-start(bf16[2,2,4,8,64,128]{5,4,3,2,1,0:T(8,128)(2,1)} %get-tuple-element.84), channel_id=1, source_target_pairs={{0,4},{1,5},{2,6},{3,7},{4,0},{5,1},{6,2},{7,3},{8,12},{9,13},{10,... | collective-permute-start | bytes 6291464 | tf_op jit(solution)/shard_map/ppermute | solution.py:249
  242.4 71.2 %collective-permute-start.15 = (bf16[2,2,4,8,64,128]{5,4,3,2,1,0:T(8,128)(2,1)}, bf16[2,2,4,8,64,128]{5,4,3,2,1,0:T(8,128)(2,1)}, u32[]{:S(2)}, u32[]{:S(2)}) collective-permute-start(bf16[2,2,4,8,64,128]{5,4,3,2,1,0:T(8,128)(2,1)} %get-tuple-element.86), channel_id=1, source_target_pairs={{0,4},{1,5},{2,6},{3,7},{4,0},{5,1},{6,2},{7,3},{8,12},{9,13},{10,... | collective-permute-start | bytes 6291464 | tf_op jit(solution)/shard_map/ppermute | solution.py:249
  244.1 14.0 %collective-permute-start.29 = (bf16[4,8,64,128]{3,2,1,0:T(8,128)(2,1)S(1)}, bf16[4,8,64,128]{3,2,1,0:T(8,128)(2,1)S(1)}, u32[]{:S(2)}, u32[]{:S(2)}) collective-permute-start(bf16[4,8,64,128]{3,2,1,0:T(8,128)(2,1)S(1)} %fusion.28), channel_id=1, source_target_pairs={{0,8},{1,9},{2,10},{3,11},{4,12},{5,13},{6,14},{7,15},{8,0},{9,1},... | collective-permute-start | bytes 1572872 | tf_op jit(solution)/shard_map/ppermute | solution.py:249
  247.5 13.5 %collective-permute-start.11 = (bf16[4,8,64,128]{3,2,1,0:T(8,128)(2,1)S(1)}, bf16[4,8,64,128]{3,2,1,0:T(8,128)(2,1)S(1)}, u32[]{:S(2)}, u32[]{:S(2)}) collective-permute-start(bf16[4,8,64,128]{3,2,1,0:T(8,128)(2,1)S(1)} %fusion.30), channel_id=1, source_target_pairs={{0,24},{1,25},{2,26},{3,27},{4,28},{5,29},{6,30},{7,31},{8,16},{9,... | collective-permute-start | bytes 1572872 | tf_op jit(solution)/shard_map/ppermute | solution.py:249
  258.1 14.3 %collective-permute-start.8 = (bf16[4,8,64,128]{3,2,1,0:T(8,128)(2,1)S(1)}, bf16[4,8,64,128]{3,2,1,0:T(8,128)(2,1)S(1)}, u32[]{:S(2)}, u32[]{:S(2)}) collective-permute-start(bf16[4,8,64,128]{3,2,1,0:T(8,128)(2,1)S(1)} %fusion.34), channel_id=1, source_target_pairs={{0,3},{1,2},{2,1},{3,0},{4,7},{5,6},{6,5},{7,4},{8,11},{9,10},{10,... | collective-permute-start | bytes 1572872 | tf_op jit(solution)/shard_map/ppermute | solution.py:249
  293.7 50.1 %collective-permute-start.21 = (bf16[2,2,4,8,64,128]{5,4,3,2,1,0:T(8,128)(2,1)}, bf16[2,2,4,8,64,128]{5,4,3,2,1,0:T(8,128)(2,1)S(1)}, u32[]{:S(2)}, u32[]{:S(2)}) collective-permute-start(bf16[2,2,4,8,64,128]{5,4,3,2,1,0:T(8,128)(2,1)} %get-tuple-element.90), channel_id=1, source_target_pairs={{0,4},{1,5},{2,6},{3,7},{4,0},{5,1},{6,2},{7,3},{8,12},{9,13},{10,... | collective-permute-start | bytes 6291464 | tf_op jit(solution)/shard_map/ppermute | solution.py:249
  317.2 24.6 %collective-permute-start.32 = (bf16[2,4,8,64,128]{4,3,2,1,0:T(8,128)(2,1)S(1)}, bf16[2,4,8,64,128]{4,3,2,1,0:T(8,128)(2,1)S(1)}, u32[]{:S(2)}, u32[]{:S(2)}) collective-permute-start(bf16[2,4,8,64,128]{4,3,2,1,0:T(8,128)(2,1)S(1)} %get-tuple-element.119), channel_id=1, source_target_pairs={{0,3},{1,2},{2,1},{3,0},{4,7},{5,6},{6,5},{7,4},{8,11},{9,10},{10,... | collective-permute-start | bytes 3145736 | tf_op jit(solution)/shard_map/ppermute | solution.py:249
  318.7 24.9 %collective-permute-start.16 = (bf16[2,4,8,64,128]{4,3,2,1,0:T(8,128)(2,1)S(1)}, bf16[2,4,8,64,128]{4,3,2,1,0:T(8,128)(2,1)S(1)}, u32[]{:S(2)}, u32[]{:S(2)}) collective-permute-start(bf16[2,4,8,64,128]{4,3,2,1,0:T(8,128)(2,1)S(1)} %get-tuple-element.120), channel_id=1, source_target_pairs={{0,1},{1,0},{2,3},{3,2},{4,5},{5,4},{6,7},{7,6},{8,9},{9,8},{10,11... | collective-permute-start | bytes 3145736 | tf_op jit(solution)/shard_map/ppermute | solution.py:249
  318.9 41.5 %collective-permute-start.20 = (bf16[2,2,4,8,64,128]{5,4,3,2,1,0:T(8,128)(2,1)S(1)}, bf16[2,2,4,8,64,128]{5,4,3,2,1,0:T(8,128)(2,1)S(1)}, u32[]{:S(2)}, u32[]{:S(2)}) collective-permute-start(bf16[2,2,4,8,64,128]{5,4,3,2,1,0:T(8,128)(2,1)S(1)} %copy-done.6), channel_id=1, source_target_pairs={{0,4},{1,5},{2,6},{3,7},{4,0},{5,1},{6,2},{7,3},{8,12},{9,13},{10,... | collective-permute-start | bytes 6291464 | tf_op jit(solution)/shard_map/ppermute | solution.py:249
  319.1 92.9 %collective-permute-start.31 = (bf16[8,64,128]{2,1,0:T(8,128)(2,1)S(1)}, bf16[8,64,128]{2,1,0:T(8,128)(2,1)S(1)}, u32[]{:S(2)}, u32[]{:S(2)}) collective-permute-start(bf16[8,64,128]{2,1,0:T(8,128)(2,1)S(1)} %fusion.51), channel_id=1, source_target_pairs={{0,1},{1,0},{2,3},{3,2},{4,5},{5,4},{6,7},{7,6},{8,9},{9,8},{10,11... | collective-permute-start | bytes 393224 | tf_op jit(solution)/shard_map/ppermute | solution.py:249
  341.8 70.1 %collective-permute-start.28 = (bf16[8,64,128]{2,1,0:T(8,128)(2,1)S(1)}, bf16[8,64,128]{2,1,0:T(8,128)(2,1)S(1)}, u32[]{:S(2)}, u32[]{:S(2)}) collective-permute-start(bf16[8,64,128]{2,1,0:T(8,128)(2,1)S(1)} %fusion.55), channel_id=1, source_target_pairs={{0,8},{1,9},{2,10},{3,11},{4,12},{5,13},{6,14},{7,15},{8,0},{9,1},... | collective-permute-start | bytes 393224 | tf_op jit(solution)/shard_map/ppermute | solution.py:249
  355.9 25.3 %collective-permute-start.36 = (bf16[2,4,8,64,128]{4,3,2,1,0:T(8,128)(2,1)S(1)}, bf16[2,4,8,64,128]{4,3,2,1,0:T(8,128)(2,1)S(1)}, u32[]{:S(2)}, u32[]{:S(2)}) collective-permute-start(bf16[2,4,8,64,128]{4,3,2,1,0:T(8,128)(2,1)S(1)} %get-tuple-element.115), channel_id=1, source_target_pairs={{0,24},{1,25},{2,26},{3,27},{4,28},{5,29},{6,30},{7,31},{8,16},{9,... | collective-permute-start | bytes 3145736 | tf_op jit(solution)/shard_map/ppermute | solution.py:249
  356.8 26.6 %collective-permute-start.22 = (bf16[2,4,8,64,128]{4,3,2,1,0:T(8,128)(2,1)S(1)}, bf16[2,4,8,64,128]{4,3,2,1,0:T(8,128)(2,1)S(1)}, u32[]{:S(2)}, u32[]{:S(2)}) collective-permute-start(bf16[2,4,8,64,128]{4,3,2,1,0:T(8,128)(2,1)S(1)} %get-tuple-element.116), channel_id=1, source_target_pairs={{0,8},{1,9},{2,10},{3,11},{4,12},{5,13},{6,14},{7,15},{8,0},{9,1},... | collective-permute-start | bytes 3145736 | tf_op jit(solution)/shard_map/ppermute | solution.py:249
  360.4 24.5 %collective-permute-start.34 = (bf16[2,8,64,128]{3,2,1,0:T(8,128)(2,1)S(1)}, bf16[2,8,64,128]{3,2,1,0:T(8,128)(2,1)S(1)}, u32[]{:S(2)}, u32[]{:S(2)}) collective-permute-start(bf16[2,8,64,128]{3,2,1,0:T(8,128)(2,1)S(1)} %pad_maximum_fusion.5), channel_id=1, source_target_pairs={{0,24},{1,25},{2,26},{3,27},{4,28},{5,29},{6,30},{7,31},{8,16},{9,... | collective-permute-start | bytes 786440 | tf_op jit(solution)/shard_map/ppermute | solution.py:249
  383.4 14.0 %collective-permute-start.37 = (bf16[4,8,64,128]{3,2,1,0:T(8,128)(2,1)S(1)}, bf16[4,8,64,128]{3,2,1,0:T(8,128)(2,1)S(1)}, u32[]{:S(2)}, u32[]{:S(2)}) collective-permute-start(bf16[4,8,64,128]{3,2,1,0:T(8,128)(2,1)S(1)} %fusion.16), channel_id=1, source_target_pairs={{0,8},{1,9},{2,10},{3,11},{4,12},{5,13},{6,14},{7,15},{8,0},{9,1},... | collective-permute-start | bytes 1572872 | tf_op jit(solution)/shard_map/ppermute | solution.py:249
  384.9 13.9 %collective-permute-start.23 = (bf16[4,8,64,128]{3,2,1,0:T(8,128)(2,1)S(1)}, bf16[4,8,64,128]{3,2,1,0:T(8,128)(2,1)S(1)}, u32[]{:S(2)}, u32[]{:S(2)}) collective-permute-start(bf16[4,8,64,128]{3,2,1,0:T(8,128)(2,1)S(1)} %fusion.22), channel_id=1, source_target_pairs={{0,24},{1,25},{2,26},{3,27},{4,28},{5,29},{6,30},{7,31},{8,16},{9,... | collective-permute-start | bytes 1572872 | tf_op jit(solution)/shard_map/ppermute | solution.py:249
  390.6 21.5 %collective-permute-start.35 = (bf16[8,64,128]{2,1,0:T(8,128)(2,1)S(1)}, bf16[8,64,128]{2,1,0:T(8,128)(2,1)S(1)}, u32[]{:S(2)}, u32[]{:S(2)}) collective-permute-start(bf16[8,64,128]{2,1,0:T(8,128)(2,1)S(1)} %fusion.47), channel_id=1, source_target_pairs={{0,8},{1,9},{2,10},{3,11},{4,12},{5,13},{6,14},{7,15},{8,0},{9,1},... | collective-permute-start | bytes 393224 | tf_op jit(solution)/shard_map/ppermute | solution.py:249
  415.3 13.5 %collective-permute-start.41 = (bf16[64,1024]{1,0:T(8,128)(2,1)S(1)}, bf16[64,1024]{1,0:T(8,128)(2,1)S(1)}, u32[]{:S(2)}, u32[]{:S(2)}) collective-permute-start(bf16[64,1024]{1,0:T(8,128)(2,1)S(1)} %get-tuple-element.135), channel_id=1, source_target_pairs={{0,64},{1,65},{2,66},{3,67},{4,68},{5,69},{6,70},{7,71},{8,72},{9,... | collective-permute-start | bytes 393224 | tf_op jit(solution)/shard_map/ppermute | solution.py:249
  (32 other events, 275.8 us)
Sparse Core Ops, SparseCore 0:
  12.4 155.1 all-gather.1

commit v3 on v2

--- a/solution.py
+++ b/solution.py
@@ -295,40 +295,42 @@
             order, owners, spot, queries, output_gradient, response_keys, response_values, gathered, head, gates
         )
 
-    def over_core(head, result):
-        sent_there, kept_there = swap(result[8], "c", 1), swap(result[7], "c", 1)
-        return {
-            (way, head): (result[3 + 2 * way] + kept_there[way], result[4 + 2 * way] + sent_there[way])
-            for way in WAYS
-        }
-
-    def near_first(sums):
-        return {(w, h): halve_near(kept, sent, w, FIRST[h]) for (w, h), (kept, sent) in sums.items()}
-
-    def far_first(halves, *gates):
-        return {(w, h): halve_far(mine, after(far, *gates), w, FIRST[h]) for (w, h), (mine, far) in halves.items()}
-
-    def second(mine, *gates):
-        out = {}
-        for (w, h), blocks in mine.items():
-            blocks, axis = after(blocks, *gates), other(FIRST[h])
-            kept, sent = pick(blocks, KEEP_SEND[w][0]), pick(blocks, KEEP_SEND[w][1])
-            out[w, h] = halve_far(*halve_near(kept, sent, w, axis), w, axis)
-        return out
-
-    def flat(pairs):
-        return [array for pair in pairs.values() for array in pair]
-
     results = {0: run(0)}
     results[1] = run(1, results[0][1])
-    sums = over_core(0, results[0]) | over_core(1, results[1])
-    results[2] = run(2, *flat(sums))
-    halves = near_first(sums)
-    results[3] = run(3, results[2][1], *flat(halves))
-    mine = far_first(halves, results[2][1])
-    total = second(mine, results[3][1])
-    sums = over_core(2, results[2]) | over_core(3, results[3])
-    total |= second(far_first(near_first(sums)))
+
+    def over_core(heads, slot):
+        there = {h: swap(results[h][7 + slot], "c", 1) for h in heads}
+        return {(w, h): results[h][3 + 2 * w + slot] + there[h][w] for h in heads for w in WAYS}
+
+    def near_first(sent):
+        return {(w, h): swap(array, FIRST[h], NEAR_FAR[w][0]) for (w, h), array in sent.items()}
+
+    def far_first(kept, got, *gates):
+        out = {}
+        for (w, h), mine in kept.items():
+            far = after(mine[1] + got[w, h][1], *gates)
+            out[w, h] = mine[0] + got[w, h][0] + swap(far, FIRST[h], NEAR_FAR[w][1])
+        return out
+
+    sent = over_core((0, 1), 1)
+    got = near_first(sent)
+    kept = over_core((0, 1), 0)
+    results[2] = run(2, *sent.values())
+    results[3] = run(3, results[2][1])
+    mine = far_first(kept, got, results[3][1])
+    sent = over_core((2, 3), 1)
+    got = near_first(sent)
+    kept = over_core((2, 3), 0)
+    mine |= far_first(kept, got)
+    total = {}
+    for w in WAYS:
+        for axis in ("x", "y"):
+            heads = [h for h in range(KEY_VALUE_HEADS) if other(FIRST[h]) == axis]
+            blocks = jnp.concatenate([mine[w, h] for h in heads], axis=-1)
+            pairs = pick(blocks, KEEP_SEND[w][0]), pick(blocks, KEEP_SEND[w][1])
+            result = halve_far(*halve_near(*pairs, w, axis), w, axis)
+            for i, h in enumerate(heads):
+                total[w, h] = result[..., i * HEAD : (i + 1) * HEAD]
     joined = jnp.concatenate([total[w, h] for w in WAYS for h in range(KEY_VALUE_HEADS)], axis=-1)
     summed = sum_z(joined)
     width = summed.shape[1] // 2

time: 450 us -> 409 us (0.909)
  waiting for transfers between devices: 269 us -> 237 us
  starting transfers between devices: 56.3 us -> 45.4 us
    ppermute x47 -> x39, waiting for transfers between devices: 115 us -> 82.3 us  [swap(): lax.ppermute(array, ('wide', 'narrow'), [(i, i ^ flip) for i in range(cou...]
    add x8 -> x24, other arithmetic: 6.47 us -> 18.6 us  [the longest x8 8.92 us: over_core(): results[h][3 + 2 * w + slot] + there[h][w]]
    ppermute x47 -> x39, starting transfers between devices: 56.3 us -> 45.4 us  [swap(): lax.ppermute(array, ('wide', 'narrow'), [(i, i ^ flip) for i in range(cou...]
    add x8 -> x4, other arithmetic: 5.52 us -> 0.46 us  [halve_far(): return mine + swap(other_sum, axis, NEAR_FAR[way][1])]
  transfers between devices with their start and end apart: 48 -> 40, of which waited for: 24 -> 19; matrix products, arithmetic and copies ran while one was open for 5% -> 7% of each run, Pallas kernels for 9% -> 14%
where the time goes in v3:
time: 409 us; the launch traced here: 407 us
  waiting for transfers between devices  237 us (58%)
  Pallas kernels  77.6 us (19%)
  starting transfers between devices  45.4 us (11%)
  other arithmetic  28.3 us (7%)
  between operations  15.1 us (4%)
    all_gather x1, waiting for transfers between devices, body(): gathered = lax.all_gather(held, ('wide', 'narrow'), axis=0, tiled=True)  155 us
    ppermute x39, waiting for transfers between devices, swap(): lax.ppermute(array, ('wide', 'narrow'), [(i, i ^ flip) for i in range(cou...  82.3 us
    pallas_call x4, Pallas kernels, attend(): pl.pallas_call(functools.partial(attend_kernel, FIRST[head], head), grid_...  77.6 us
    ppermute x39, starting transfers between devices, swap(): lax.ppermute(array, ('wide', 'narrow'), [(i, i ^ flip) for i in range(cou...  45.4 us
    add x8, other arithmetic, over_core(): results[h][3 + 2 * w + slot] + there[h][w]  8.92 us
  transfers between devices with their start and end apart: 40, of which 19 were waited for; matrix products, arithmetic and copies ran while one was open for 7% of the time, Pallas kernels for 14%

profile of v3, /device:TPU:8, one launch (start us, length us, event | category | flops | bytes accessed | tf_op | source)
XLA Modules:
  0.0 406.8 jit_solution(6354207922091656018)
XLA Ops:
  13.0 154.6 %all-gather.2.cloned.1.call-done = bf16[16384,1024]{1,0:T(8,128)(2,1)} async-done(((bf16[64,1024]{1,0:T(8,128)(2,1)}), bf16[16384,1024]{1,0:T(8,128)(2,1)}) %all-gather.2.cloned.1.call-update) | async-done | bytes 33554448 | tf_op jit(solution)/shard_map/all_gather | solution.py:290
  169.6 19.4 %shard_map.110 = (bf16[384,1024]{1,0:T(8,128)(2,1)S(1)}, bf16[384,128]{1,0:T(8,128)(2,1)S(1)}, bf16[384,128]{1,0:T(8,128)(2,1)S(1)}, bf16[2,4,8,64,128]{4,3,2,1,...) custom-call(s32[48]{0:T(128)S(1)} %get-tuple-element.61.order, ...), custom_call_target="tpu_custom_call" | custom-call | flops 1006632960 | bytes 69468160 | tf_op jit(solution)/shard_map/pallas_call | solution.py:206
  189.4 19.4 %shard_map.111 = (bf16[384,1024]{1,0:T(8,128)(2,1)S(1)}, bf16[384,128]{1,0:T(8,128)(2,1)S(1)}, bf16[384,128]{1,0:T(8,128)(2,1)S(1)}, bf16[2,4,8,64,128]{4,3,2,1,...) custom-call(s32[48]{0:T(128)S(1)} %get-tuple-element.61.order, ...), custom_call_target="tpu_custom_call" | custom-call | flops 1006632960 | bytes 69468160 | tf_op jit(solution)/shard_map/pallas_call | solution.py:206
  209.6 3.1 fusion.14
  221.0 19.4 %shard_map.112 = (bf16[384,1024]{1,0:T(8,128)(2,1)S(1)}, bf16[384,128]{1,0:T(8,128)(2,1)S(1)}, bf16[384,128]{1,0:T(8,128)(2,1)S(1)}, bf16[2,4,8,64,128]{4,3,2,1,...) custom-call(s32[48]{0:T(128)S(1)} %get-tuple-element.61.order, ...), custom_call_target="tpu_custom_call" | custom-call | flops 1006632960 | bytes 69468160 | tf_op jit(solution)/shard_map/pallas_call | solution.py:206
  240.4 19.4 %shard_map.113 = (bf16[384,1024]{1,0:T(8,128)(2,1)S(1)}, bf16[384,128]{1,0:T(8,128)(2,1)S(1)}, bf16[384,128]{1,0:T(8,128)(2,1)S(1)}, bf16[2,4,8,64,128]{4,3,2,1,...) custom-call(s32[48]{0:T(128)S(1)} %get-tuple-element.61.order, ...), custom_call_target="tpu_custom_call" | custom-call | flops 1006632960 | bytes 69468160 | tf_op jit(solution)/shard_map/pallas_call | solution.py:206
  263.8 2.3 collective-permute-start.4
  269.4 9.8 %collective-permute-done.4 = bf16[4,8,64,128]{3,2,1,0:T(8,128)(2,1)S(1)} collective-permute-done((bf16[4,8,64,128]{3,2,1,0:T(8,128)(2,1)S(1)}, bf16[4,8,64,128]{3,2,1,0:T(8,128)(2,1)S(1)}, u32[]{:S(2)}, u32[]{:S(2)}) %collective-permute-start.4) | collective-permute-done | bytes 524320 | tf_op jit(solution)/shard_map/ppermute | solution.py:249
  283.0 9.6 %collective-permute-done.21 = bf16[4,8,64,128]{3,2,1,0:T(8,128)(2,1)S(1)} collective-permute-done((bf16[4,8,64,128]{3,2,1,0:T(8,128)(2,1)S(1)}, bf16[4,8,64,128]{3,2,1,0:T(8,128)(2,1)S(1)}, u32[]{:S(2)}, u32[]{:S(2)}) %collective-permute-start.21) | collective-permute-done | bytes 524320 | tf_op jit(solution)/shard_map/ppermute | solution.py:249
  296.3 8.7 %collective-permute-done.27 = bf16[4,8,64,128]{3,2,1,0:T(8,128)(2,1)S(1)} collective-permute-done((bf16[4,8,64,128]{3,2,1,0:T(8,128)(2,1)S(1)}, bf16[4,8,64,128]{3,2,1,0:T(8,128)(2,1)S(1)}, u32[]{:S(2)}, u32[]{:S(2)}) %collective-permute-start.27) | collective-permute-done | bytes 524320 | tf_op jit(solution)/shard_map/ppermute | solution.py:249
  306.4 2.2 collective-permute-start.28
  311.8 17.8 %collective-permute-done.28 = bf16[2,4,8,64,128]{4,3,2,1,0:T(8,128)(2,1)S(1)} collective-permute-done((bf16[2,4,8,64,128]{4,3,2,1,0:T(8,128)(2,1)S(1)}, bf16[2,4,8,64,128]{4,3,2,1,0:T(8,128)(2,1)S(1)}, u32[]{:S(2)}, u32[]{:S(2)}) %collective-permute-start.28) | collective-permute-done | bytes 1048608 | tf_op jit(solution)/shard_map/ppermute | solution.py:249
  329.6 2.4 collective-permute-start.29
  334.8 2.7 collective-permute-start.8
  337.5 4.7 %collective-permute-done.29 = bf16[4,8,64,128]{3,2,1,0:T(8,128)(2,1)S(1)} collective-permute-done((bf16[4,8,64,128]{3,2,1,0:T(8,128)(2,1)S(1)}, bf16[4,8,64,128]{3,2,1,0:T(8,128)(2,1)S(1)}, u32[]{:S(2)}, u32[]{:S(2)}) %collective-permute-start.29) | collective-permute-done | bytes 524320 | tf_op jit(solution)/shard_map/ppermute | solution.py:249
  344.1 4.3 %collective-permute-done.8 = bf16[4,8,64,128]{3,2,1,0:T(8,128)(2,1)S(1)} collective-permute-done((bf16[4,8,64,128]{3,2,1,0:T(8,128)(2,1)S(1)}, bf16[4,8,64,128]{3,2,1,0:T(8,128)(2,1)S(1)}, u32[]{:S(2)}, u32[]{:S(2)}) %collective-permute-start.8) | collective-permute-done | bytes 524320 | tf_op jit(solution)/shard_map/ppermute | solution.py:249
  349.8 2.1 collective-permute-start.24
  351.9 5.5 %collective-permute-done.30 = bf16[2,8,64,256]{3,2,1,0:T(8,128)(2,1)S(1)} collective-permute-done((bf16[2,8,64,256]{3,2,1,0:T(8,128)(2,1)S(1)}, bf16[2,8,64,256]{3,2,1,0:T(8,128)(2,1)S(1)}, u32[]{:S(2)}, u32[]{:S(2)}) %collective-permute-start.30) | collective-permute-done | bytes 524320 | tf_op jit(solution)/shard_map/ppermute | solution.py:249
  365.1 2.5 collective-permute-done.19
  368.6 2.8 collective-permute-start.38
  373.3 2.7 collective-permute-start.37
  379.7 2.9 collective-permute-start.34
  386.9 9.6 %collective-permute-done.36 = bf16[64,1024]{1,0:T(8,128)(2,1)S(1)} collective-permute-done((bf16[64,1024]{1,0:T(8,128)(2,1)S(1)}, bf16[64,1024]{1,0:T(8,128)(2,1)S(1)}, u32[]{:S(2)}, u32[]{:S(2)}) %collective-permute-start.36) | collective-permute-done | bytes 131104 | tf_op jit(solution)/shard_map/ppermute | solution.py:249
  396.5 2.6 collective-permute-done.33
  (136 shorter events, 61.2 us)
Async XLA Ops:
  7.2 160.5 %all-gather.2.cloned.1.call-start = ((), (), s32[]{:S(2)}) async-start(), calls=%async_computation | async-start | bytes 33685504 | tf_op jit(solution)/shard_map/all_gather | solution.py:290
  189.0 20.6 %collective-permute-start = (bf16[2,2,4,8,64,128]{5,4,3,2,1,0:T(8,128)(2,1)}, bf16[2,2,4,8,64,128]{5,4,3,2,1,0:T(8,128)(2,1)}, u32[]{:S(2)}, u32[]{:S(2)}) collective-permute-start(bf16[2,2,4,8,64,128]{5,4,3,2,1,0:T(8,128)(2,1)} %get-tuple-element.53), channel_id=1, source_target_pairs={{0,4},{1,5},{2,6},{3,7},{4,0},{5,1},{6,2},{7,3},{8,12},{9,13},{10,... | collective-permute-start | bytes 6291464 | tf_op jit(solution)/shard_map/ppermute | solution.py:249
  209.4 50.5 %collective-permute-start.11 = (bf16[2,2,4,8,64,128]{5,4,3,2,1,0:T(8,128)(2,1)}, bf16[2,2,4,8,64,128]{5,4,3,2,1,0:T(8,128)(2,1)}, u32[]{:S(2)}, u32[]{:S(2)}) collective-permute-start(bf16[2,2,4,8,64,128]{5,4,3,2,1,0:T(8,128)(2,1)} %get-tuple-element.77), channel_id=1, source_target_pairs={{0,4},{1,5},{2,6},{3,7},{4,0},{5,1},{6,2},{7,3},{8,12},{9,13},{10,... | collective-permute-start | bytes 6291464 | tf_op jit(solution)/shard_map/ppermute | solution.py:249
  212.7 54.6 %collective-permute-start.20 = (bf16[2,4,8,64,128]{4,3,2,1,0:T(8,128)(2,1)}, bf16[2,4,8,64,128]{4,3,2,1,0:T(8,128)(2,1)}, u32[]{:S(2)}, u32[]{:S(2)}) collective-permute-start(bf16[2,4,8,64,128]{4,3,2,1,0:T(8,128)(2,1)} %get-tuple-element.111), channel_id=1, source_target_pairs={{0,3},{1,2},{2,1},{3,0},{4,7},{5,6},{6,5},{7,4},{8,11},{9,10},{10,... | collective-permute-start | bytes 3145736 | tf_op jit(solution)/shard_map/ppermute | solution.py:249
  213.7 48.2 %collective-permute-start.3 = (bf16[2,4,8,64,128]{4,3,2,1,0:T(8,128)(2,1)}, bf16[2,4,8,64,128]{4,3,2,1,0:T(8,128)(2,1)}, u32[]{:S(2)}, u32[]{:S(2)}) collective-permute-start(bf16[2,4,8,64,128]{4,3,2,1,0:T(8,128)(2,1)} %get-tuple-element.112), channel_id=1, source_target_pairs={{0,1},{1,0},{2,3},{3,2},{4,5},{5,4},{6,7},{7,6},{8,9},{9,8},{10,11... | collective-permute-start | bytes 3145736 | tf_op jit(solution)/shard_map/ppermute | solution.py:249
  215.8 51.8 %collective-permute-start.26 = (bf16[2,4,8,64,128]{4,3,2,1,0:T(8,128)(2,1)}, bf16[2,4,8,64,128]{4,3,2,1,0:T(8,128)(2,1)}, u32[]{:S(2)}, u32[]{:S(2)}) collective-permute-start(bf16[2,4,8,64,128]{4,3,2,1,0:T(8,128)(2,1)} %get-tuple-element.109), channel_id=1, source_target_pairs={{0,24},{1,25},{2,26},{3,27},{4,28},{5,29},{6,30},{7,31},{8,16},{9,... | collective-permute-start | bytes 3145736 | tf_op jit(solution)/shard_map/ppermute | solution.py:249
  219.2 44.6 %collective-permute-start.12 = (bf16[2,4,8,64,128]{4,3,2,1,0:T(8,128)(2,1)}, bf16[2,4,8,64,128]{4,3,2,1,0:T(8,128)(2,1)}, u32[]{:S(2)}, u32[]{:S(2)}) collective-permute-start(bf16[2,4,8,64,128]{4,3,2,1,0:T(8,128)(2,1)} %get-tuple-element.110), channel_id=1, source_target_pairs={{0,8},{1,9},{2,10},{3,11},{4,12},{5,13},{6,14},{7,15},{8,0},{9,1},... | collective-permute-start | bytes 3145736 | tf_op jit(solution)/shard_map/ppermute | solution.py:249
  259.8 46.3 %collective-permute-start.15 = (bf16[2,2,4,8,64,128]{5,4,3,2,1,0:T(8,128)(2,1)}, bf16[2,2,4,8,64,128]{5,4,3,2,1,0:T(8,128)(2,1)S(1)}, u32[]{:S(2)}, u32[]{:S(2)}) collective-permute-start(bf16[2,2,4,8,64,128]{5,4,3,2,1,0:T(8,128)(2,1)} %get-tuple-element.82), channel_id=1, source_target_pairs={{0,4},{1,5},{2,6},{3,7},{4,0},{5,1},{6,2},{7,3},{8,12},{9,13},{10,... | collective-permute-start | bytes 6291464 | tf_op jit(solution)/shard_map/ppermute | solution.py:249
  262.1 47.9 %collective-permute-start.6 = (bf16[2,2,4,8,64,128]{5,4,3,2,1,0:T(8,128)(2,1)S(1)}, bf16[2,2,4,8,64,128]{5,4,3,2,1,0:T(8,128)(2,1)S(1)}, u32[]{:S(2)}, u32[]{:S(2)}) collective-permute-start(bf16[2,2,4,8,64,128]{5,4,3,2,1,0:T(8,128)(2,1)S(1)} %copy-done.5), channel_id=1, source_target_pairs={{0,4},{1,5},{2,6},{3,7},{4,0},{5,1},{6,2},{7,3},{8,12},{9,13},{10,... | collective-permute-start | bytes 6291464 | tf_op jit(solution)/shard_map/ppermute | solution.py:249
  263.8 15.4 %collective-permute-start.4 = (bf16[4,8,64,128]{3,2,1,0:T(8,128)(2,1)S(1)}, bf16[4,8,64,128]{3,2,1,0:T(8,128)(2,1)S(1)}, u32[]{:S(2)}, u32[]{:S(2)}) collective-permute-start(bf16[4,8,64,128]{3,2,1,0:T(8,128)(2,1)S(1)} %fusion.39), channel_id=1, source_target_pairs={{0,3},{1,2},{2,1},{3,0},{4,7},{5,6},{6,5},{7,4},{8,11},{9,10},{10,... | collective-permute-start | bytes 1572872 | tf_op jit(solution)/shard_map/ppermute | solution.py:249
  267.4 43.9 %collective-permute-start.14 = (bf16[2,2,4,8,64,128]{5,4,3,2,1,0:T(8,128)(2,1)S(1)}, bf16[2,2,4,8,64,128]{5,4,3,2,1,0:T(8,128)(2,1)S(1)}, u32[]{:S(2)}, u32[]{:S(2)}) collective-permute-start(bf16[2,2,4,8,64,128]{5,4,3,2,1,0:T(8,128)(2,1)S(1)} %copy-done.4), channel_id=1, source_target_pairs={{0,4},{1,5},{2,6},{3,7},{4,0},{5,1},{6,2},{7,3},{8,12},{9,13},{10,... | collective-permute-start | bytes 6291464 | tf_op jit(solution)/shard_map/ppermute | solution.py:249
  267.5 14.3 %collective-permute-start.13 = (bf16[4,8,64,128]{3,2,1,0:T(8,128)(2,1)S(1)}, bf16[4,8,64,128]{3,2,1,0:T(8,128)(2,1)S(1)}, u32[]{:S(2)}, u32[]{:S(2)}) collective-permute-start(bf16[4,8,64,128]{3,2,1,0:T(8,128)(2,1)S(1)} %fusion.33), channel_id=1, source_target_pairs={{0,24},{1,25},{2,26},{3,27},{4,28},{5,29},{6,30},{7,31},{8,16},{9,... | collective-permute-start | bytes 1572872 | tf_op jit(solution)/shard_map/ppermute | solution.py:249
  281.8 29.7 %collective-permute-start.5 = (bf16[2,2,4,8,64,128]{5,4,3,2,1,0:T(8,128)(2,1)S(1)}, bf16[2,2,4,8,64,128]{5,4,3,2,1,0:T(8,128)(2,1)S(1)}, u32[]{:S(2)}, u32[]{:S(2)}) collective-permute-start(bf16[2,2,4,8,64,128]{5,4,3,2,1,0:T(8,128)(2,1)S(1)} %copy-done.3), channel_id=1, source_target_pairs={{0,4},{1,5},{2,6},{3,7},{4,0},{5,1},{6,2},{7,3},{8,12},{9,13},{10,... | collective-permute-start | bytes 6291464 | tf_op jit(solution)/shard_map/ppermute | solution.py:249
  306.4 23.2 %collective-permute-start.28 = (bf16[2,4,8,64,128]{4,3,2,1,0:T(8,128)(2,1)S(1)}, bf16[2,4,8,64,128]{4,3,2,1,0:T(8,128)(2,1)S(1)}, u32[]{:S(2)}, u32[]{:S(2)}) collective-permute-start(bf16[2,4,8,64,128]{4,3,2,1,0:T(8,128)(2,1)S(1)} %get-tuple-element.99), channel_id=1, source_target_pairs={{0,24},{1,25},{2,26},{3,27},{4,28},{5,29},{6,30},{7,31},{8,16},{9,... | collective-permute-start | bytes 3145736 | tf_op jit(solution)/shard_map/ppermute | solution.py:249
  308.6 23.8 %collective-permute-start.16 = (bf16[2,4,8,64,128]{4,3,2,1,0:T(8,128)(2,1)S(1)}, bf16[2,4,8,64,128]{4,3,2,1,0:T(8,128)(2,1)S(1)}, u32[]{:S(2)}, u32[]{:S(2)}) collective-permute-start(bf16[2,4,8,64,128]{4,3,2,1,0:T(8,128)(2,1)S(1)} %get-tuple-element.100), channel_id=1, source_target_pairs={{0,8},{1,9},{2,10},{3,11},{4,12},{5,13},{6,14},{7,15},{8,0},{9,1},... | collective-permute-start | bytes 3145736 | tf_op jit(solution)/shard_map/ppermute | solution.py:249
  310.3 23.5 %collective-permute-start.22 = (bf16[2,4,8,64,128]{4,3,2,1,0:T(8,128)(2,1)S(1)}, bf16[2,4,8,64,128]{4,3,2,1,0:T(8,128)(2,1)S(1)}, u32[]{:S(2)}, u32[]{:S(2)}) collective-permute-start(bf16[2,4,8,64,128]{4,3,2,1,0:T(8,128)(2,1)S(1)} %get-tuple-element.105), channel_id=1, source_target_pairs={{0,3},{1,2},{2,1},{3,0},{4,7},{5,6},{6,5},{7,4},{8,11},{9,10},{10,... | collective-permute-start | bytes 3145736 | tf_op jit(solution)/shard_map/ppermute | solution.py:249
  311.3 23.5 %collective-permute-start.7 = (bf16[2,4,8,64,128]{4,3,2,1,0:T(8,128)(2,1)S(1)}, bf16[2,4,8,64,128]{4,3,2,1,0:T(8,128)(2,1)S(1)}, u32[]{:S(2)}, u32[]{:S(2)}) collective-permute-start(bf16[2,4,8,64,128]{4,3,2,1,0:T(8,128)(2,1)S(1)} %get-tuple-element.106), channel_id=1, source_target_pairs={{0,1},{1,0},{2,3},{3,2},{4,5},{5,4},{6,7},{7,6},{8,9},{9,8},{10,11... | collective-permute-start | bytes 3145736 | tf_op jit(solution)/shard_map/ppermute | solution.py:249
  333.8 15.8 %collective-permute-start.23 = (bf16[4,8,64,128]{3,2,1,0:T(8,128)(2,1)S(1)}, bf16[4,8,64,128]{3,2,1,0:T(8,128)(2,1)S(1)}, u32[]{:S(2)}, u32[]{:S(2)}) collective-permute-start(bf16[4,8,64,128]{3,2,1,0:T(8,128)(2,1)S(1)} %fusion.24), channel_id=1, source_target_pairs={{0,1},{1,0},{2,3},{3,2},{4,5},{5,4},{6,7},{7,6},{8,9},{9,8},{10,11... | collective-permute-start | bytes 1572872 | tf_op jit(solution)/shard_map/ppermute | solution.py:249
  342.5 14.9 %collective-permute-start.30 = (bf16[2,8,64,256]{3,2,1,0:T(8,128)(2,1)S(1)}, bf16[2,8,64,256]{3,2,1,0:T(8,128)(2,1)S(1)}, u32[]{:S(2)}, u32[]{:S(2)}) collective-permute-start(bf16[2,8,64,256]{3,2,1,0:T(8,128)(2,1)S(1)} %pad_maximum_fusion.2), channel_id=1, source_target_pairs={{0,3},{1,2},{2,1},{3,0},{4,7},{5,6},{6,5},{7,4},{8,11},{9,10},{10,... | collective-permute-start | bytes 1572872 | tf_op jit(solution)/shard_map/ppermute | solution.py:249
  343.7 16.1 %collective-permute-start.18 = (bf16[2,8,64,256]{3,2,1,0:T(8,128)(2,1)S(1)}, bf16[2,8,64,256]{3,2,1,0:T(8,128)(2,1)S(1)}, u32[]{:S(2)}, u32[]{:S(2)}) collective-permute-start(bf16[2,8,64,256]{3,2,1,0:T(8,128)(2,1)S(1)} %fusion.16), channel_id=1, source_target_pairs={{0,1},{1,0},{2,3},{3,2},{4,5},{5,4},{6,7},{7,6},{8,9},{9,8},{10,11... | collective-permute-start | bytes 1572872 | tf_op jit(solution)/shard_map/ppermute | solution.py:249
  376.0 20.5 %collective-permute-start.36 = (bf16[64,1024]{1,0:T(8,128)(2,1)S(1)}, bf16[64,1024]{1,0:T(8,128)(2,1)S(1)}, u32[]{:S(2)}, u32[]{:S(2)}) collective-permute-start(bf16[64,1024]{1,0:T(8,128)(2,1)S(1)} %get-tuple-element.116), channel_id=1, source_target_pairs={{0,160},{1,161},{2,162},{3,163},{4,164},{5,165},{6,166},{7,167},{8... | collective-permute-start | bytes 393224 | tf_op jit(solution)/shard_map/ppermute | solution.py:249
  378.1 18.4 %collective-permute-start.35 = (bf16[64,1024]{1,0:T(8,128)(2,1)S(1)}, bf16[64,1024]{1,0:T(8,128)(2,1)S(1)}, u32[]{:S(2)}, u32[]{:S(2)}) collective-permute-start(bf16[64,1024]{1,0:T(8,128)(2,1)S(1)} %get-tuple-element.117), channel_id=1, source_target_pairs={{0,128},{1,129},{2,130},{3,131},{4,132},{5,133},{6,134},{7,135},{8... | collective-permute-start | bytes 393224 | tf_op jit(solution)/shard_map/ppermute | solution.py:249
  379.7 16.8 %collective-permute-start.34 = (bf16[64,1024]{1,0:T(8,128)(2,1)S(1)}, bf16[64,1024]{1,0:T(8,128)(2,1)S(1)}, u32[]{:S(2)}, u32[]{:S(2)}) collective-permute-start(bf16[64,1024]{1,0:T(8,128)(2,1)S(1)} %get-tuple-element.118), channel_id=1, source_target_pairs={{0,96},{1,97},{2,98},{3,99},{4,100},{5,101},{6,102},{7,103},{8,104... | collective-permute-start | bytes 393224 | tf_op jit(solution)/shard_map/ppermute | solution.py:249
  382.5 16.6 %collective-permute-start.33 = (bf16[64,1024]{1,0:T(8,128)(2,1)S(1)}, bf16[64,1024]{1,0:T(8,128)(2,1)S(1)}, u32[]{:S(2)}, u32[]{:S(2)}) collective-permute-start(bf16[64,1024]{1,0:T(8,128)(2,1)S(1)} %get-tuple-element.119), channel_id=1, source_target_pairs={{0,64},{1,65},{2,66},{3,67},{4,68},{5,69},{6,70},{7,71},{8,72},{9,... | collective-permute-start | bytes 393224 | tf_op jit(solution)/shard_map/ppermute | solution.py:249
  (22 other events, 198.0 us)
Sparse Core Ops, SparseCore 0:
  12.4 155.1 all-gather.1

commit v4 on v3

--- a/solution.py
+++ b/solution.py
@@ -172,7 +172,7 @@
         give(dv_out, ga, dv[:, :HEAD] + shared * dv[:, HEAD:])
         return 0
 
-    lax.fori_loop(0, responses // 2, visit, 0, unroll=2)
+    lax.fori_loop(0, responses // 2, visit, 0, unroll=3)
     stores = []
     for which in range(2):
         for group in range(2):
@@ -258,9 +258,11 @@
 
 
 def sum_z(blocks):
-    total = blocks[0].astype(jnp.float32)
-    for step in range(1, 8):
-        total = total + swap(blocks[step], "z", step).astype(jnp.float32)
+    even, odd = blocks[0::2], blocks[1::2]
+    pairs = even + swap(odd, "z", 1)
+    total = pairs[0].astype(jnp.float32)
+    for step in range(1, 4):
+        total = total + swap(pairs[step], "z", 2 * step).astype(jnp.float32)
     return total.astype(jnp.bfloat16)
 
 
@@ -298,8 +300,8 @@
     results = {0: run(0)}
     results[1] = run(1, results[0][1])
 
-    def over_core(heads, slot):
-        there = {h: swap(results[h][7 + slot], "c", 1) for h in heads}
+    def over_core(heads, slot, *gates):
+        there = {h: swap(after(results[h][7 + slot], *gates), "c", 1) for h in heads}
         return {(w, h): results[h][3 + 2 * w + slot] + there[h][w] for h in heads for w in WAYS}
 
     def near_first(sent):
@@ -318,9 +320,9 @@
     results[2] = run(2, *sent.values())
     results[3] = run(3, results[2][1])
     mine = far_first(kept, got, results[3][1])
-    sent = over_core((2, 3), 1)
+    sent = over_core((2, 3), 1, *mine.values())
     got = near_first(sent)
-    kept = over_core((2, 3), 0)
+    kept = over_core((2, 3), 0, *sent.values())
     mine |= far_first(kept, got)
     total = {}
     for w in WAYS:

time: 409 us -> 394 us (0.963)
  Pallas kernels: 77.6 us -> 71.9 us
  waiting for transfers between devices: 237 us -> 232 us
    pallas_call x4, Pallas kernels: 77.6 us -> 71.9 us  [attend(): pl.pallas_call(functools.partial(attend_kernel, FIRST[head], head), grid_...]
    ppermute x39 -> x36, waiting for transfers between devices: 82.3 us -> 77.5 us  [swap(): lax.ppermute(array, ('wide', 'narrow'), [(i, i ^ flip) for i in range(cou...]
    ppermute x39 -> x36, starting transfers between devices: 45.4 us -> 42.1 us  [swap(): lax.ppermute(array, ('wide', 'narrow'), [(i, i ^ flip) for i in range(cou...]
  transfers between devices with their start and end apart: 40 -> 37, of which waited for: 19 -> 20; matrix products, arithmetic and copies ran while one was open for 7% -> 6% of each run, Pallas kernels for 14% -> 9%
where the time goes in v4:
time: 394 us; the launch traced here: 393 us
  waiting for transfers between devices  232 us (59%)
  Pallas kernels  71.9 us (18%)
  starting transfers between devices  42.1 us (11%)
  other arithmetic  26.8 us (7%)
  between operations  15.1 us (4%)
  local copies, waits for them, and re-layouts  4.95 us (1%)
    all_gather x1, waiting for transfers between devices, body(): gathered = lax.all_gather(held, ('wide', 'narrow'), axis=0, tiled=True)  155 us
    ppermute x36, waiting for transfers between devices, swap(): lax.ppermute(array, ('wide', 'narrow'), [(i, i ^ flip) for i in range(cou...  77.5 us
    pallas_call x4, Pallas kernels, attend(): pl.pallas_call(functools.partial(attend_kernel, FIRST[head], head), grid_...  71.9 us
    ppermute x36, starting transfers between devices, swap(): lax.ppermute(array, ('wide', 'narrow'), [(i, i ^ flip) for i in range(cou...  42.1 us
  transfers between devices with their start and end apart: 37, of which 20 were waited for; matrix products, arithmetic and copies ran while one was open for 6% of the time, Pallas kernels for 9%

profile of v4, /device:TPU:8, one launch (start us, length us, event | category | flops | bytes accessed | tf_op | source)
XLA Modules:
  0.0 393.1 jit_solution(8114559112980520998)
XLA Ops:
  13.0 154.6 %all-gather.2.cloned.1.call-done = bf16[16384,1024]{1,0:T(8,128)(2,1)} async-done(((bf16[64,1024]{1,0:T(8,128)(2,1)}), bf16[16384,1024]{1,0:T(8,128)(2,1)}) %all-gather.2.cloned.1.call-update) | async-done | bytes 33554448 | tf_op jit(solution)/shard_map/all_gather | solution.py:292
  169.6 18.0 %shard_map.110 = (bf16[384,1024]{1,0:T(8,128)(2,1)S(1)}, bf16[384,128]{1,0:T(8,128)(2,1)S(1)}, bf16[384,128]{1,0:T(8,128)(2,1)S(1)}, bf16[2,4,8,64,128]{4,3,2,1,...) custom-call(s32[48]{0:T(128)S(1)} %get-tuple-element.65.order, ...), custom_call_target="tpu_custom_call" | custom-call | flops 1006632960 | bytes 69468160 | tf_op jit(solution)/shard_map/pallas_call | solution.py:206
  187.6 18.0 %shard_map.111 = (bf16[384,1024]{1,0:T(8,128)(2,1)S(1)}, bf16[384,128]{1,0:T(8,128)(2,1)S(1)}, bf16[384,128]{1,0:T(8,128)(2,1)S(1)}, bf16[2,4,8,64,128]{4,3,2,1,...) custom-call(s32[48]{0:T(128)S(1)} %get-tuple-element.65.order, ...), custom_call_target="tpu_custom_call" | custom-call | flops 1006632960 | bytes 69468160 | tf_op jit(solution)/shard_map/pallas_call | solution.py:206
  206.7 3.3 collective-permute-done.1
  213.1 2.9 collective-permute-done
  221.9 18.0 %shard_map.112 = (bf16[384,1024]{1,0:T(8,128)(2,1)S(1)}, bf16[384,128]{1,0:T(8,128)(2,1)S(1)}, bf16[384,128]{1,0:T(8,128)(2,1)S(1)}, bf16[2,4,8,64,128]{4,3,2,1,...) custom-call(s32[48]{0:T(128)S(1)} %get-tuple-element.65.order, ...), custom_call_target="tpu_custom_call" | custom-call | flops 1006632960 | bytes 69468160 | tf_op jit(solution)/shard_map/pallas_call | solution.py:206
  239.9 18.0 %shard_map.113 = (bf16[384,1024]{1,0:T(8,128)(2,1)S(1)}, bf16[384,128]{1,0:T(8,128)(2,1)S(1)}, bf16[384,128]{1,0:T(8,128)(2,1)S(1)}, bf16[2,4,8,64,128]{4,3,2,1,...) custom-call(s32[48]{0:T(128)S(1)} %get-tuple-element.65.order, ...), custom_call_target="tpu_custom_call" | custom-call | flops 1006632960 | bytes 69468160 | tf_op jit(solution)/shard_map/pallas_call | solution.py:206
  266.6 2.2 collective-permute-start.9
  270.2 6.4 %collective-permute-done.4 = bf16[4,8,64,128]{3,2,1,0:T(8,128)(2,1)S(1)} collective-permute-done((bf16[4,8,64,128]{3,2,1,0:T(8,128)(2,1)S(1)}, bf16[4,8,64,128]{3,2,1,0:T(8,128)(2,1)S(1)}, u32[]{:S(2)}, u32[]{:S(2)}) %collective-permute-start.4) | collective-permute-done | bytes 524320 | tf_op jit(solution)/shard_map/ppermute | solution.py:249
  282.9 3.6 collective-permute-done.12
  286.8 2.7 collective-permute-done.13
  295.9 2.7 collective-permute-start.20
  298.8 18.5 %collective-permute-done.15 = bf16[2,4,8,64,128]{4,3,2,1,0:T(8,128)(2,1)S(1)} collective-permute-done((bf16[2,4,8,64,128]{4,3,2,1,0:T(8,128)(2,1)S(1)}, bf16[2,4,8,64,128]{4,3,2,1,0:T(8,128)(2,1)S(1)}, u32[]{:S(2)}, u32[]{:S(2)}) %collective-permute-start.15) | collective-permute-done | bytes 1048608 | tf_op jit(solution)/shard_map/ppermute | solution.py:249
  317.4 2.2 collective-permute-start.16
  322.5 2.4 collective-permute-start.29
  324.9 7.4 %collective-permute-done.16 = bf16[4,8,64,128]{3,2,1,0:T(8,128)(2,1)S(1)} collective-permute-done((bf16[4,8,64,128]{3,2,1,0:T(8,128)(2,1)S(1)}, bf16[4,8,64,128]{3,2,1,0:T(8,128)(2,1)S(1)}, u32[]{:S(2)}, u32[]{:S(2)}) %collective-permute-start.16) | collective-permute-done | bytes 524320 | tf_op jit(solution)/shard_map/ppermute | solution.py:249
  332.5 2.1 collective-permute-start.17
  338.3 8.5 %collective-permute-done.17 = bf16[2,8,64,256]{3,2,1,0:T(8,128)(2,1)S(1)} collective-permute-done((bf16[2,8,64,256]{3,2,1,0:T(8,128)(2,1)S(1)}, bf16[2,8,64,256]{3,2,1,0:T(8,128)(2,1)S(1)}, u32[]{:S(2)}, u32[]{:S(2)}) %collective-permute-start.17) | collective-permute-done | bytes 524320 | tf_op jit(solution)/shard_map/ppermute | solution.py:249
  348.0 2.4 collective-permute-start.27
  354.0 4.2 %collective-permute-done.23 = bf16[8,64,256]{2,1,0:T(8,128)(2,1)S(1)} collective-permute-done((bf16[8,64,256]{2,1,0:T(8,128)(2,1)S(1)}, bf16[8,64,256]{2,1,0:T(8,128)(2,1)S(1)}, u32[]{:S(2)}, u32[]{:S(2)}) %collective-permute-start.23) | collective-permute-done | bytes 262176 | tf_op jit(solution)/shard_map/ppermute | solution.py:249
  360.9 9.6 %collective-permute-done.32 = bf16[4,64,1024]{2,1,0:T(8,128)(2,1)S(1)} collective-permute-done((bf16[4,64,1024]{2,1,0:T(8,128)(2,1)S(1)}, bf16[4,64,1024]{2,1,0:T(8,128)(2,1)S(1)}, u32[]{:S(2)}, u32[]{:S(2)}) %collective-permute-start.32) | collective-permute-done | bytes 524320 | tf_op jit(solution)/shard_map/ppermute | solution.py:249
  370.6 2.3 collective-permute-start.33
  374.9 2.2 collective-permute-start.34
  381.3 4.2 %collective-permute-done.34 = bf16[64,1024]{1,0:T(8,128)(2,1)S(1)} collective-permute-done((bf16[64,1024]{1,0:T(8,128)(2,1)S(1)}, bf16[64,1024]{1,0:T(8,128)(2,1)S(1)}, u32[]{:S(2)}, u32[]{:S(2)}) %collective-permute-start.34) | collective-permute-done | bytes 131104 | tf_op jit(solution)/shard_map/ppermute | solution.py:249
  (134 shorter events, 61.5 us)
Async XLA Ops:
  7.2 160.5 %all-gather.2.cloned.1.call-start = ((), (), s32[]{:S(2)}) async-start(), calls=%async_computation | async-start | bytes 33685504 | tf_op jit(solution)/shard_map/all_gather | solution.py:292
  206.2 12.9 %collective-permute-start.2 = (bf16[2,2,4,8,64,128]{5,4,3,2,1,0:T(8,128)(2,1)}, bf16[2,2,4,8,64,128]{5,4,3,2,1,0:T(8,128)(2,1)S(1)}, u32[]{:S(2)}, u32[]{:S(2)}) collective-permute-start(bf16[2,2,4,8,64,128]{5,4,3,2,1,0:T(8,128)(2,1)} %get-tuple-element.74), channel_id=1, source_target_pairs={{0,4},{1,5},{2,6},{3,7},{4,0},{5,1},{6,2},{7,3},{8,12},{9,13},{10,... | collective-permute-start | bytes 6291464 | tf_op jit(solution)/shard_map/ppermute | solution.py:249
  206.5 51.4 %collective-permute-start.7 = (bf16[2,2,4,8,64,128]{5,4,3,2,1,0:T(8,128)(2,1)}, bf16[2,2,4,8,64,128]{5,4,3,2,1,0:T(8,128)(2,1)}, u32[]{:S(2)}, u32[]{:S(2)}) collective-permute-start(bf16[2,2,4,8,64,128]{5,4,3,2,1,0:T(8,128)(2,1)} %get-tuple-element.83), channel_id=1, source_target_pairs={{0,4},{1,5},{2,6},{3,7},{4,0},{5,1},{6,2},{7,3},{8,12},{9,13},{10,... | collective-permute-start | bytes 6291464 | tf_op jit(solution)/shard_map/ppermute | solution.py:249
  211.7 48.1 %collective-permute-start.10 = (bf16[2,4,8,64,128]{4,3,2,1,0:T(8,128)(2,1)}, bf16[2,4,8,64,128]{4,3,2,1,0:T(8,128)(2,1)}, u32[]{:S(2)}, u32[]{:S(2)}) collective-permute-start(bf16[2,4,8,64,128]{4,3,2,1,0:T(8,128)(2,1)} %get-tuple-element.117), channel_id=1, source_target_pairs={{0,24},{1,25},{2,26},{3,27},{4,28},{5,29},{6,30},{7,31},{8,16},{9,... | collective-permute-start | bytes 3145736 | tf_op jit(solution)/shard_map/ppermute | solution.py:249
  217.6 45.7 %collective-permute-start.5 = (bf16[2,4,8,64,128]{4,3,2,1,0:T(8,128)(2,1)}, bf16[2,4,8,64,128]{4,3,2,1,0:T(8,128)(2,1)}, u32[]{:S(2)}, u32[]{:S(2)}) collective-permute-start(bf16[2,4,8,64,128]{4,3,2,1,0:T(8,128)(2,1)} %get-tuple-element.119), channel_id=1, source_target_pairs={{0,3},{1,2},{2,1},{3,0},{4,7},{5,6},{6,5},{7,4},{8,11},{9,10},{10,... | collective-permute-start | bytes 3145736 | tf_op jit(solution)/shard_map/ppermute | solution.py:249
  218.6 42.3 %collective-permute-start.3 = (bf16[2,4,8,64,128]{4,3,2,1,0:T(8,128)(2,1)}, bf16[2,4,8,64,128]{4,3,2,1,0:T(8,128)(2,1)}, u32[]{:S(2)}, u32[]{:S(2)}) collective-permute-start(bf16[2,4,8,64,128]{4,3,2,1,0:T(8,128)(2,1)} %get-tuple-element.120), channel_id=1, source_target_pairs={{0,1},{1,0},{2,3},{3,2},{4,5},{5,4},{6,7},{7,6},{8,9},{9,8},{10,11... | collective-permute-start | bytes 3145736 | tf_op jit(solution)/shard_map/ppermute | solution.py:249
  219.1 46.4 %collective-permute-start.8 = (bf16[2,4,8,64,128]{4,3,2,1,0:T(8,128)(2,1)}, bf16[2,4,8,64,128]{4,3,2,1,0:T(8,128)(2,1)}, u32[]{:S(2)}, u32[]{:S(2)}) collective-permute-start(bf16[2,4,8,64,128]{4,3,2,1,0:T(8,128)(2,1)} %get-tuple-element.118), channel_id=1, source_target_pairs={{0,8},{1,9},{2,10},{3,11},{4,12},{5,13},{6,14},{7,15},{8,0},{9,1},... | collective-permute-start | bytes 3145736 | tf_op jit(solution)/shard_map/ppermute | solution.py:249
  262.0 14.6 %collective-permute-start.4 = (bf16[4,8,64,128]{3,2,1,0:T(8,128)(2,1)S(1)}, bf16[4,8,64,128]{3,2,1,0:T(8,128)(2,1)S(1)}, u32[]{:S(2)}, u32[]{:S(2)}) collective-permute-start(bf16[4,8,64,128]{3,2,1,0:T(8,128)(2,1)S(1)} %fusion.39), channel_id=1, source_target_pairs={{0,3},{1,2},{2,1},{3,0},{4,7},{5,6},{6,5},{7,4},{8,11},{9,10},{10,... | collective-permute-start | bytes 1572872 | tf_op jit(solution)/shard_map/ppermute | solution.py:249
  264.4 13.6 %collective-permute-start.6 = (bf16[4,8,64,128]{3,2,1,0:T(8,128)(2,1)S(1)}, bf16[4,8,64,128]{3,2,1,0:T(8,128)(2,1)S(1)}, u32[]{:S(2)}, u32[]{:S(2)}) collective-permute-start(bf16[4,8,64,128]{3,2,1,0:T(8,128)(2,1)S(1)} %fusion.36), channel_id=1, source_target_pairs={{0,1},{1,0},{2,3},{3,2},{4,5},{5,4},{6,7},{7,6},{8,9},{9,8},{10,11... | collective-permute-start | bytes 1572872 | tf_op jit(solution)/shard_map/ppermute | solution.py:249
  266.6 13.1 %collective-permute-start.9 = (bf16[4,8,64,128]{3,2,1,0:T(8,128)(2,1)S(1)}, bf16[4,8,64,128]{3,2,1,0:T(8,128)(2,1)S(1)}, u32[]{:S(2)}, u32[]{:S(2)}) collective-permute-start(bf16[4,8,64,128]{3,2,1,0:T(8,128)(2,1)S(1)} %fusion.33), channel_id=1, source_target_pairs={{0,24},{1,25},{2,26},{3,27},{4,28},{5,29},{6,30},{7,31},{8,16},{9,... | collective-permute-start | bytes 1572872 | tf_op jit(solution)/shard_map/ppermute | solution.py:249
  268.8 12.4 %collective-permute-start.11 = (bf16[4,8,64,128]{3,2,1,0:T(8,128)(2,1)S(1)}, bf16[4,8,64,128]{3,2,1,0:T(8,128)(2,1)S(1)}, u32[]{:S(2)}, u32[]{:S(2)}) collective-permute-start(bf16[4,8,64,128]{3,2,1,0:T(8,128)(2,1)S(1)} %fusion.30), channel_id=1, source_target_pairs={{0,8},{1,9},{2,10},{3,11},{4,12},{5,13},{6,14},{7,15},{8,0},{9,1},... | collective-permute-start | bytes 1572872 | tf_op jit(solution)/shard_map/ppermute | solution.py:249
  291.8 28.3 %collective-permute-start.19 = (bf16[2,2,4,8,64,128]{5,4,3,2,1,0:T(8,128)(2,1)S(1)}, bf16[2,2,4,8,64,128]{5,4,3,2,1,0:T(8,128)(2,1)S(1)}, u32[]{:S(2)}, u32[]{:S(2)}) collective-permute-start(bf16[2,2,4,8,64,128]{5,4,3,2,1,0:T(8,128)(2,1)S(1)} %copy-done.3), channel_id=1, source_target_pairs={{0,4},{1,5},{2,6},{3,7},{4,0},{5,1},{6,2},{7,3},{8,12},{9,13},{10,... | collective-permute-start | bytes 6291464 | tf_op jit(solution)/shard_map/ppermute | solution.py:249
  291.9 25.4 %collective-permute-start.15 = (bf16[2,4,8,64,128]{4,3,2,1,0:T(8,128)(2,1)S(1)}, bf16[2,4,8,64,128]{4,3,2,1,0:T(8,128)(2,1)S(1)}, u32[]{:S(2)}, u32[]{:S(2)}) collective-permute-start(bf16[2,4,8,64,128]{4,3,2,1,0:T(8,128)(2,1)S(1)} %get-tuple-element.112), channel_id=1, source_target_pairs={{0,1},{1,0},{2,3},{3,2},{4,5},{5,4},{6,7},{7,6},{8,9},{9,8},{10,11... | collective-permute-start | bytes 3145736 | tf_op jit(solution)/shard_map/ppermute | solution.py:249
  292.8 26.8 %collective-permute-start.24 = (bf16[2,4,8,64,128]{4,3,2,1,0:T(8,128)(2,1)S(1)}, bf16[2,4,8,64,128]{4,3,2,1,0:T(8,128)(2,1)S(1)}, u32[]{:S(2)}, u32[]{:S(2)}) collective-permute-start(bf16[2,4,8,64,128]{4,3,2,1,0:T(8,128)(2,1)S(1)} %get-tuple-element.111), channel_id=1, source_target_pairs={{0,3},{1,2},{2,1},{3,0},{4,7},{5,6},{6,5},{7,4},{8,11},{9,10},{10,... | collective-permute-start | bytes 3145736 | tf_op jit(solution)/shard_map/ppermute | solution.py:249
  294.7 27.8 %collective-permute-start.28 = (bf16[2,4,8,64,128]{4,3,2,1,0:T(8,128)(2,1)S(1)}, bf16[2,4,8,64,128]{4,3,2,1,0:T(8,128)(2,1)S(1)}, u32[]{:S(2)}, u32[]{:S(2)}) collective-permute-start(bf16[2,4,8,64,128]{4,3,2,1,0:T(8,128)(2,1)S(1)} %get-tuple-element.109), channel_id=1, source_target_pairs={{0,24},{1,25},{2,26},{3,27},{4,28},{5,29},{6,30},{7,31},{8,16},{9,... | collective-permute-start | bytes 3145736 | tf_op jit(solution)/shard_map/ppermute | solution.py:249
  295.9 25.5 %collective-permute-start.20 = (bf16[2,4,8,64,128]{4,3,2,1,0:T(8,128)(2,1)S(1)}, bf16[2,4,8,64,128]{4,3,2,1,0:T(8,128)(2,1)S(1)}, u32[]{:S(2)}, u32[]{:S(2)}) collective-permute-start(bf16[2,4,8,64,128]{4,3,2,1,0:T(8,128)(2,1)S(1)} %get-tuple-element.110), channel_id=1, source_target_pairs={{0,8},{1,9},{2,10},{3,11},{4,12},{5,13},{6,14},{7,15},{8,0},{9,1},... | collective-permute-start | bytes 3145736 | tf_op jit(solution)/shard_map/ppermute | solution.py:249
  317.4 14.9 %collective-permute-start.16 = (bf16[4,8,64,128]{3,2,1,0:T(8,128)(2,1)S(1)}, bf16[4,8,64,128]{3,2,1,0:T(8,128)(2,1)S(1)}, u32[]{:S(2)}, u32[]{:S(2)}) collective-permute-start(bf16[4,8,64,128]{3,2,1,0:T(8,128)(2,1)S(1)} %fusion.27), channel_id=1, source_target_pairs={{0,3},{1,2},{2,1},{3,0},{4,7},{5,6},{6,5},{7,4},{8,11},{9,10},{10,... | collective-permute-start | bytes 1572872 | tf_op jit(solution)/shard_map/ppermute | solution.py:249
  319.7 14.9 %collective-permute-start.25 = (bf16[4,8,64,128]{3,2,1,0:T(8,128)(2,1)S(1)}, bf16[4,8,64,128]{3,2,1,0:T(8,128)(2,1)S(1)}, u32[]{:S(2)}, u32[]{:S(2)}) collective-permute-start(bf16[4,8,64,128]{3,2,1,0:T(8,128)(2,1)S(1)} %fusion.21), channel_id=1, source_target_pairs={{0,1},{1,0},{2,3},{3,2},{4,5},{5,4},{6,7},{7,6},{8,9},{9,8},{10,11... | collective-permute-start | bytes 1572872 | tf_op jit(solution)/shard_map/ppermute | solution.py:249
  321.5 14.9 %collective-permute-start.21 = (bf16[4,8,64,128]{3,2,1,0:T(8,128)(2,1)S(1)}, bf16[4,8,64,128]{3,2,1,0:T(8,128)(2,1)S(1)}, u32[]{:S(2)}, u32[]{:S(2)}) collective-permute-start(bf16[4,8,64,128]{3,2,1,0:T(8,128)(2,1)S(1)} %fusion.24), channel_id=1, source_target_pairs={{0,24},{1,25},{2,26},{3,27},{4,28},{5,29},{6,30},{7,31},{8,16},{9,... | collective-permute-start | bytes 1572872 | tf_op jit(solution)/shard_map/ppermute | solution.py:249
  322.5 14.6 %collective-permute-start.29 = (bf16[4,8,64,128]{3,2,1,0:T(8,128)(2,1)S(1)}, bf16[4,8,64,128]{3,2,1,0:T(8,128)(2,1)S(1)}, u32[]{:S(2)}, u32[]{:S(2)}) collective-permute-start(bf16[4,8,64,128]{3,2,1,0:T(8,128)(2,1)S(1)} %fusion.18), channel_id=1, source_target_pairs={{0,8},{1,9},{2,10},{3,11},{4,12},{5,13},{6,14},{7,15},{8,0},{9,1},... | collective-permute-start | bytes 1572872 | tf_op jit(solution)/shard_map/ppermute | solution.py:249
  332.5 14.4 %collective-permute-start.17 = (bf16[2,8,64,256]{3,2,1,0:T(8,128)(2,1)S(1)}, bf16[2,8,64,256]{3,2,1,0:T(8,128)(2,1)S(1)}, u32[]{:S(2)}, u32[]{:S(2)}) collective-permute-start(bf16[2,8,64,256]{3,2,1,0:T(8,128)(2,1)S(1)} %fusion.17), channel_id=1, source_target_pairs={{0,8},{1,9},{2,10},{3,11},{4,12},{5,13},{6,14},{7,15},{8,0},{9,1},... | collective-permute-start | bytes 1572872 | tf_op jit(solution)/shard_map/ppermute | solution.py:249
  334.8 13.1 %collective-permute-start.26 = (bf16[2,8,64,256]{3,2,1,0:T(8,128)(2,1)S(1)}, bf16[2,8,64,256]{3,2,1,0:T(8,128)(2,1)S(1)}, u32[]{:S(2)}, u32[]{:S(2)}) collective-permute-start(bf16[2,8,64,256]{3,2,1,0:T(8,128)(2,1)S(1)} %pad_maximum_fusion.1), channel_id=1, source_target_pairs={{0,24},{1,25},{2,26},{3,27},{4,28},{5,29},{6,30},{7,31},{8,16},{9,... | collective-permute-start | bytes 1572872 | tf_op jit(solution)/shard_map/ppermute | solution.py:249
  336.6 13.9 %collective-permute-start.22 = (bf16[2,8,64,256]{3,2,1,0:T(8,128)(2,1)S(1)}, bf16[2,8,64,256]{3,2,1,0:T(8,128)(2,1)S(1)}, u32[]{:S(2)}, u32[]{:S(2)}) collective-permute-start(bf16[2,8,64,256]{3,2,1,0:T(8,128)(2,1)S(1)} %fusion.16), channel_id=1, source_target_pairs={{0,1},{1,0},{2,3},{3,2},{4,5},{5,4},{6,7},{7,6},{8,9},{9,8},{10,11... | collective-permute-start | bytes 1572872 | tf_op jit(solution)/shard_map/ppermute | solution.py:249
  337.3 14.8 %collective-permute-start.30 = (bf16[2,8,64,256]{3,2,1,0:T(8,128)(2,1)S(1)}, bf16[2,8,64,256]{3,2,1,0:T(8,128)(2,1)S(1)}, u32[]{:S(2)}, u32[]{:S(2)}) collective-permute-start(bf16[2,8,64,256]{3,2,1,0:T(8,128)(2,1)S(1)} %pad_maximum_fusion.2), channel_id=1, source_target_pairs={{0,3},{1,2},{2,1},{3,0},{4,7},{5,6},{6,5},{7,4},{8,11},{9,10},{10,... | collective-permute-start | bytes 1572872 | tf_op jit(solution)/shard_map/ppermute | solution.py:249
  (20 other events, 117.5 us)
Sparse Core Ops, SparseCore 0:
  12.4 155.1 all-gather.1

commit v5 on v4

--- a/solution.py
+++ b/solution.py
@@ -48,9 +48,10 @@
 FIRST = ("x", "y", "x", "y")
 
 
-def attend_kernel(first, head, order, owners, spot, q_ref, d_ref, rk_ref, rv_ref, gathered, *refs):
+def attend_kernel(first, head, joint, order, owners, spot, q_ref, d_ref, rk_ref, rv_ref, gathered, *refs):
     dq_ref, drk_ref, drv_ref = refs[:3]
-    here_k, here_v, there, refs = refs[3:5], refs[5:7], refs[7:9], refs[9:]
+    here_k, here_v, refs = refs[3:5], refs[5:7], refs[7:]
+    there, refs = ((refs[0].at[0], refs[0].at[1]), refs[1:]) if joint else (refs[:2], refs[2:])
     q_rows, d_rows, own_k, own_v, dq_acc, drk_acc, drv_acc, k_in, v_in, dk_out, dv_out, arrived, left = refs
     responses = q_ref.shape[0] // TOKENS
 
@@ -191,7 +192,7 @@
         store.wait()
 
 
-def attend(order, owners, spot, queries, cotangents, keys, values, gathered, head, gates):
+def attend(order, owners, spot, queries, cotangents, keys, values, gathered, head, joint, gates):
     rows = queries.shape[0]
     prompts, _, length, _ = gathered.shape
     deep = prompts // 8
@@ -204,13 +205,13 @@
     outward = pltpu.VMEM((2, 4, 4, deep, length, HEAD), jnp.bfloat16)
     share = jax.ShapeDtypeStruct((2, 4, deep, length, HEAD), jnp.bfloat16)
     return pl.pallas_call(
-        functools.partial(attend_kernel, FIRST[head], head),
+        functools.partial(attend_kernel, FIRST[head], head, joint),
         grid_spec=pltpu.PrefetchScalarGridSpec(
             num_scalar_prefetch=3,
             grid=(1,),
             in_specs=[here((rows, wide)), here((rows, wide)), here((rows, HEAD)), here((rows, HEAD))]
             + [far],
-            out_specs=[out((rows, wide)), out((rows, HEAD)), out((rows, HEAD))] + [far] * 6,
+            out_specs=[out((rows, wide)), out((rows, HEAD)), out((rows, HEAD))] + [far] * (5 if joint else 6),
             scratch_shapes=[
                 pltpu.VMEM((rows * PER_GROUP, HEAD), jnp.bfloat16),
                 pltpu.VMEM((rows * PER_GROUP, HEAD), jnp.bfloat16),
@@ -233,7 +234,8 @@
             jax.ShapeDtypeStruct((rows, HEAD), jnp.bfloat16),
         ]
         + [share] * 4
-        + [jax.ShapeDtypeStruct((2,) + share.shape, jnp.bfloat16)] * 2,
+        + [jax.ShapeDtypeStruct((2, 2) + share.shape, jnp.bfloat16)] * joint
+        + [jax.ShapeDtypeStruct((2,) + share.shape, jnp.bfloat16)] * (0 if joint else 2),
         compiler_params=pltpu.CompilerParams(vmem_limit_bytes=48 * 2**20),
         cost_estimate=pl.CostEstimate(
             flops=10 * rows * PER_GROUP * positions * HEAD,
@@ -294,14 +296,14 @@
 
     def run(head, *gates):
         return attend(
-            order, owners, spot, queries, output_gradient, response_keys, response_values, gathered, head, gates
+            order, owners, spot, queries, output_gradient, response_keys, response_values, gathered, head, head > 1, gates
         )
 
     results = {0: run(0)}
     results[1] = run(1, results[0][1])
 
-    def over_core(heads, slot, *gates):
-        there = {h: swap(after(results[h][7 + slot], *gates), "c", 1) for h in heads}
+    def over_core(heads, slot):
+        there = {h: crossed[h][slot] if h in crossed else swap(results[h][7 + slot], "c", 1) for h in heads}
         return {(w, h): results[h][3 + 2 * w + slot] + there[h][w] for h in heads for w in WAYS}
 
     def near_first(sent):
@@ -314,15 +316,17 @@
             out[w, h] = mine[0] + got[w, h][0] + swap(far, FIRST[h], NEAR_FAR[w][1])
         return out
 
+    crossed = {}
     sent = over_core((0, 1), 1)
     got = near_first(sent)
     kept = over_core((0, 1), 0)
-    results[2] = run(2, *sent.values())
+    results[2] = run(2, *sent.values(), kept[0, 0])
     results[3] = run(3, results[2][1])
     mine = far_first(kept, got, results[3][1])
-    sent = over_core((2, 3), 1, *mine.values())
-    got = near_first(sent)
-    kept = over_core((2, 3), 0, *sent.values())
+    crossed = {h: swap(after(results[h][7], *got.values()), "c", 1) for h in (2, 3)}
+    sent = over_core((2, 3), 1)
+    got = near_first({key: after(array, *mine.values()) for key, array in sent.items()})
+    kept = over_core((2, 3), 0)
     mine |= far_first(kept, got)
     total = {}
     for w in WAYS:

time: 394 us -> 390 us (0.990)
  starting transfers between devices: 42.1 us -> 32 us
  waiting for transfers between devices: 232 us -> 238 us
    ppermute x36 -> x34, starting transfers between devices: 42.1 us -> 31.9 us  [swap(): lax.ppermute(array, ('wide', 'narrow'), [(i, i ^ flip) for i in range(cou...]
    ppermute x36 -> x34, waiting for transfers between devices: 77.5 us -> 83.7 us  [swap(): lax.ppermute(array, ('wide', 'narrow'), [(i, i ^ flip) for i in range(cou...]
    add x8 -> x6, other arithmetic: 7.29 us -> 8.79 us  [over_core(): results[h][3 + 2 * w + slot] + there[h][w]]
  transfers between devices with their start and end apart: 37 -> 35, of which waited for: 20 -> 17; matrix products, arithmetic and copies ran while one was open for 6% -> 7% of each run, Pallas kernels for 9% -> 14%
where the time goes in v5:
time: 390 us; the launch traced here: 389 us
  waiting for transfers between devices  238 us (61%)
  Pallas kernels  72 us (18%)
  starting transfers between devices  32 us (8%)
  other arithmetic  28 us (7%)
  between operations  15.1 us (4%)
    all_gather x1, waiting for transfers between devices, body(): gathered = lax.all_gather(held, ('wide', 'narrow'), axis=0, tiled=True)  155 us
    ppermute x34, waiting for transfers between devices, swap(): lax.ppermute(array, ('wide', 'narrow'), [(i, i ^ flip) for i in range(cou...  83.7 us
    pallas_call x4, Pallas kernels, attend(): pl.pallas_call(functools.partial(attend_kernel, FIRST[head], head, joint)...  72 us
    ppermute x34, starting transfers between devices, swap(): lax.ppermute(array, ('wide', 'narrow'), [(i, i ^ flip) for i in range(cou...  31.9 us
    add x6, other arithmetic, over_core(): results[h][3 + 2 * w + slot] + there[h][w]  8.79 us
  transfers between devices with their start and end apart: 35, of which 17 were waited for; matrix products, arithmetic and copies ran while one was open for 7% of the time, Pallas kernels for 14%

profile of v5, /device:TPU:8, one launch (start us, length us, event | category | flops | bytes accessed | tf_op | source)
XLA Modules:
  0.0 388.6 jit_solution(8956739537008997989)
XLA Ops:
  13.0 154.6 %all-gather.2.cloned.1.call-done = bf16[16384,1024]{1,0:T(8,128)(2,1)} async-done(((bf16[64,1024]{1,0:T(8,128)(2,1)}), bf16[16384,1024]{1,0:T(8,128)(2,1)}) %all-gather.2.cloned.1.call-update) | async-done | bytes 33554448 | tf_op jit(solution)/shard_map/all_gather | solution.py:294
  169.6 18.0 %shard_map.110 = (bf16[384,1024]{1,0:T(8,128)(2,1)S(1)}, bf16[384,128]{1,0:T(8,128)(2,1)S(1)}, bf16[384,128]{1,0:T(8,128)(2,1)S(1)}, bf16[2,4,8,64,128]{4,3,2,1,...) custom-call(s32[48]{0:T(128)S(1)} %get-tuple-element.67.order, ...), custom_call_target="tpu_custom_call" | custom-call | flops 1006632960 | bytes 69468160 | tf_op jit(solution)/shard_map/pallas_call | solution.py:207
  187.9 18.0 %shard_map.111 = (bf16[384,1024]{1,0:T(8,128)(2,1)S(1)}, bf16[384,128]{1,0:T(8,128)(2,1)S(1)}, bf16[384,128]{1,0:T(8,128)(2,1)S(1)}, bf16[2,4,8,64,128]{4,3,2,1,...) custom-call(s32[48]{0:T(128)S(1)} %get-tuple-element.67.order, ...), custom_call_target="tpu_custom_call" | custom-call | flops 1006632960 | bytes 69468160 | tf_op jit(solution)/shard_map/pallas_call | solution.py:207
  206.5 3.1 fusion.14
  217.1 18.0 %shard_map.112 = (bf16[384,1024]{1,0:T(8,128)(2,1)S(1)}, bf16[384,128]{1,0:T(8,128)(2,1)S(1)}, bf16[384,128]{1,0:T(8,128)(2,1)S(1)}, bf16[2,4,8,64,128]{4,3,2,1,...) custom-call(s32[48]{0:T(128)S(1)} %get-tuple-element.67.order, ...), custom_call_target="tpu_custom_call" | custom-call | flops 1006632960 | bytes 69468160 | tf_op jit(solution)/shard_map/pallas_call | solution.py:207
  235.1 18.0 %shard_map.113 = (bf16[384,1024]{1,0:T(8,128)(2,1)S(1)}, bf16[384,128]{1,0:T(8,128)(2,1)S(1)}, bf16[384,128]{1,0:T(8,128)(2,1)S(1)}, bf16[2,4,8,64,128]{4,3,2,1,...) custom-call(s32[48]{0:T(128)S(1)} %get-tuple-element.67.order, ...), custom_call_target="tpu_custom_call" | custom-call | flops 1006632960 | bytes 69468160 | tf_op jit(solution)/shard_map/pallas_call | solution.py:207
  263.9 9.8 %collective-permute-done.4 = bf16[4,8,64,128]{3,2,1,0:T(8,128)(2,1)S(1)} collective-permute-done((bf16[4,8,64,128]{3,2,1,0:T(8,128)(2,1)S(1)}, bf16[4,8,64,128]{3,2,1,0:T(8,128)(2,1)S(1)}, u32[]{:S(2)}, u32[]{:S(2)}) %collective-permute-start.4) | collective-permute-done | bytes 524320 | tf_op jit(solution)/shard_map/ppermute | solution.py:251
  278.7 8.5 %collective-permute-done.12 = bf16[4,8,64,128]{3,2,1,0:T(8,128)(2,1)S(1)} collective-permute-done((bf16[4,8,64,128]{3,2,1,0:T(8,128)(2,1)S(1)}, bf16[4,8,64,128]{3,2,1,0:T(8,128)(2,1)S(1)}, u32[]{:S(2)}, u32[]{:S(2)}) %collective-permute-start.12) | collective-permute-done | bytes 524320 | tf_op jit(solution)/shard_map/ppermute | solution.py:251
  293.0 19.8 %collective-permute-done.18 = bf16[2,4,8,64,128]{4,3,2,1,0:T(8,128)(2,1)S(1)} collective-permute-done((bf16[2,4,8,64,128]{4,3,2,1,0:T(8,128)(2,1)S(1)}, bf16[2,4,8,64,128]{4,3,2,1,0:T(8,128)(2,1)S(1)}, u32[]{:S(2)}, u32[]{:S(2)}) %collective-permute-start.18) | collective-permute-done | bytes 1048608 | tf_op jit(solution)/shard_map/ppermute | solution.py:251
  314.0 2.6 collective-permute-start.27
  316.6 1.9 collective-permute-start.14
  318.9 5.6 %collective-permute-done.19 = bf16[4,8,64,128]{3,2,1,0:T(8,128)(2,1)S(1)} collective-permute-done((bf16[4,8,64,128]{3,2,1,0:T(8,128)(2,1)S(1)}, bf16[4,8,64,128]{3,2,1,0:T(8,128)(2,1)S(1)}, u32[]{:S(2)}, u32[]{:S(2)}) %collective-permute-start.19) | collective-permute-done | bytes 524320 | tf_op jit(solution)/shard_map/ppermute | solution.py:251
  325.7 2.0 collective-permute-start.28
  327.8 3.0 collective-permute-done.14
  331.0 2.2 collective-permute-done.23
  333.8 6.3 %collective-permute-done.20 = bf16[2,8,64,256]{3,2,1,0:T(8,128)(2,1)S(1)} collective-permute-done((bf16[2,8,64,256]{3,2,1,0:T(8,128)(2,1)S(1)}, bf16[2,8,64,256]{3,2,1,0:T(8,128)(2,1)S(1)}, u32[]{:S(2)}, u32[]{:S(2)}) %collective-permute-start.20) | collective-permute-done | bytes 524320 | tf_op jit(solution)/shard_map/ppermute | solution.py:251
  343.0 2.6 collective-permute-done.24
  345.8 2.7 collective-permute-done.16
  349.0 3.2 collective-permute-done.25
  354.7 11.9 %collective-permute-done.30 = bf16[4,64,1024]{2,1,0:T(8,128)(2,1)S(1)} collective-permute-done((bf16[4,64,1024]{2,1,0:T(8,128)(2,1)S(1)}, bf16[4,64,1024]{2,1,0:T(8,128)(2,1)S(1)}, u32[]{:S(2)}, u32[]{:S(2)}) %collective-permute-start.30) | collective-permute-done | bytes 524320 | tf_op jit(solution)/shard_map/ppermute | solution.py:251
  366.7 2.1 collective-permute-start.31
  368.8 2.5 collective-permute-start.33
  374.9 2.3 collective-permute-done.33
  377.2 3.8 collective-permute-done.32
  (120 shorter events, 50.7 us)
Async XLA Ops:
  7.2 160.5 %all-gather.2.cloned.1.call-start = ((), (), s32[]{:S(2)}) async-start(), calls=%async_computation | async-start | bytes 33685504 | tf_op jit(solution)/shard_map/all_gather | solution.py:294
  187.6 18.9 %collective-permute-start = (bf16[2,2,4,8,64,128]{5,4,3,2,1,0:T(8,128)(2,1)}, bf16[2,2,4,8,64,128]{5,4,3,2,1,0:T(8,128)(2,1)}, u32[]{:S(2)}, u32[]{:S(2)}) collective-permute-start(bf16[2,2,4,8,64,128]{5,4,3,2,1,0:T(8,128)(2,1)} %get-tuple-element.57), channel_id=1, source_target_pairs={{0,4},{1,5},{2,6},{3,7},{4,0},{5,1},{6,2},{7,3},{8,12},{9,13},{10,... | collective-permute-start | bytes 6291464 | tf_op jit(solution)/shard_map/ppermute | solution.py:251
  209.6 43.5 %collective-permute-start.5 = (bf16[2,4,8,64,128]{4,3,2,1,0:T(8,128)(2,1)}, bf16[2,4,8,64,128]{4,3,2,1,0:T(8,128)(2,1)}, u32[]{:S(2)}, u32[]{:S(2)}) collective-permute-start(bf16[2,4,8,64,128]{4,3,2,1,0:T(8,128)(2,1)} %get-tuple-element.119), channel_id=1, source_target_pairs={{0,3},{1,2},{2,1},{3,0},{4,7},{5,6},{6,5},{7,4},{8,11},{9,10},{10,... | collective-permute-start | bytes 3145736 | tf_op jit(solution)/shard_map/ppermute | solution.py:251
  210.6 42.5 %collective-permute-start.3 = (bf16[2,4,8,64,128]{4,3,2,1,0:T(8,128)(2,1)}, bf16[2,4,8,64,128]{4,3,2,1,0:T(8,128)(2,1)}, u32[]{:S(2)}, u32[]{:S(2)}) collective-permute-start(bf16[2,4,8,64,128]{4,3,2,1,0:T(8,128)(2,1)} %get-tuple-element.120), channel_id=1, source_target_pairs={{0,1},{1,0},{2,3},{3,2},{4,5},{5,4},{6,7},{7,6},{8,9},{9,8},{10,11... | collective-permute-start | bytes 3145736 | tf_op jit(solution)/shard_map/ppermute | solution.py:251
  212.6 40.5 %collective-permute-start.7 = (bf16[2,4,8,64,128]{4,3,2,1,0:T(8,128)(2,1)}, bf16[2,4,8,64,128]{4,3,2,1,0:T(8,128)(2,1)}, u32[]{:S(2)}, u32[]{:S(2)}) collective-permute-start(bf16[2,4,8,64,128]{4,3,2,1,0:T(8,128)(2,1)} %get-tuple-element.117), channel_id=1, source_target_pairs={{0,24},{1,25},{2,26},{3,27},{4,28},{5,29},{6,30},{7,31},{8,16},{9,... | collective-permute-start | bytes 3145736 | tf_op jit(solution)/shard_map/ppermute | solution.py:251
  214.1 39.1 %collective-permute-start.6 = (bf16[2,4,8,64,128]{4,3,2,1,0:T(8,128)(2,1)}, bf16[2,4,8,64,128]{4,3,2,1,0:T(8,128)(2,1)}, u32[]{:S(2)}, u32[]{:S(2)}) collective-permute-start(bf16[2,4,8,64,128]{4,3,2,1,0:T(8,128)(2,1)} %get-tuple-element.118), channel_id=1, source_target_pairs={{0,8},{1,9},{2,10},{3,11},{4,12},{5,13},{6,14},{7,15},{8,0},{9,1},... | collective-permute-start | bytes 3145736 | tf_op jit(solution)/shard_map/ppermute | solution.py:251
  215.9 38.2 %collective-permute-start.10 = (bf16[2,2,4,8,64,128]{5,4,3,2,1,0:T(8,128)(2,1)}, bf16[2,2,4,8,64,128]{5,4,3,2,1,0:T(8,128)(2,1)}, u32[]{:S(2)}, u32[]{:S(2)}) collective-permute-start(bf16[2,2,4,8,64,128]{5,4,3,2,1,0:T(8,128)(2,1)} %get-tuple-element.83), channel_id=1, source_target_pairs={{0,4},{1,5},{2,6},{3,7},{4,0},{5,1},{6,2},{7,3},{8,12},{9,13},{10,... | collective-permute-start | bytes 6291464 | tf_op jit(solution)/shard_map/ppermute | solution.py:251
  253.2 35.1 %collective-permute-start.17 = (bf16[2,2,2,4,8,64,128]{6,5,4,3,2,1,0:T(8,128)(2,1)}, bf16[2,2,2,4,8,64,128]{6,5,4,3,2,1,0:T(8,128)(2,1)S(1)}, u32[]{:S(2)}, u32[]{:S(2)}) collective-permute-start(bf16[2,2,2,4,8,64,128]{6,5,4,3,2,1,0:T(8,128)(2,1)} %get-tuple-element.90), channel_id=1, source_target_pairs={{0,4},{1,5},{2,6},{3,7},{4,0},{5,1},{6,2},{7,3},{8,12},{9,13},{10,... | collective-permute-start | bytes 12582920 | tf_op jit(solution)/shard_map/ppermute | solution.py:251
  254.0 36.3 %collective-permute-start.8 = (bf16[2,2,2,4,8,64,128]{6,5,4,3,2,1,0:T(8,128)(2,1)}, bf16[2,2,2,4,8,64,128]{6,5,4,3,2,1,0:T(8,128)(2,1)S(1)}, u32[]{:S(2)}, u32[]{:S(2)}) collective-permute-start(bf16[2,2,2,4,8,64,128]{6,5,4,3,2,1,0:T(8,128)(2,1)} %get-tuple-element.78), channel_id=1, source_target_pairs={{0,4},{1,5},{2,6},{3,7},{4,0},{5,1},{6,2},{7,3},{8,12},{9,13},{10,... | collective-permute-start | bytes 12582920 | tf_op jit(solution)/shard_map/ppermute | solution.py:251
  258.2 15.6 %collective-permute-start.4 = (bf16[4,8,64,128]{3,2,1,0:T(8,128)(2,1)S(1)}, bf16[4,8,64,128]{3,2,1,0:T(8,128)(2,1)S(1)}, u32[]{:S(2)}, u32[]{:S(2)}) collective-permute-start(bf16[4,8,64,128]{3,2,1,0:T(8,128)(2,1)S(1)} %fusion.39), channel_id=1, source_target_pairs={{0,3},{1,2},{2,1},{3,0},{4,7},{5,6},{6,5},{7,4},{8,11},{9,10},{10,... | collective-permute-start | bytes 1572872 | tf_op jit(solution)/shard_map/ppermute | solution.py:251
  261.2 14.1 %collective-permute-start.9 = (bf16[4,8,64,128]{3,2,1,0:T(8,128)(2,1)S(1)}, bf16[4,8,64,128]{3,2,1,0:T(8,128)(2,1)S(1)}, u32[]{:S(2)}, u32[]{:S(2)}) collective-permute-start(bf16[4,8,64,128]{3,2,1,0:T(8,128)(2,1)S(1)} %fusion.36), channel_id=1, source_target_pairs={{0,1},{1,0},{2,3},{3,2},{4,5},{5,4},{6,7},{7,6},{8,9},{9,8},{10,11... | collective-permute-start | bytes 1572872 | tf_op jit(solution)/shard_map/ppermute | solution.py:251
  263.8 13.8 %collective-permute-start.11 = (bf16[4,8,64,128]{3,2,1,0:T(8,128)(2,1)S(1)}, bf16[4,8,64,128]{3,2,1,0:T(8,128)(2,1)S(1)}, u32[]{:S(2)}, u32[]{:S(2)}) collective-permute-start(bf16[4,8,64,128]{3,2,1,0:T(8,128)(2,1)S(1)} %fusion.33), channel_id=1, source_target_pairs={{0,24},{1,25},{2,26},{3,27},{4,28},{5,29},{6,30},{7,31},{8,16},{9,... | collective-permute-start | bytes 1572872 | tf_op jit(solution)/shard_map/ppermute | solution.py:251
  273.7 13.5 %collective-permute-start.12 = (bf16[4,8,64,128]{3,2,1,0:T(8,128)(2,1)S(1)}, bf16[4,8,64,128]{3,2,1,0:T(8,128)(2,1)S(1)}, u32[]{:S(2)}, u32[]{:S(2)}) collective-permute-start(bf16[4,8,64,128]{3,2,1,0:T(8,128)(2,1)S(1)} %fusion.30), channel_id=1, source_target_pairs={{0,8},{1,9},{2,10},{3,11},{4,12},{5,13},{6,14},{7,15},{8,0},{9,1},... | collective-permute-start | bytes 1572872 | tf_op jit(solution)/shard_map/ppermute | solution.py:251
  288.9 23.9 %collective-permute-start.18 = (bf16[2,4,8,64,128]{4,3,2,1,0:T(8,128)(2,1)S(1)}, bf16[2,4,8,64,128]{4,3,2,1,0:T(8,128)(2,1)S(1)}, u32[]{:S(2)}, u32[]{:S(2)}) collective-permute-start(bf16[2,4,8,64,128]{4,3,2,1,0:T(8,128)(2,1)S(1)} %get-tuple-element.92), channel_id=1, source_target_pairs={{0,8},{1,9},{2,10},{3,11},{4,12},{5,13},{6,14},{7,15},{8,0},{9,1},... | collective-permute-start | bytes 3145736 | tf_op jit(solution)/shard_map/ppermute | solution.py:251
  289.2 24.7 %collective-permute-start.26 = (bf16[2,4,8,64,128]{4,3,2,1,0:T(8,128)(2,1)S(1)}, bf16[2,4,8,64,128]{4,3,2,1,0:T(8,128)(2,1)S(1)}, u32[]{:S(2)}, u32[]{:S(2)}) collective-permute-start(bf16[2,4,8,64,128]{4,3,2,1,0:T(8,128)(2,1)S(1)} %get-tuple-element.98), channel_id=1, source_target_pairs={{0,24},{1,25},{2,26},{3,27},{4,28},{5,29},{6,30},{7,31},{8,16},{9,... | collective-permute-start | bytes 3145736 | tf_op jit(solution)/shard_map/ppermute | solution.py:251
  290.8 25.8 %collective-permute-start.13 = (bf16[2,4,8,64,128]{4,3,2,1,0:T(8,128)(2,1)S(1)}, bf16[2,4,8,64,128]{4,3,2,1,0:T(8,128)(2,1)S(1)}, u32[]{:S(2)}, u32[]{:S(2)}) collective-permute-start(bf16[2,4,8,64,128]{4,3,2,1,0:T(8,128)(2,1)S(1)} %get-tuple-element.87), channel_id=1, source_target_pairs={{0,1},{1,0},{2,3},{3,2},{4,5},{5,4},{6,7},{7,6},{8,9},{9,8},{10,11... | collective-permute-start | bytes 3145736 | tf_op jit(solution)/shard_map/ppermute | solution.py:251
  291.4 27.1 %collective-permute-start.22 = (bf16[2,4,8,64,128]{4,3,2,1,0:T(8,128)(2,1)S(1)}, bf16[2,4,8,64,128]{4,3,2,1,0:T(8,128)(2,1)S(1)}, u32[]{:S(2)}, u32[]{:S(2)}) collective-permute-start(bf16[2,4,8,64,128]{4,3,2,1,0:T(8,128)(2,1)S(1)} %get-tuple-element.95), channel_id=1, source_target_pairs={{0,3},{1,2},{2,1},{3,0},{4,7},{5,6},{6,5},{7,4},{8,11},{9,10},{10,... | collective-permute-start | bytes 3145736 | tf_op jit(solution)/shard_map/ppermute | solution.py:251
  312.8 11.7 %collective-permute-start.19 = (bf16[4,8,64,128]{3,2,1,0:T(8,128)(2,1)S(1)}, bf16[4,8,64,128]{3,2,1,0:T(8,128)(2,1)S(1)}, u32[]{:S(2)}, u32[]{:S(2)}) collective-permute-start(bf16[4,8,64,128]{3,2,1,0:T(8,128)(2,1)S(1)} %fusion.24), channel_id=1, source_target_pairs={{0,24},{1,25},{2,26},{3,27},{4,28},{5,29},{6,30},{7,31},{8,16},{9,... | collective-permute-start | bytes 1572872 | tf_op jit(solution)/shard_map/ppermute | solution.py:251
  316.6 14.1 %collective-permute-start.14 = (bf16[4,8,64,128]{3,2,1,0:T(8,128)(2,1)S(1)}, bf16[4,8,64,128]{3,2,1,0:T(8,128)(2,1)S(1)}, u32[]{:S(2)}, u32[]{:S(2)}) collective-permute-start(bf16[4,8,64,128]{3,2,1,0:T(8,128)(2,1)S(1)} %fusion.27), channel_id=1, source_target_pairs={{0,3},{1,2},{2,1},{3,0},{4,7},{5,6},{6,5},{7,4},{8,11},{9,10},{10,... | collective-permute-start | bytes 1572872 | tf_op jit(solution)/shard_map/ppermute | solution.py:251
  318.6 14.6 %collective-permute-start.23 = (bf16[4,8,64,128]{3,2,1,0:T(8,128)(2,1)S(1)}, bf16[4,8,64,128]{3,2,1,0:T(8,128)(2,1)S(1)}, u32[]{:S(2)}, u32[]{:S(2)}) collective-permute-start(bf16[4,8,64,128]{3,2,1,0:T(8,128)(2,1)S(1)} %fusion.21), channel_id=1, source_target_pairs={{0,1},{1,0},{2,3},{3,2},{4,5},{5,4},{6,7},{7,6},{8,9},{9,8},{10,11... | collective-permute-start | bytes 1572872 | tf_op jit(solution)/shard_map/ppermute | solution.py:251
  324.7 15.3 %collective-permute-start.20 = (bf16[2,8,64,256]{3,2,1,0:T(8,128)(2,1)S(1)}, bf16[2,8,64,256]{3,2,1,0:T(8,128)(2,1)S(1)}, u32[]{:S(2)}, u32[]{:S(2)}) collective-permute-start(bf16[2,8,64,256]{3,2,1,0:T(8,128)(2,1)S(1)} %fusion.16), channel_id=1, source_target_pairs={{0,1},{1,0},{2,3},{3,2},{4,5},{5,4},{6,7},{7,6},{8,9},{9,8},{10,11... | collective-permute-start | bytes 1572872 | tf_op jit(solution)/shard_map/ppermute | solution.py:251
  325.7 17.1 %collective-permute-start.28 = (bf16[2,8,64,256]{3,2,1,0:T(8,128)(2,1)S(1)}, bf16[2,8,64,256]{3,2,1,0:T(8,128)(2,1)S(1)}, u32[]{:S(2)}, u32[]{:S(2)}) collective-permute-start(bf16[2,8,64,256]{3,2,1,0:T(8,128)(2,1)S(1)} %pad_maximum_fusion.2), channel_id=1, source_target_pairs={{0,3},{1,2},{2,1},{3,0},{4,7},{5,6},{6,5},{7,4},{8,11},{9,10},{10,... | collective-permute-start | bytes 1572872 | tf_op jit(solution)/shard_map/ppermute | solution.py:251
  333.4 12.2 %collective-permute-start.24 = (bf16[2,8,64,256]{3,2,1,0:T(8,128)(2,1)S(1)}, bf16[2,8,64,256]{3,2,1,0:T(8,128)(2,1)S(1)}, u32[]{:S(2)}, u32[]{:S(2)}) collective-permute-start(bf16[2,8,64,256]{3,2,1,0:T(8,128)(2,1)S(1)} %pad_maximum_fusion.1), channel_id=1, source_target_pairs={{0,24},{1,25},{2,26},{3,27},{4,28},{5,29},{6,30},{7,31},{8,16},{9,... | collective-permute-start | bytes 1572872 | tf_op jit(solution)/shard_map/ppermute | solution.py:251
  352.7 13.8 %collective-permute-start.30 = (bf16[4,64,1024]{2,1,0:T(8,128)(2,1)S(1)}, bf16[4,64,1024]{2,1,0:T(8,128)(2,1)S(1)}, u32[]{:S(2)}, u32[]{:S(2)}) collective-permute-start(bf16[4,64,1024]{2,1,0:T(8,128)(2,1)S(1)} %slice.355), channel_id=1, source_target_pairs={{0,32},{1,33},{2,34},{3,35},{4,36},{5,37},{6,38},{7,39},{8,40},{9,... | collective-permute-start | bytes 1572872 | tf_op jit(solution)/shard_map/ppermute | solution.py:251
  (14 other events, 99.6 us)
Sparse Core Ops, SparseCore 0:
  12.4 155.1 all-gather.1

commit v6 on v5

--- a/solution.py
+++ b/solution.py
@@ -323,9 +323,10 @@
     results[2] = run(2, *sent.values(), kept[0, 0])
     results[3] = run(3, results[2][1])
     mine = far_first(kept, got, results[3][1])
-    crossed = {h: swap(after(results[h][7], *got.values()), "c", 1) for h in (2, 3)}
+    crossed = {2: swap(after(results[2][7], *got.values(), results[3][1]), "c", 1)}
+    crossed[3] = swap(after(results[3][7], crossed[2]), "c", 1)
     sent = over_core((2, 3), 1)
-    got = near_first({key: after(array, *mine.values()) for key, array in sent.items()})
+    got = near_first({key: after(array, *mine.values(), *sent.values()) for key, array in sent.items()})
     kept = over_core((2, 3), 0)
     mine |= far_first(kept, got)
     total = {}

time: 390 us -> 386 us (0.990)
  waiting for transfers between devices: 238 us -> 231 us
    ppermute x34, waiting for transfers between devices: 83.7 us -> 76.8 us  [swap(): lax.ppermute(array, ('wide', 'narrow'), [(i, i ^ flip) for i in range(cou...]
  transfers between devices with their start and end apart: 35 -> 35, of which waited for: 17 -> 17; matrix products, arithmetic and copies ran while one was open for 7% -> 6% of each run, Pallas kernels for 14% -> 14%
where the time goes in v6:
time: 386 us; the launch traced here: 384 us
  waiting for transfers between devices  231 us (60%)
  Pallas kernels  72 us (19%)
  starting transfers between devices  35.8 us (9%)
  other arithmetic  26.6 us (7%)
  between operations  15.1 us (4%)
    all_gather x1, waiting for transfers between devices, body(): gathered = lax.all_gather(held, ('wide', 'narrow'), axis=0, tiled=True)  155 us
    ppermute x34, waiting for transfers between devices, swap(): lax.ppermute(array, ('wide', 'narrow'), [(i, i ^ flip) for i in range(cou...  76.8 us
    pallas_call x4, Pallas kernels, attend(): pl.pallas_call(functools.partial(attend_kernel, FIRST[head], head, joint)...  72 us
    ppermute x34, starting transfers between devices, swap(): lax.ppermute(array, ('wide', 'narrow'), [(i, i ^ flip) for i in range(cou...  35.8 us
  transfers between devices with their start and end apart: 35, of which 17 were waited for; matrix products, arithmetic and copies ran while one was open for 6% of the time, Pallas kernels for 14%

profile of v6, /device:TPU:8, one launch (start us, length us, event | category | flops | bytes accessed | tf_op | source)
XLA Modules:
  0.0 384.1 jit_solution(16456649615794454869)
XLA Ops:
  13.0 154.6 %all-gather.2.cloned.1.call-done = bf16[16384,1024]{1,0:T(8,128)(2,1)} async-done(((bf16[64,1024]{1,0:T(8,128)(2,1)}), bf16[16384,1024]{1,0:T(8,128)(2,1)}) %all-gather.2.cloned.1.call-update) | async-done | bytes 33554448 | tf_op jit(solution)/shard_map/all_gather | solution.py:294
  169.6 18.0 %shard_map.110 = (bf16[384,1024]{1,0:T(8,128)(2,1)S(1)}, bf16[384,128]{1,0:T(8,128)(2,1)S(1)}, bf16[384,128]{1,0:T(8,128)(2,1)S(1)}, bf16[2,4,8,64,128]{4,3,2,1,...) custom-call(s32[48]{0:T(128)S(1)} %get-tuple-element.67.order, ...), custom_call_target="tpu_custom_call" | custom-call | flops 1006632960 | bytes 69468160 | tf_op jit(solution)/shard_map/pallas_call | solution.py:207
  188.0 18.0 %shard_map.111 = (bf16[384,1024]{1,0:T(8,128)(2,1)S(1)}, bf16[384,128]{1,0:T(8,128)(2,1)S(1)}, bf16[384,128]{1,0:T(8,128)(2,1)S(1)}, bf16[2,4,8,64,128]{4,3,2,1,...) custom-call(s32[48]{0:T(128)S(1)} %get-tuple-element.67.order, ...), custom_call_target="tpu_custom_call" | custom-call | flops 1006632960 | bytes 69468160 | tf_op jit(solution)/shard_map/pallas_call | solution.py:207
  206.5 3.2 fusion.14
  217.2 18.0 %shard_map.112 = (bf16[384,1024]{1,0:T(8,128)(2,1)S(1)}, bf16[384,128]{1,0:T(8,128)(2,1)S(1)}, bf16[384,128]{1,0:T(8,128)(2,1)S(1)}, bf16[2,4,8,64,128]{4,3,2,1,...) custom-call(s32[48]{0:T(128)S(1)} %get-tuple-element.67.order, ...), custom_call_target="tpu_custom_call" | custom-call | flops 1006632960 | bytes 69468160 | tf_op jit(solution)/shard_map/pallas_call | solution.py:207
  235.2 18.0 %shard_map.113 = (bf16[384,1024]{1,0:T(8,128)(2,1)S(1)}, bf16[384,128]{1,0:T(8,128)(2,1)S(1)}, bf16[384,128]{1,0:T(8,128)(2,1)S(1)}, bf16[2,4,8,64,128]{4,3,2,1,...) custom-call(s32[48]{0:T(128)S(1)} %get-tuple-element.67.order, ...), custom_call_target="tpu_custom_call" | custom-call | flops 1006632960 | bytes 69468160 | tf_op jit(solution)/shard_map/pallas_call | solution.py:207
  253.9 6.9 %collective-permute-done.8 = bf16[2,2,2,4,8,64,128]{6,5,4,3,2,1,0:T(8,128)(2,1)S(1)} collective-permute-done((bf16[2,2,2,4,8,64,128]{6,5,4,3,2,1,0:T(8,128)(2,1)}, bf16[2,2,2,4,8,64,128]{6,5,4,3,2,1,0:T(8,128)(2,1)S(1)}, u32[]{:S(2)}, u32[]{:S(2)}) %collective-permute-start.8) | collective-permute-done | bytes 4194336 | tf_op jit(solution)/shard_map/ppermute | solution.py:251
  260.9 2.9 collective-permute-done.10
  266.3 1.9 collective-permute-start.4
  273.4 8.2 %collective-permute-done.4 = bf16[4,8,64,128]{3,2,1,0:T(8,128)(2,1)S(1)} collective-permute-done((bf16[4,8,64,128]{3,2,1,0:T(8,128)(2,1)S(1)}, bf16[4,8,64,128]{3,2,1,0:T(8,128)(2,1)S(1)}, u32[]{:S(2)}, u32[]{:S(2)}) %collective-permute-start.4) | collective-permute-done | bytes 524320 | tf_op jit(solution)/shard_map/ppermute | solution.py:251
  293.1 19.5 %collective-permute-done.14 = bf16[2,4,8,64,128]{4,3,2,1,0:T(8,128)(2,1)S(1)} collective-permute-done((bf16[2,4,8,64,128]{4,3,2,1,0:T(8,128)(2,1)S(1)}, bf16[2,4,8,64,128]{4,3,2,1,0:T(8,128)(2,1)S(1)}, u32[]{:S(2)}, u32[]{:S(2)}) %collective-permute-start.14) | collective-permute-done | bytes 1048608 | tf_op jit(solution)/shard_map/ppermute | solution.py:251
  317.6 9.0 %collective-permute-done.15 = bf16[4,8,64,128]{3,2,1,0:T(8,128)(2,1)S(1)} collective-permute-done((bf16[4,8,64,128]{3,2,1,0:T(8,128)(2,1)S(1)}, bf16[4,8,64,128]{3,2,1,0:T(8,128)(2,1)S(1)}, u32[]{:S(2)}, u32[]{:S(2)}) %collective-permute-start.15) | collective-permute-done | bytes 524320 | tf_op jit(solution)/shard_map/ppermute | solution.py:251
  329.0 1.9 collective-permute-start.28
  330.9 7.5 %collective-permute-done.16 = bf16[2,8,64,256]{3,2,1,0:T(8,128)(2,1)S(1)} collective-permute-done((bf16[2,8,64,256]{3,2,1,0:T(8,128)(2,1)S(1)}, bf16[2,8,64,256]{3,2,1,0:T(8,128)(2,1)S(1)}, u32[]{:S(2)}, u32[]{:S(2)}) %collective-permute-start.16) | collective-permute-done | bytes 524320 | tf_op jit(solution)/shard_map/ppermute | solution.py:251
  339.3 2.0 collective-permute-start.21
  341.5 2.8 collective-permute-start.25
  348.8 1.9 collective-permute-done.29
  351.2 1.8 pad_maximum_fusion
  353.0 9.8 %collective-permute-done.30 = bf16[4,64,1024]{2,1,0:T(8,128)(2,1)S(1)} collective-permute-done((bf16[4,64,1024]{2,1,0:T(8,128)(2,1)S(1)}, bf16[4,64,1024]{2,1,0:T(8,128)(2,1)S(1)}, u32[]{:S(2)}, u32[]{:S(2)}) %collective-permute-start.30) | collective-permute-done | bytes 524320 | tf_op jit(solution)/shard_map/ppermute | solution.py:251
  362.9 2.6 collective-permute-start.31
  365.4 1.8 collective-permute-start.33
  367.3 2.2 collective-permute-start.32
  371.7 2.2 collective-permute-done.33
  373.9 2.6 collective-permute-done.32
  (120 shorter events, 51.9 us)
Async XLA Ops:
  7.2 160.5 %all-gather.2.cloned.1.call-start = ((), (), s32[]{:S(2)}) async-start(), calls=%async_computation | async-start | bytes 33685504 | tf_op jit(solution)/shard_map/all_gather | solution.py:294
  187.6 19.0 %collective-permute-start = (bf16[2,2,4,8,64,128]{5,4,3,2,1,0:T(8,128)(2,1)}, bf16[2,2,4,8,64,128]{5,4,3,2,1,0:T(8,128)(2,1)}, u32[]{:S(2)}, u32[]{:S(2)}) collective-permute-start(bf16[2,2,4,8,64,128]{5,4,3,2,1,0:T(8,128)(2,1)} %get-tuple-element.57), channel_id=1, source_target_pairs={{0,4},{1,5},{2,6},{3,7},{4,0},{5,1},{6,2},{7,3},{8,12},{9,13},{10,... | collective-permute-start | bytes 6291464 | tf_op jit(solution)/shard_map/ppermute | solution.py:251
  209.7 43.6 %collective-permute-start.5 = (bf16[2,4,8,64,128]{4,3,2,1,0:T(8,128)(2,1)}, bf16[2,4,8,64,128]{4,3,2,1,0:T(8,128)(2,1)}, u32[]{:S(2)}, u32[]{:S(2)}) collective-permute-start(bf16[2,4,8,64,128]{4,3,2,1,0:T(8,128)(2,1)} %get-tuple-element.119), channel_id=1, source_target_pairs={{0,3},{1,2},{2,1},{3,0},{4,7},{5,6},{6,5},{7,4},{8,11},{9,10},{10,... | collective-permute-start | bytes 3145736 | tf_op jit(solution)/shard_map/ppermute | solution.py:251
  210.7 42.6 %collective-permute-start.3 = (bf16[2,4,8,64,128]{4,3,2,1,0:T(8,128)(2,1)}, bf16[2,4,8,64,128]{4,3,2,1,0:T(8,128)(2,1)}, u32[]{:S(2)}, u32[]{:S(2)}) collective-permute-start(bf16[2,4,8,64,128]{4,3,2,1,0:T(8,128)(2,1)} %get-tuple-element.120), channel_id=1, source_target_pairs={{0,1},{1,0},{2,3},{3,2},{4,5},{5,4},{6,7},{7,6},{8,9},{9,8},{10,11... | collective-permute-start | bytes 3145736 | tf_op jit(solution)/shard_map/ppermute | solution.py:251
  212.7 40.6 %collective-permute-start.7 = (bf16[2,4,8,64,128]{4,3,2,1,0:T(8,128)(2,1)}, bf16[2,4,8,64,128]{4,3,2,1,0:T(8,128)(2,1)}, u32[]{:S(2)}, u32[]{:S(2)}) collective-permute-start(bf16[2,4,8,64,128]{4,3,2,1,0:T(8,128)(2,1)} %get-tuple-element.117), channel_id=1, source_target_pairs={{0,24},{1,25},{2,26},{3,27},{4,28},{5,29},{6,30},{7,31},{8,16},{9,... | collective-permute-start | bytes 3145736 | tf_op jit(solution)/shard_map/ppermute | solution.py:251
  214.2 39.1 %collective-permute-start.6 = (bf16[2,4,8,64,128]{4,3,2,1,0:T(8,128)(2,1)}, bf16[2,4,8,64,128]{4,3,2,1,0:T(8,128)(2,1)}, u32[]{:S(2)}, u32[]{:S(2)}) collective-permute-start(bf16[2,4,8,64,128]{4,3,2,1,0:T(8,128)(2,1)} %get-tuple-element.118), channel_id=1, source_target_pairs={{0,8},{1,9},{2,10},{3,11},{4,12},{5,13},{6,14},{7,15},{8,0},{9,1},... | collective-permute-start | bytes 3145736 | tf_op jit(solution)/shard_map/ppermute | solution.py:251
  260.8 27.5 %collective-permute-start.13 = (bf16[2,2,2,4,8,64,128]{6,5,4,3,2,1,0:T(8,128)(2,1)}, bf16[2,2,2,4,8,64,128]{6,5,4,3,2,1,0:T(8,128)(2,1)S(1)}, u32[]{:S(2)}, u32[]{:S(2)}) collective-permute-start(bf16[2,2,2,4,8,64,128]{6,5,4,3,2,1,0:T(8,128)(2,1)} %get-tuple-element.90), channel_id=1, source_target_pairs={{0,4},{1,5},{2,6},{3,7},{4,0},{5,1},{6,2},{7,3},{8,12},{9,13},{10,... | collective-permute-start | bytes 12582920 | tf_op jit(solution)/shard_map/ppermute | solution.py:251
  266.3 15.3 %collective-permute-start.4 = (bf16[4,8,64,128]{3,2,1,0:T(8,128)(2,1)S(1)}, bf16[4,8,64,128]{3,2,1,0:T(8,128)(2,1)S(1)}, u32[]{:S(2)}, u32[]{:S(2)}) collective-permute-start(bf16[4,8,64,128]{3,2,1,0:T(8,128)(2,1)S(1)} %fusion.39), channel_id=1, source_target_pairs={{0,3},{1,2},{2,1},{3,0},{4,7},{5,6},{6,5},{7,4},{8,11},{9,10},{10,... | collective-permute-start | bytes 1572872 | tf_op jit(solution)/shard_map/ppermute | solution.py:251
  269.3 13.8 %collective-permute-start.9 = (bf16[4,8,64,128]{3,2,1,0:T(8,128)(2,1)S(1)}, bf16[4,8,64,128]{3,2,1,0:T(8,128)(2,1)S(1)}, u32[]{:S(2)}, u32[]{:S(2)}) collective-permute-start(bf16[4,8,64,128]{3,2,1,0:T(8,128)(2,1)S(1)} %fusion.36), channel_id=1, source_target_pairs={{0,1},{1,0},{2,3},{3,2},{4,5},{5,4},{6,7},{7,6},{8,9},{9,8},{10,11... | collective-permute-start | bytes 1572872 | tf_op jit(solution)/shard_map/ppermute | solution.py:251
  271.9 13.5 %collective-permute-start.11 = (bf16[4,8,64,128]{3,2,1,0:T(8,128)(2,1)S(1)}, bf16[4,8,64,128]{3,2,1,0:T(8,128)(2,1)S(1)}, u32[]{:S(2)}, u32[]{:S(2)}) collective-permute-start(bf16[4,8,64,128]{3,2,1,0:T(8,128)(2,1)S(1)} %fusion.33), channel_id=1, source_target_pairs={{0,24},{1,25},{2,26},{3,27},{4,28},{5,29},{6,30},{7,31},{8,16},{9,... | collective-permute-start | bytes 1572872 | tf_op jit(solution)/shard_map/ppermute | solution.py:251
  272.0 14.5 %collective-permute-start.12 = (bf16[4,8,64,128]{3,2,1,0:T(8,128)(2,1)S(1)}, bf16[4,8,64,128]{3,2,1,0:T(8,128)(2,1)S(1)}, u32[]{:S(2)}, u32[]{:S(2)}) collective-permute-start(bf16[4,8,64,128]{3,2,1,0:T(8,128)(2,1)S(1)} %fusion.30), channel_id=1, source_target_pairs={{0,8},{1,9},{2,10},{3,11},{4,12},{5,13},{6,14},{7,15},{8,0},{9,1},... | collective-permute-start | bytes 1572872 | tf_op jit(solution)/shard_map/ppermute | solution.py:251
  288.8 23.8 %collective-permute-start.14 = (bf16[2,4,8,64,128]{4,3,2,1,0:T(8,128)(2,1)S(1)}, bf16[2,4,8,64,128]{4,3,2,1,0:T(8,128)(2,1)S(1)}, u32[]{:S(2)}, u32[]{:S(2)}) collective-permute-start(bf16[2,4,8,64,128]{4,3,2,1,0:T(8,128)(2,1)S(1)} %get-tuple-element.92), channel_id=1, source_target_pairs={{0,1},{1,0},{2,3},{3,2},{4,5},{5,4},{6,7},{7,6},{8,9},{9,8},{10,11... | collective-permute-start | bytes 3145736 | tf_op jit(solution)/shard_map/ppermute | solution.py:251
  289.5 24.2 %collective-permute-start.18 = (bf16[2,4,8,64,128]{4,3,2,1,0:T(8,128)(2,1)S(1)}, bf16[2,4,8,64,128]{4,3,2,1,0:T(8,128)(2,1)S(1)}, u32[]{:S(2)}, u32[]{:S(2)}) collective-permute-start(bf16[2,4,8,64,128]{4,3,2,1,0:T(8,128)(2,1)S(1)} %get-tuple-element.94), channel_id=1, source_target_pairs={{0,8},{1,9},{2,10},{3,11},{4,12},{5,13},{6,14},{7,15},{8,0},{9,1},... | collective-permute-start | bytes 3145736 | tf_op jit(solution)/shard_map/ppermute | solution.py:251
  290.9 25.3 %collective-permute-start.22 = (bf16[2,4,8,64,128]{4,3,2,1,0:T(8,128)(2,1)S(1)}, bf16[2,4,8,64,128]{4,3,2,1,0:T(8,128)(2,1)S(1)}, u32[]{:S(2)}, u32[]{:S(2)}) collective-permute-start(bf16[2,4,8,64,128]{4,3,2,1,0:T(8,128)(2,1)S(1)} %get-tuple-element.96), channel_id=1, source_target_pairs={{0,3},{1,2},{2,1},{3,0},{4,7},{5,6},{6,5},{7,4},{8,11},{9,10},{10,... | collective-permute-start | bytes 3145736 | tf_op jit(solution)/shard_map/ppermute | solution.py:251
  292.3 25.1 %collective-permute-start.26 = (bf16[2,4,8,64,128]{4,3,2,1,0:T(8,128)(2,1)S(1)}, bf16[2,4,8,64,128]{4,3,2,1,0:T(8,128)(2,1)S(1)}, u32[]{:S(2)}, u32[]{:S(2)}) collective-permute-start(bf16[2,4,8,64,128]{4,3,2,1,0:T(8,128)(2,1)S(1)} %get-tuple-element.98), channel_id=1, source_target_pairs={{0,24},{1,25},{2,26},{3,27},{4,28},{5,29},{6,30},{7,31},{8,16},{9,... | collective-permute-start | bytes 3145736 | tf_op jit(solution)/shard_map/ppermute | solution.py:251
  312.7 13.9 %collective-permute-start.15 = (bf16[4,8,64,128]{3,2,1,0:T(8,128)(2,1)S(1)}, bf16[4,8,64,128]{3,2,1,0:T(8,128)(2,1)S(1)}, u32[]{:S(2)}, u32[]{:S(2)}) collective-permute-start(bf16[4,8,64,128]{3,2,1,0:T(8,128)(2,1)S(1)} %fusion.27), channel_id=1, source_target_pairs={{0,3},{1,2},{2,1},{3,0},{4,7},{5,6},{6,5},{7,4},{8,11},{9,10},{10,... | collective-permute-start | bytes 1572872 | tf_op jit(solution)/shard_map/ppermute | solution.py:251
  313.7 13.6 %collective-permute-start.19 = (bf16[4,8,64,128]{3,2,1,0:T(8,128)(2,1)S(1)}, bf16[4,8,64,128]{3,2,1,0:T(8,128)(2,1)S(1)}, u32[]{:S(2)}, u32[]{:S(2)}) collective-permute-start(bf16[4,8,64,128]{3,2,1,0:T(8,128)(2,1)S(1)} %fusion.24), channel_id=1, source_target_pairs={{0,24},{1,25},{2,26},{3,27},{4,28},{5,29},{6,30},{7,31},{8,16},{9,... | collective-permute-start | bytes 1572872 | tf_op jit(solution)/shard_map/ppermute | solution.py:251
  316.3 11.5 %collective-permute-start.23 = (bf16[4,8,64,128]{3,2,1,0:T(8,128)(2,1)S(1)}, bf16[4,8,64,128]{3,2,1,0:T(8,128)(2,1)S(1)}, u32[]{:S(2)}, u32[]{:S(2)}) collective-permute-start(bf16[4,8,64,128]{3,2,1,0:T(8,128)(2,1)S(1)} %fusion.21), channel_id=1, source_target_pairs={{0,1},{1,0},{2,3},{3,2},{4,5},{5,4},{6,7},{7,6},{8,9},{9,8},{10,11... | collective-permute-start | bytes 1572872 | tf_op jit(solution)/shard_map/ppermute | solution.py:251
  317.5 11.3 %collective-permute-start.27 = (bf16[4,8,64,128]{3,2,1,0:T(8,128)(2,1)S(1)}, bf16[4,8,64,128]{3,2,1,0:T(8,128)(2,1)S(1)}, u32[]{:S(2)}, u32[]{:S(2)}) collective-permute-start(bf16[4,8,64,128]{3,2,1,0:T(8,128)(2,1)S(1)} %fusion.18), channel_id=1, source_target_pairs={{0,8},{1,9},{2,10},{3,11},{4,12},{5,13},{6,14},{7,15},{8,0},{9,1},... | collective-permute-start | bytes 1572872 | tf_op jit(solution)/shard_map/ppermute | solution.py:251
  326.7 11.7 %collective-permute-start.16 = (bf16[2,8,64,256]{3,2,1,0:T(8,128)(2,1)S(1)}, bf16[2,8,64,256]{3,2,1,0:T(8,128)(2,1)S(1)}, u32[]{:S(2)}, u32[]{:S(2)}) collective-permute-start(bf16[2,8,64,256]{3,2,1,0:T(8,128)(2,1)S(1)} %fusion.17), channel_id=1, source_target_pairs={{0,8},{1,9},{2,10},{3,11},{4,12},{5,13},{6,14},{7,15},{8,0},{9,1},... | collective-permute-start | bytes 1572872 | tf_op jit(solution)/shard_map/ppermute | solution.py:251
  327.5 11.7 %collective-permute-start.20 = (bf16[2,8,64,256]{3,2,1,0:T(8,128)(2,1)S(1)}, bf16[2,8,64,256]{3,2,1,0:T(8,128)(2,1)S(1)}, u32[]{:S(2)}, u32[]{:S(2)}) collective-permute-start(bf16[2,8,64,256]{3,2,1,0:T(8,128)(2,1)S(1)} %fusion.16), channel_id=1, source_target_pairs={{0,1},{1,0},{2,3},{3,2},{4,5},{5,4},{6,7},{7,6},{8,9},{9,8},{10,11... | collective-permute-start | bytes 1572872 | tf_op jit(solution)/shard_map/ppermute | solution.py:251
  328.1 13.3 %collective-permute-start.24 = (bf16[2,8,64,256]{3,2,1,0:T(8,128)(2,1)S(1)}, bf16[2,8,64,256]{3,2,1,0:T(8,128)(2,1)S(1)}, u32[]{:S(2)}, u32[]{:S(2)}) collective-permute-start(bf16[2,8,64,256]{3,2,1,0:T(8,128)(2,1)S(1)} %pad_maximum_fusion.1), channel_id=1, source_target_pairs={{0,24},{1,25},{2,26},{3,27},{4,28},{5,29},{6,30},{7,31},{8,16},{9,... | collective-permute-start | bytes 1572872 | tf_op jit(solution)/shard_map/ppermute | solution.py:251
  329.0 15.2 %collective-permute-start.28 = (bf16[2,8,64,256]{3,2,1,0:T(8,128)(2,1)S(1)}, bf16[2,8,64,256]{3,2,1,0:T(8,128)(2,1)S(1)}, u32[]{:S(2)}, u32[]{:S(2)}) collective-permute-start(bf16[2,8,64,256]{3,2,1,0:T(8,128)(2,1)S(1)} %pad_maximum_fusion.2), channel_id=1, source_target_pairs={{0,3},{1,2},{2,1},{3,0},{4,7},{5,6},{6,5},{7,4},{8,11},{9,10},{10,... | collective-permute-start | bytes 1572872 | tf_op jit(solution)/shard_map/ppermute | solution.py:251
  351.1 11.7 %collective-permute-start.30 = (bf16[4,64,1024]{2,1,0:T(8,128)(2,1)S(1)}, bf16[4,64,1024]{2,1,0:T(8,128)(2,1)S(1)}, u32[]{:S(2)}, u32[]{:S(2)}) collective-permute-start(bf16[4,64,1024]{2,1,0:T(8,128)(2,1)S(1)} %slice.355), channel_id=1, source_target_pairs={{0,32},{1,33},{2,34},{3,35},{4,36},{5,37},{6,38},{7,39},{8,40},{9,... | collective-permute-start | bytes 1572872 | tf_op jit(solution)/shard_map/ppermute | solution.py:251
  (14 other events, 90.6 us)
Sparse Core Ops, SparseCore 0:
  12.4 155.1 all-gather.1
